TPU v7x, 32 devices: a whole 2x2x4 slice. The times are simulated.
32 devices in a mesh: traj: 4 (over x, core), tx: 2 (over y), ty: 4 (over z).
Axes of the slice: x: 2, y: 2, z: 4, core: 2. Of those that a mesh axis runs over, the one named last changes fastest.
Arguments:
- density: float32 [4, 256, 1024], P('traj', None, ('tx', 'ty')), may hold values from 1 to 2
- momentum: float32 [4, 2, 256, 1024], P('traj', None, None, ('tx', 'ty')), may hold values from -0.5 to 0.5
- tracer: float32 [4, 256, 1024], P('traj', None, ('tx', 'ty')), may hold values from -1 to 1
- cotangent: float32 [4, 4, 256, 1024], P('traj', None, None, ('tx', 'ty')), may hold values from -6 to 6
- w_in: float32 [32, 16], replicated, may hold values from -1.5 to 1.5
- b_in: float32 [32], replicated, may hold values from -3 to 3
- w_mid: float32 [32, 32], replicated, may hold values from -1 to 1
- b_mid: float32 [32], replicated, may hold values from -3 to 3
- w_out: float32 [8, 32], replicated, may hold values from -1 to 1
- b_out: float32 [8], replicated, may hold values from -3 to 3
Outputs:
- grad_density: float32 [4, 256, 1024], P('traj', None, ('tx', 'ty'))
- grad_momentum: float32 [4, 2, 256, 1024], P('traj', None, None, ('tx', 'ty'))
- grad_tracer: float32 [4, 256, 1024], P('traj', None, ('tx', 'ty'))
- grad_w_in: float32 [32, 16], replicated
- grad_b_in: float32 [32], replicated
- grad_w_mid: float32 [32, 32], replicated
- grad_b_mid: float32 [32], replicated
- grad_w_out: float32 [8, 32], replicated
- grad_b_out: float32 [8], replicated
All inputs are finite; a program needn't handle non-finite values.
Results may differ from a plain program's by a relative error of at most 0.0003.
Values sent between devices are 32-bit elements; how exact they have to be, the bound alone decides.
No kernel may reach another device: no remote copies, remote signals or barrier semaphores. Data moves between devices by JAX's collectives and lax.ppermute only.
A program may use at most 128 MiB of HBM per device.

v0:
```python
import functools

import jax
import jax.numpy as jnp
from jax import lax
from jax.experimental import pallas as pl
from jax.experimental.pallas import tpu as pltpu
from jax.sharding import PartitionSpec as P

courant = 0.1
slope_gain = 0.25
F32 = jnp.float32
BF16 = jnp.bfloat16
FACES = 8
SEG = 16
RIM = 4
PAIR = 2
ONES = 16
VMEM_BYTES = 48 * 2**20


def dot(a, b):
    return lax.dot_general(a, b, (((1,), (0,)), ((), ())), preferred_element_type=F32)


def dot_nt(a, b):
    return lax.dot_general(a, b, (((1,), (1,)), ((), ())), preferred_element_type=F32)


def exact(a, b):
    return lax.dot_general(
        a, b, (((1,), (0,)), ((), ())), precision=lax.Precision.HIGHEST, preferred_element_type=F32
    )


def exact_nt(a, b):
    return lax.dot_general(
        a, b, (((1,), (1,)), ((), ())), precision=lax.Precision.HIGHEST, preferred_element_type=F32
    )


def split(values):
    high = values.astype(BF16)
    return high, (values - high.astype(F32)).astype(BF16)


def split3(values):
    high = values.astype(BF16)
    rest = values - high.astype(F32)
    middle = rest.astype(BF16)
    return high, middle, (rest - middle.astype(F32)).astype(BF16)


def rows_cols(shape):
    return lax.broadcasted_iota(jnp.int32, shape, 0), lax.broadcasted_iota(jnp.int32, shape, 1)


def pick(shape, test, dtype=BF16):
    r, c = rows_cols(shape)
    return jnp.where(test(r, c), 1.0, 0.0).astype(dtype)


def stack(parts):
    return jnp.concatenate(parts, 0)


def side(parts):
    return jnp.concatenate(parts, 1)


def place(left, levels, rights):
    total = None
    for values, right in zip(levels, rights):
        values = values if left is None else left(values).astype(BF16)
        part = dot(values, right)
        total = part if total is None else total + part
    return total


STACKED = (0, 0, 0, 1, 1, 2)


def stacked(parts):
    return [parts[0], parts[1], parts[2], parts[0], parts[1], parts[0]]


def level_of(block):
    return jnp.where(block < 3, 0, jnp.where(block < 5, 1, 2))


def build_first_x(w, b, hid):
    wide, cols = FACES * hid, 6 * 64 + ONES
    shape = (wide, cols)
    r, c = rows_cols(shape)
    total = jnp.zeros(shape, F32)
    for s in range(4):
        rights = [
            pick((16, cols), lambda q, n: (n < 384) & (level_of(n >> 6) == lev) & (q == 4 * s + ((n >> 4) & 3)))
            for lev in range(3)
        ]
        part = place(None, w, rights)
        total = total + jnp.where((c & 15) - (r // hid) == s, stack([part] * FACES), 0.0)
    levels = split3(b)
    at, _ = rows_cols((cols, hid))
    rows = jnp.zeros((cols, hid), F32)
    for lev in range(3):
        rows = jnp.where(at == 384 + lev, jnp.broadcast_to(levels[lev].astype(F32), (cols, hid)), rows)
    bias = dot_nt(pick((wide, hid), lambda q, n: (q % hid) == n), rows.astype(BF16))
    return (jnp.where(c < 384, total, 0.0) + bias).astype(BF16)


def build_first_y(w, hid):
    wide, cols = FACES * hid, 6 * 128
    shape = (wide, cols)
    r, c = rows_cols(shape)
    rights = [
        pick((16, cols), lambda q, n: (level_of(n >> 7) == lev) & (q == ((n & 127) >> 3))) for lev in range(3)
    ]
    part = place(None, w, rights)
    return jnp.where((c & 7) == (r // hid), stack([part] * FACES), 0.0).astype(BF16)


def build_mid(w, hid):
    block = 2 * hid
    shape = (2 * block, 4 * block)
    r, c = rows_cols(shape)

    def rights(levels):
        def test(lev):
            def inner(q, n):
                at = jnp.full(n.shape, -1, jnp.int32)
                for k, level in enumerate(levels):
                    at = jnp.where(n // block == k, level, at)
                return (at == lev) & ((n % hid) == q)

            return inner

        return [pick((hid, 4 * block), test(lev)) for lev in range(3)]

    upper = place(None, w, rights((0, 0, 0, 2)))
    lower = place(None, w, rights((1, 1, -1, -1)))
    keep = ((r % block) // hid) == ((c % block) // hid)
    return jnp.where(keep, stack([upper, upper, lower, lower]), 0.0).astype(BF16)


def build_mid_back(w, hid):
    block = 2 * hid
    shape = (block, 3 * block)
    r, c = rows_cols(shape)
    eye = pick((hid, hid), lambda q, n: q == n)
    rights = [
        pick((hid, 3 * block), lambda q, n: ((n // block == 1) == (lev == 1)) & ((n % hid) == q))
        for lev in range(2)
    ]
    part = place(lambda v: dot_nt(eye, v), w[:2], rights)
    return jnp.where((r // hid) == ((c % block) // hid), stack([part] * 2), 0.0).astype(BF16)


def build_out(w, hid):
    wide = FACES * hid
    shape = (64, wide)
    r, c = rows_cols(shape)
    right = pick((hid, wide), lambda q, n: (n % hid) == q)
    left = pick((64, 8), lambda q, n: (q >> 3) == n)
    keep = (r & 7) == (c // hid)
    return stack([jnp.where(keep, dot(dot(left, v).astype(BF16), right), 0.0) for v in w]).astype(BF16)


def spread_bias(b, rows, lanes, unit):
    n = b.shape[1]
    return exact_nt(pick((rows, n), lambda q, m: unit(q) == m, F32), jnp.broadcast_to(b, (lanes, n)))


def build_out_back(w, hid):
    wide = FACES * hid
    shape = (wide, 192)
    r, c = rows_cols(shape)
    left = pick((wide, hid), lambda q, n: (q % hid) == n)

    rights = [
        pick((8, 192), lambda q, n: (((n >> 6) == 1) == (lev == 1)) & (((n & 63) >> 3) == q)) for lev in range(2)
    ]
    part = place(lambda v: dot_nt(left, v), w[:2], rights)
    return jnp.where((r // hid) == (c & 7), part, 0.0).astype(BF16)


def build_first_x_back(w, hid):
    wide = FACES * hid
    shape = (128, 2 * wide)
    r, c = rows_cols(shape)
    right = pick((hid, 2 * wide), lambda q, n: (n % hid) == q)
    total = jnp.zeros(shape, F32)
    for s in range(4):
        left = pick((128, 16), lambda q, n: n == 4 * s + ((q & 63) >> 4))

        def one(values):
            return dot(dot_nt(left, values).astype(BF16), right)

        value = jnp.where(r < 64, one(w[0]), jnp.where(c < wide, one(w[1]), 0.0))
        total = total + jnp.where((r & 15) - ((c % wide) // hid) == s, value, 0.0)
    return total.astype(BF16)


def build_first_y_back(w, hid):
    wide = FACES * hid
    shape = (256, 2 * wide)
    r, c = rows_cols(shape)
    right = pick((hid, 2 * wide), lambda q, n: (n % hid) == q)
    left = pick((256, 16), lambda q, n: n == ((q & 127) >> 3))

    def one(values):
        return dot(dot_nt(left, values).astype(BF16), right)

    value = jnp.where(r < 128, one(w[0]), jnp.where(c < wide, one(w[1]), 0.0))
    return jnp.where((r & 7) == ((c % wide) // hid), value, 0.0).astype(BF16)


def limiter_forward(first, weights, hid):
    first_ref, first_bias_ref, mid_ref, mid_bias_ref, out_ref, out_bias_ref = weights
    width = first[0].shape[1]
    if first_bias_ref is None:
        h1 = jnp.tanh(dot(first_ref[...], stack(stacked(first) + [jnp.ones((ONES, width), BF16)])))
    else:
        h1 = jnp.tanh(dot(first_ref[...], stack(stacked(first))) + first_bias_ref[...])
    h1_parts = split3(h1)
    block = 2 * hid
    parts = []
    for at in range(0, FACES * hid, block):
        high, middle, low = (p[at : at + block] for p in h1_parts)
        both = dot(mid_ref[...], stack([high, middle, low, high]))
        parts.append(jnp.tanh(both[:block] + both[block:] + mid_bias_ref[...]))
    h2 = stack(parts)
    h2_parts = split3(h2)
    rows = 8 * FACES
    a = dot(out_ref[...], h2_parts[0])
    b = dot(out_ref[: 2 * rows, :], h2_parts[1])
    c = dot(out_ref[:rows, :], h2_parts[2])
    gates = jnp.tanh(
        ((a[2 * rows :] + b[rows:] + c) + (a[rows : 2 * rows] + b[:rows])) + a[:rows] + out_bias_ref[...]
    )
    return h1, h1_parts[:2], h2, h2_parts[:2], gates


def limiter_backward(d3, h1, h2, out_back_ref, mid_back_ref, hid):
    d3_hi, d3_lo = split(d3)
    d2 = dot(out_back_ref[...], stack([d3_hi, d3_hi, d3_lo])) * (1.0 - h2 * h2)
    d2_hi, d2_lo = split(d2)
    block = 2 * hid
    parts = []
    for at in range(0, FACES * hid, block):
        hi, lo = d2_hi[at : at + block], d2_lo[at : at + block]
        parts.append(dot(mid_back_ref[...], stack([hi, hi, lo])))
    d1 = stack(parts) * (1.0 - h1 * h1)
    return (d3_hi, d3_lo), (d2_hi, d2_lo), split(d1)


def first_backward(d1, back_ref):
    both = dot(back_ref[...], stack([d1[0], d1[1]]))
    half = both.shape[0] // 2
    return both[:half] + both[half:]


def add_weight_grads(first, h1, h2, d1, d2, d3, d3_full, acc, hid):
    acc_in, acc_mid, acc_out, acc_out_bias = acc
    width = d3_full.shape[1]
    ones = jnp.ones((ONES, width), BF16)
    nothing = jnp.zeros((ONES, width), BF16)
    acc_in[...] += dot_nt(
        side([stack([first[0], ones]), stack([first[0], ones]), stack([first[1], nothing])]),
        side([d1[0], d1[1], d1[0]]),
    )
    lefts, rights = [], []
    for at in range(0, FACES * hid, hid):
        lefts.append(stack([h1[0][at : at + hid], h1[1][at : at + hid], ones]))
        rights.append(stack([d2[0][at : at + hid], d2[1][at : at + hid]]))
    acc_mid[...] += dot_nt(side(lefts), side(rights))
    acc_out[...] += dot_nt(side([d3[0], d3[0], d3[1]]), side([h2[0], h2[1], h2[0]]))
    acc_out_bias[...] += d3_full


def edge_states(cells, gates):
    left, right = [], []
    for c in range(4):
        low = gates[FACES * c : FACES * (c + 1)]
        high = gates[FACES * (c + 4) : FACES * (c + 5)]
        left.append(cells[1][c] + slope_gain * low * (cells[2][c] - cells[0][c]))
        right.append(cells[2][c] - slope_gain * high * (cells[3][c] - cells[1][c]))
    return left, right


def face_flux(left, right):
    ul = left[1] / left[0]
    ur = right[1] / right[0]
    half_speed = 0.5 * (jnp.maximum(jnp.abs(ul), jnp.abs(ur)) + 1.0)
    fl = [left[1], left[1] * ul + left[0], left[2] * ul, left[3] * ul]
    fr = [right[1], right[1] * ur + right[0], right[2] * ur, right[3] * ur]
    return [0.5 * (fl[c] + fr[c]) - half_speed * (right[c] - left[c]) for c in range(4)]


def sign_of(values):
    return jnp.where(values > 0.0, 1.0, jnp.where(values < 0.0, -1.0, 0.0))


def face_flux_backward(left, right, d_flux):
    inv_l, inv_r = 1.0 / left[0], 1.0 / right[0]
    ul, ur = left[1] / left[0], right[1] / right[0]
    al, ar = jnp.abs(ul), jnp.abs(ur)
    half_speed = 0.5 * (jnp.maximum(al, ar) + 1.0)
    d_speed = -0.5 * sum(d_flux[c] * (right[c] - left[c]) for c in range(4))
    share = jnp.where(al > ar, 1.0, jnp.where(al < ar, 0.0, 0.5))
    half = [0.5 * d for d in d_flux]
    spread = [half_speed * d for d in d_flux]

    def one(state, u, inv, speed_part, sign):
        du = half[1] * state[1] + half[2] * state[2] + half[3] * state[3] + speed_part * sign_of(u)
        over = du * inv
        return [
            half[1] - over * u + sign * spread[0],
            half[0] + half[1] * u + over + sign * spread[1],
            half[2] * u + sign * spread[2],
            half[3] * u + sign * spread[3],
        ]

    return (
        one(left, ul, inv_l, d_speed * share, 1.0),
        one(right, ur, inv_r, d_speed * (1.0 - share), -1.0),
    )


def edge_backward(cells, gates, d_left, d_right):
    lows, highs = [], []
    direct = [[None] * 4 for _ in range(4)]
    for c in range(4):
        low = gates[FACES * c : FACES * (c + 1)]
        high = gates[FACES * (c + 4) : FACES * (c + 5)]
        lows.append(slope_gain * (cells[2][c] - cells[0][c]) * d_left[c])
        highs.append(-slope_gain * (cells[3][c] - cells[1][c]) * d_right[c])
        low_part = slope_gain * low * d_left[c]
        high_part = slope_gain * high * d_right[c]
        direct[0][c] = -low_part
        direct[1][c] = d_left[c] + high_part
        direct[2][c] = d_right[c] + low_part
        direct[3][c] = -high_part
    return stack(lows + highs) * (1.0 - gates * gates), direct


def turn(values, shift, axis):
    size = values.shape[axis]
    return values if shift % size == 0 else pltpu.roll(values, shift % size, axis)


def x_cells(tiles):
    return [[turn(t, -s, 0)[:FACES] for t in tiles] for s in range(4)]


def pack_kernel(den, mom, tra, cot, w_in, b_in, w_mid, b_mid, w_out, b_out,
                rim, first_x, first_y, first_bias, mid, mid_bias, out, out_bias,
                out_back, mid_back, first_x_back, first_y_back):
    nx, ny = den.shape[1:]
    segs = ny // SEG
    rows = nx // segs
    hid = w_in.shape[0]
    planes = [den.at[0], mom.at[0, 0], mom.at[0, 1], tra.at[0]] + [cot.at[0, c] for c in range(4)]
    lane = lax.broadcasted_iota(jnp.int32, (FACES, ny), 1)
    for v, plane in enumerate(planes):
        for at in range(0, rows, FACES):
            total = jnp.zeros((FACES, ny), F32)
            for s in range(segs):
                first = s * SEG + RIM
                moved = turn(plane[pl.ds(s * rows + at, FACES), :], first + RIM, 1)
                total = jnp.where((lane >= first) & (lane < first + 2 * RIM), moved, total)
            rim[v, pl.ds(at, FACES), :] = total

    wi, wm, wo = split3(w_in[...]), split3(w_mid[...]), split3(w_out[...])
    lanes = out_bias.shape[1]
    first_x[...] = build_first_x(wi, b_in[...], hid)
    first_y[...] = build_first_y(wi, hid)
    first_bias[...] = spread_bias(b_in[...], FACES * hid, lanes, lambda q: q % hid)
    mid[...] = build_mid(wm, hid)
    mid_bias[...] = spread_bias(b_mid[...], 2 * hid, lanes, lambda q: q % hid)
    out[...] = build_out(wo, hid)
    out_bias[...] = spread_bias(b_out[...], 64, lanes, lambda q: q >> 3)
    out_back[...] = build_out_back(wo, hid)
    mid_back[...] = build_mid_back(wm, hid)
    first_x_back[...] = build_first_x_back(wi, hid)
    first_y_back[...] = build_first_y_back(wi, hid)


def row_block(at):
    return pl.ds(pl.multiple_of(at * FACES, FACES), FACES)


def state_planes(den, mom, tra):
    return [den.at[0], mom.at[0, 0], mom.at[0, 1], tra.at[0]]


def x_tiles(planes, group, groups):
    after = jnp.where(group + 1 == groups, 0, group + 1)
    return [stack([plane[row_block(group), :], plane[row_block(after), :]]) for plane in planes]


def pair_tiles(planes, step, half):
    sets = [x_tiles(planes, step + k * half, PAIR * half) for k in range(PAIR)]
    return [side([one[c] for one in sets]) for c in range(len(planes))]


def x_forward(tiles, weights, hid):
    h1, h1_pair, h2, h2_pair, gates = limiter_forward(split3(stack(tiles)), weights, hid)
    cells = x_cells(tiles)
    return h1_pair, h2_pair, gates, face_flux(*edge_states(cells, gates))


def update_cells(plane_rows, flux_rows):
    upper = turn(flux_rows, -7, 0)[:FACES]
    lower = turn(flux_rows, -6, 0)[:FACES]
    return plane_rows - courant * (upper - lower)


def x_forward_kernel(den, mom, tra, first_x, mid, mid_bias, out, out_bias,
                     middle, h1_hi, h1_lo, h2_hi, h2_lo, gates_out,
                     flux, kept, kept_gates, sems):
    nx, ny = den.shape[1:]
    groups = nx // FACES
    half = groups // PAIR
    hid = mid.shape[0] // 4
    x_weights = (first_x, None, mid, mid_bias, out, out_bias)
    planes = state_planes(den, mom, tra)
    targets = [h1_hi, h1_lo, h2_hi, h2_lo]

    def copies(step):
        all_of = [
            pltpu.make_async_copy(kept.at[k, step], target.at[step], sems.at[k, step])
            for k, target in enumerate(targets)
        ]
        return all_of + [pltpu.make_async_copy(kept_gates.at[step], gates_out.at[step], sems.at[4, step])]

    def step_of(step, _):
        tiles = pair_tiles(planes, step, half)
        h1_pair, h2_pair, gates, fluxes = x_forward(tiles, x_weights, hid)
        for k, value in enumerate(h1_pair + h2_pair):
            kept[k, step] = value
        kept_gates[step] = gates
        for one in copies(step):
            one.start()
        for c in range(4):
            for k in range(PAIR):
                flux[c, row_block(step + k * half + 1), :] = fluxes[c][:, k * ny : (k + 1) * ny]
        return 0

    lax.fori_loop(0, half, step_of, 0)
    for c in range(4):
        flux[c, :FACES, :] = flux[c, nx : nx + FACES, :]

    def update(group, _):
        for c in range(4):
            both = stack([flux[c, row_block(group), :], flux[c, row_block(group + 1), :]])
            middle[c, row_block(group), :] = update_cells(planes[c][row_block(group), :], both)
        return 0

    lax.fori_loop(0, groups, update, 0)

    def finish(step, _):
        for one in copies(step):
            one.wait()
        return 0

    lax.fori_loop(0, half, finish, 0)


def y_order(planes):
    return [planes[0], planes[2], planes[1], planes[3]]


def lane_index(width):
    return lax.broadcasted_iota(jnp.int32, (FACES, width), 1)


def y_step(cells, cots, halo_mask, refs, hid):
    weights, out_back, mid_back, first_y_back = refs
    window = split3(stack([cells[s][c] for s in range(4) for c in range(4)]))
    h1, h1_pair, h2, h2_pair, gates = limiter_forward(window, weights, hid)
    left, right = edge_states(cells, gates)
    d_flux = [courant * (cots[1][c] - cots[0][c]) for c in range(4)]
    d_left, d_right = face_flux_backward(left, right, d_flux)
    if halo_mask is not None:
        d_left = [jnp.where(halo_mask, d, 0.0) for d in d_left]
        d_right = [jnp.where(halo_mask, d, 0.0) for d in d_right]
    d3_full, direct = edge_backward(cells, gates, d_left, d_right)
    d3, d2, d1 = limiter_backward(d3_full, h1, h2, out_back, mid_back, hid)
    d_window = first_backward(d1, first_y_back)
    parts = [
        [d_window[FACES * (4 * s + c) : FACES * (4 * s + c + 1)] + direct[s][c] for c in range(4)]
        for s in range(4)
    ]
    return parts, (window, h1_pair, h2_pair, d1, d2, d3, d3_full)


def y_gather(parts, ny):
    lane = lane_index(ny)
    out = []
    for c in range(4):
        a = turn(jnp.where(lane >= 1, parts[0][c], 0.0), -1, 1)
        b = turn(jnp.where(lane < ny - 1, parts[2][c], 0.0), 1, 1)
        d = turn(jnp.where(lane < ny - 2, parts[3][c], 0.0), 2, 1)
        out.append(parts[1][c] + a + b + d)
    return out


def fold_first_x(acc, hid):
    shape = acc.shape
    r, c = rows_cols(shape)
    fold = pick((shape[1], hid), lambda q, n: (q % hid) == n, F32)
    total = jnp.zeros((24, hid), F32)
    for s in range(4):
        keep = ((r & 15) - (c // hid) == s) & (r < 64)
        sel = lambda q, n: (n < 64) & (q == 4 * s + (n >> 4))
        if s == 0:
            keep = keep | (r >= 64)
            sel = lambda q, n: ((n < 64) & (q == (n >> 4))) | ((n == 64) & (q == 16))
        total = total + exact(pick((24, shape[0]), sel, F32), exact(jnp.where(keep, acc, 0.0), fold))
    return total


def fold_first_y(acc, hid):
    shape = acc.shape
    r, c = rows_cols(shape)
    fold = pick((shape[1], hid), lambda q, n: (q % hid) == n, F32)
    keep = ((r & 7) == (c // hid)) | (r >= 128)
    sel = lambda q, n: ((n < 128) & (q == (n >> 3))) | ((n == 128) & (q == 16))
    return exact(pick((24, shape[0]), sel, F32), exact(jnp.where(keep, acc, 0.0), fold))


def back_kernel(den, mom, tra, cot, middle, own, from_left, from_right,
                first_x, first_y, first_bias, mid, mid_bias, out, out_bias,
                out_back, mid_back, first_x_back, first_y_back,
                h1_hi, h1_lo, h2_hi, h2_lo, gates_in,
                g_den, g_mom, g_tra, g_weights,
                rim_state, rim_cot, rim_flux, rim_middle, rim_grad, d_middle,
                kept, kept_gates, acc_x, acc_y, acc_mid, acc_out, acc_out_bias, sems):
    nx, ny = den.shape[1:]
    groups = nx // FACES
    half = groups // PAIR
    hid = mid.shape[0] // 4
    x_weights = (first_x, None, mid, mid_bias, out, out_bias)
    segs = ny // SEG
    rim_rows = nx // segs
    rim_groups = rim_rows // FACES
    rim_half = rim_groups // PAIR

    fetches = [
        pltpu.make_async_copy(source, kept.at[k], sems.at[k])
        for k, source in enumerate([h1_hi, h1_lo, h2_hi, h2_lo])
    ] + [pltpu.make_async_copy(gates_in, kept_gates, sems.at[4])]
    for one in fetches:
        one.start()

    for acc in (acc_x, acc_y, acc_mid, acc_out, acc_out_bias):
        acc[...] = jnp.zeros(acc.shape, F32)

    lane = lane_index(ny)
    spot = lane & (SEG - 1)
    for v in range(8):
        for g in range(rim_groups):
            rows = pl.ds(g * FACES, FACES)
            mine = own[v, rows, :]
            value = jnp.where(
                spot < RIM,
                turn(from_left[v, rows, :], -RIM, 1),
                jnp.where(
                    spot < 2 * RIM,
                    turn(mine, -RIM, 1),
                    jnp.where(spot < 3 * RIM, turn(mine, RIM, 1), turn(from_right[v, rows, :], RIM, 1)),
                ),
            )
            if v < 4:
                rim_state[v, rows, :] = value
                if g == 0:
                    rim_state[v, pl.ds(rim_rows, FACES), :] = turn(value, -SEG, 1)
            else:
                rim_cot[v - 4, rows, :] = value

    def rim_forward(step, _):
        sets = [
            [
                stack([
                    rim_state[c, row_block(step + k * rim_half), :],
                    rim_state[c, row_block(step + k * rim_half + 1), :],
                ])
                for c in range(4)
            ]
            for k in range(PAIR)
        ]
        tiles = [side([one[c] for one in sets]) for c in range(4)]
        fluxes = x_forward(tiles, x_weights, hid)[3]
        for c in range(4):
            for k in range(PAIR):
                rim_flux[c, row_block(step + k * rim_half + 1), :] = fluxes[c][:, k * ny : (k + 1) * ny]
        return 0

    lax.fori_loop(0, rim_half, rim_forward, 0)
    for c in range(4):
        rim_flux[c, :FACES, :] = turn(rim_flux[c, rim_rows : rim_rows + FACES, :], SEG, 1)
        for g in range(rim_groups):
            rows = pl.ds(g * FACES, FACES)
            both = stack([rim_flux[c, rows, :], rim_flux[c, pl.ds((g + 1) * FACES, FACES), :]])
            rim_middle[c, rows, :] = update_cells(rim_state[c, rows, :], both)

    refs = ((first_y, first_bias, mid, mid_bias, out, out_bias), out_back, mid_back, first_y_back)
    spot_wide = lane_index(PAIR * ny) & (SEG - 1)
    rim_faces = (spot_wide == RIM - 2) | (spot_wide == RIM - 1) | (spot_wide == 3 * RIM)

    def rim_back(step, _):
        cells = [[[] for _ in range(4)] for _ in range(4)]
        cots = [[[] for _ in range(4)] for _ in range(2)]
        for k in range(PAIR):
            rows = row_block(step + k * rim_half)
            for c in range(4):
                value = rim_middle[c, rows, :]
                for s in range(4):
                    cells[s][c].append(turn(value, 1 - s, 1))
                value = rim_cot[c, rows, :]
                for s in range(2):
                    cots[s][c].append(turn(value, -s, 1))
        cells = [y_order([side(one) for one in row]) for row in cells]
        cots = [y_order([side(one) for one in row]) for row in cots]
        parts, _ = y_step(cells, cots, rim_faces, refs, hid)
        for k in range(PAIR):
            own_parts = [[one[:, k * ny : (k + 1) * ny] for one in row] for row in parts]
            gathered = y_order(y_gather(own_parts, ny))
            for c in range(4):
                rim_grad[c, row_block(step + k * rim_half), :] = gathered[c]
        return 0

    lax.fori_loop(0, rim_half, rim_back, 0)

    def main_y(step, _):
        cells = [[[] for _ in range(4)] for _ in range(4)]
        cots = [[[] for _ in range(4)] for _ in range(2)]
        for k in range(PAIR):
            group = step + k * half
            rows = row_block(group)
            seg = group // rim_groups
            rim_at = row_block(group - seg * rim_groups)
            to_low = ny - (seg * SEG + 3 * RIM)
            to_high = lax.rem(ny - 1 - (seg * SEG + RIM - 1) + ny, ny)
            for c in range(4):
                value = middle[c, rows, :]
                rim_value = rim_middle[c, rim_at, :]
                low = jnp.where(lane < 2, pltpu.roll(rim_value, to_low, 1), value)
                high = jnp.where(lane == ny - 1, pltpu.roll(rim_value, to_high, 1), value)
                cells[0][c].append(turn(high, 1, 1))
                cells[1][c].append(value)
                cells[2][c].append(turn(jnp.where(lane < 1, low, value), -1, 1))
                cells[3][c].append(turn(low, -2, 1))
                value = cot[0, c, rows, :]
                rim_value = rim_cot[c, rim_at, :]
                low = jnp.where(lane < 1, pltpu.roll(rim_value, to_low, 1), value)
                cots[0][c].append(value)
                cots[1][c].append(turn(low, -1, 1))
        cells = [y_order([side(one) for one in row]) for row in cells]
        cots = [y_order([side(one) for one in row]) for row in cots]
        parts, (window, h1_pair, h2_pair, d1, d2, d3, d3_full) = y_step(cells, cots, None, refs, hid)
        add_weight_grads(
            window, h1_pair, h2_pair, d1, d2, d3, d3_full, (acc_y, acc_mid, acc_out, acc_out_bias), hid
        )
        for k in range(PAIR):
            group = step + k * half
            rows = row_block(group)
            seg = group // rim_groups
            rim_at = row_block(group - seg * rim_groups)
            own_parts = [[one[:, k * ny : (k + 1) * ny] for one in row] for row in parts]
            gathered = y_order(y_gather(own_parts, ny))
            to_low = ny - (seg * SEG + RIM)
            to_high = lax.rem(ny - 1 - (seg * SEG + 3 * RIM - 1) + ny, ny)
            for c in range(4):
                rim_value = rim_grad[c, rim_at, :]
                from_rim = jnp.where(
                    lane < 2,
                    pltpu.roll(rim_value, to_low, 1),
                    jnp.where(lane == ny - 1, pltpu.roll(rim_value, to_high, 1), 0.0),
                )
                d_middle[c, rows, :] = cot[0, c, rows, :] + gathered[c] + from_rim
        return 0

    lax.fori_loop(0, half, main_y, 0)

    for one in fetches:
        one.wait()
    planes = state_planes(den, mom, tra)
    grads = state_planes(g_den, g_mom, g_tra)
    d_planes = [d_middle.at[c] for c in range(4)]

    def main_x(step, carry):
        tiles = pair_tiles(planes, step, half)
        d_tiles = pair_tiles(d_planes, step, half)
        gates = kept_gates[step]
        h1_pair = (kept[0, step], kept[1, step])
        h2_pair = (kept[2, step], kept[3, step])
        h1 = h1_pair[0].astype(F32) + h1_pair[1].astype(F32)
        h2 = h2_pair[0].astype(F32) + h2_pair[1].astype(F32)
        cells = x_cells(tiles)
        left, right = edge_states(cells, gates)
        d_flux = [courant * (turn(d, -2, 0)[:FACES] - turn(d, -1, 0)[:FACES]) for d in d_tiles]
        d_left, d_right = face_flux_backward(left, right, d_flux)
        d3_full, direct = edge_backward(cells, gates, d_left, d_right)
        d3, d2, d1 = limiter_backward(d3_full, h1, h2, out_back, mid_back, hid)
        d_window = first_backward(d1, first_x_back)
        add_weight_grads(
            split(stack(tiles)), h1_pair, h2_pair, d1, d2, d3, d3_full,
            (acc_x, acc_mid, acc_out, acc_out_bias), hid,
        )
        later = []
        for c in range(4):
            total = d_window[2 * FACES * c : 2 * FACES * (c + 1)]
            for s in range(4):
                total = total + turn(stack([direct[s][c], jnp.zeros_like(direct[s][c])]), s, 0)
            now = total[:FACES] + d_tiles[c][:FACES] + carry[c]
            for k in range(PAIR):
                grads[c][row_block(step + k * half), :] = now[:, k * ny : (k + 1) * ny]
            later.append(total[FACES:])
        return tuple(later)

    start = tuple(jnp.zeros((FACES, PAIR * ny), F32) for _ in range(4))
    last = lax.fori_loop(0, half, main_x, start)
    for c in range(4):
        for k in range(PAIR):
            at = (k + 1) % PAIR * half * FACES
            grads[c][pl.ds(at, FACES), :] += last[c][:, k * ny : (k + 1) * ny]

    g_weights[...] = jnp.zeros(g_weights.shape, F32)
    eye = pick((hid, hid), lambda q, n: q == n, F32)
    grad_first = fold_first_x(acc_x[...], hid) + fold_first_y(acc_y[...], hid)
    g_weights[0:hid, 0:16] = exact_nt(eye, grad_first[:16])
    both = acc_mid[...]
    grad_mid = both[:hid, :hid] + both[:hid, hid:] + both[hid : 2 * hid, :hid]
    g_weights[hid : 2 * hid, 0:hid] = exact_nt(eye, grad_mid)
    grad_mid_bias = both[2 * hid :, :hid] + both[2 * hid :, hid:]
    r, c = rows_cols(acc_out.shape)
    fold = pick((acc_out.shape[1], hid), lambda q, n: (q % hid) == n, F32)
    rows = pick((8, 64), lambda q, n: (n >> 3) == q, F32)
    g_weights[2 * hid : 2 * hid + 8, 0:hid] = exact(
        rows, exact(jnp.where((r & 7) == (c // hid), acc_out[...], 0.0), fold)
    )
    out_bias_rows = exact_nt(jnp.ones((8, acc_out_bias.shape[1]), F32), acc_out_bias[...])
    r, c = rows_cols((8, hid))
    g_weights[2 * hid + 8 : 2 * hid + 16, 0:hid] = jnp.where(
        r == 0, grad_first[16:24], jnp.where(r == 1, grad_mid_bias[:8], 0.0)
    )
    g_weights[2 * hid + 16 : 2 * hid + 24, 0:8] = exact_nt(out_bias_rows, rows)


def whole(count, space=pltpu.VMEM):
    return [pl.BlockSpec(memory_space=space)] * count


def call(kernel, outs, operands, out_spaces=None, in_spaces=None, scratch=(), flops=0, moved=0):
    return pl.pallas_call(
        kernel,
        out_shape=outs,
        in_specs=in_spaces or whole(len(operands)),
        out_specs=out_spaces or whole(len(outs)),
        scratch_shapes=list(scratch),
        compiler_params=pltpu.CompilerParams(vmem_limit_bytes=VMEM_BYTES),
        cost_estimate=pl.CostEstimate(flops=flops, bytes_accessed=moved, transcendentals=0),
    )(*operands)


def body(ring, density, momentum, tracer, cotangent, w_in, b_in, w_mid, b_mid, w_out, b_out):
    nx, ny = density.shape[1:]
    hid = w_in.shape[0]
    wide = FACES * hid
    groups = nx // FACES
    half = groups // PAIR
    lanes = PAIR * ny
    segs = ny // SEG
    rim_rows = nx // segs
    shape = jax.ShapeDtypeStruct

    rim, *matrices = call(
        pack_kernel,
        [
            shape((8, rim_rows, ny), F32),
            shape((wide, 6 * 64 + ONES), BF16),
            shape((wide, 6 * 128), BF16),
            shape((wide, lanes), F32),
            shape((4 * hid, 8 * hid), BF16),
            shape((2 * hid, lanes), F32),
            shape((192, wide), BF16),
            shape((64, lanes), F32),
            shape((wide, 192), BF16),
            shape((2 * hid, 6 * hid), BF16),
            shape((128, 2 * wide), BF16),
            shape((256, 2 * wide), BF16),
        ],
        [density, momentum, tracer, cotangent, w_in, b_in[None], w_mid, b_mid[None], w_out, b_out[None]],
    )
    axes = ("tx", "ty")
    from_left = lax.ppermute(rim, axes, [(i, (i + 1) % ring) for i in range(ring)])
    from_right = lax.ppermute(rim, axes, [((i + 1) % ring, i) for i in range(ring)])

    middle, h1_hi, h1_lo, h2_hi, h2_lo, gates = call(
        x_forward_kernel,
        [shape((4, nx, ny), F32)]
        + [shape((half, wide, lanes), BF16)] * 4
        + [shape((half, 64, lanes), F32)],
        [density, momentum, tracer, matrices[0]] + matrices[3:7],
        out_spaces=whole(1) + whole(5, pl.ANY),
        scratch=[
            pltpu.VMEM((4, nx + FACES, ny), F32),
            pltpu.VMEM((4, half, wide, lanes), BF16),
            pltpu.VMEM((half, 64, lanes), F32),
            pltpu.SemaphoreType.DMA((5, half)),
        ],
        flops=10**10,
        moved=10**7,
    )
    g_den, g_mom, g_tra, g_weights = call(
        back_kernel,
        [
            shape(density.shape, F32),
            shape(momentum.shape, F32),
            shape(tracer.shape, F32),
            shape((2 * hid + 24, 128), F32),
        ],
        [density, momentum, tracer, cotangent, middle, rim, from_left, from_right]
        + matrices
        + [h1_hi, h1_lo, h2_hi, h2_lo, gates],
        in_spaces=whole(19) + whole(5, pl.ANY),
        scratch=[
            pltpu.VMEM((4, rim_rows + FACES, ny), F32),
            pltpu.VMEM((4, rim_rows, ny), F32),
            pltpu.VMEM((4, rim_rows + FACES, ny), F32),
            pltpu.VMEM((4, rim_rows, ny), F32),
            pltpu.VMEM((4, rim_rows, ny), F32),
            pltpu.VMEM((4, nx, ny), F32),
            pltpu.VMEM((4, half, wide, lanes), BF16),
            pltpu.VMEM((half, 64, lanes), F32),
            pltpu.VMEM((64 + ONES, wide), F32),
            pltpu.VMEM((128 + ONES, wide), F32),
            pltpu.VMEM((2 * hid + ONES, 2 * hid), F32),
            pltpu.VMEM((64, wide), F32),
            pltpu.VMEM((64, lanes), F32),
            pltpu.SemaphoreType.DMA((5,)),
        ],
        flops=4 * 10**10,
        moved=2 * 10**7,
    )
    totals = lax.psum(g_weights, ("traj", "tx", "ty"))
    return (
        g_den,
        g_mom,
        g_tra,
        totals[:hid, :16],
        totals[2 * hid + 8, :hid],
        totals[hid : 2 * hid, :hid],
        totals[2 * hid + 9, :hid],
        totals[2 * hid : 2 * hid + 8, :hid],
        totals[2 * hid + 16, :8],
    )


def solution(mesh):
    flow = P("traj", None, ("tx", "ty"))
    deep = P("traj", None, None, ("tx", "ty"))
    ring = mesh.shape["tx"] * mesh.shape["ty"]
    return jax.shard_map(
        functools.partial(body, ring),
        mesh=mesh,
        in_specs=(flow, deep, flow, deep) + (P(),) * 6,
        out_specs=(flow, deep, flow) + (P(),) * 6,
        check_vma=False,
    )
```

profile of v0, /device:TPU:0, one launch (start us, length us, event | category | flops | bytes accessed | tf_op | source)
XLA Modules:
  0.0 132.4 jit_solution(12788234378659349930)
XLA Ops:
  0.6 0.8 copy.19.w_in
  1.4 1.0 copy-done
  2.5 0.9 copy-done.2
  3.4 0.9 copy-done.3
  4.3 0.9 copy-done.4
  5.2 0.7 copy-done.5
  5.9 0.7 copy-done.6
  6.6 0.7 copy-done.7
  7.3 0.7 copy-done.8
  7.9 0.7 copy-done.9
  8.6 3.0 %shard_map.169 = (f32[8,32,128]{2,1,0:T(8,128)S(1)}, bf16[256,400]{1,0:T(8,128)(2,1)S(1)}, bf16[256,768]{1,0:T(8,128)(2,1)S(1)}, f32[256,256]{1,0:T(8,128)S(1)},...) custom-call(f32[1,256,128]{2,1,0:T(8,128)S(1)} %copy-done.3, ...), custom_call_target="tpu_custom_call" | custom-call | tf_op jit(solution)/shard_map/pallas_call | solution.py:757
  11.6 6.1 %collective-permute-start.1 = (f32[8,32,128]{2,1,0:T(8,128)S(1)}, f32[8,32,128]{2,1,0:T(8,128)S(1)}, u32[]{:S(2)}, u32[]{:S(2)}) collective-permute-start(f32[8,32,128]{2,1,0:T(8,128)S(1)} %get-tuple-element.37.own), channel_id=1, source_target_pairs={{1,0},{2,1},{3,2},{4,3},{5,4},{6,5},{7,6},{0,7},{9,8},{10,9},{11,1... | collective-permute-start | bytes 393224 | tf_op jit(solution)/shard_map/ppermute | solution.py:799
  17.6 0.0 collective-permute-start
  17.6 17.3 %shard_map.170 = (f32[4,256,128]{2,1,0:T(8,128)S(1)}, bf16[16,256,256]{2,1,0:T(8,128)(2,1)S(1)}, bf16[16,256,256]{2,1,0:T(8,128)(2,1)}, bf16[16,256,256]{2,1,0:T...) custom-call(f32[1,256,128]{2,1,0:T(8,128)S(1)} %copy-done.3, f32[1,2,256,128]{3,2,1,0:T(8,128)S(1)} %copy-done.2, ...), custom_call_target="tpu_custom_call" | custom-call | flops 10000000000 | bytes 10000000 | tf_op jit(solution)/shard_map/pallas_call | solution.py:757
  34.9 1.3 %copy-done.10 = bf16[16,256,256]{2,1,0:T(8,128)(2,1)} copy-done((bf16[16,256,256]{2,1,0:T(8,128)(2,1)}, bf16[16,256,256]{2,1,0:T(8,128)(2,1)S(1)}, u32[]{:S(2)}) %copy-start.10) | copy-done | bytes 2097176
  36.2 0.0 collective-permute-done.1.from_right
  36.2 0.0 collective-permute-done.from_left
  36.3 52.7 %shard_map.171 = (f32[1,256,128]{2,1,0:T(8,128)}, f32[1,2,256,128]{3,2,1,0:T(8,128)}, f32[1,256,128]{2,1,0:T(8,128)}, f32[88,128]{1,0:T(8,128)S(1)}) custom-call(f32[1,256,128]{2,1,0:T(8,128)S(1)} %copy-done.3, f32[1,2,256,128]{3,2,1,0:T(8,128)S(1)} %copy-done.2, f32[1,256,128]{2,1,0:T(8,128)S(1)} %copy-done.4, f32[1,4,256,128]{3,2,1,0:T(8,128)S(1)} %copy-done.1, ...), custom_call_target="tpu_custom_call" | custom-call | flops 40000000000 | bytes 20000000 | tf_op jit(solution)/shard_map/pallas_call | solution.py:757
  89.0 40.5 %psum.7 = f32[88,128]{1,0:T(8,128)S(1)} all-reduce(f32[88,128]{1,0:T(8,128)S(1)} %get-tuple-element.52), channel_id=1, replica_groups=mesh['traj'=4,'tx'=2,'ty'=4] {'traj','tx','ty'}, use_global_device_ids=true, to_apply=%region_0.0 | all-reduce | flops 11264 | bytes 90112 | tf_op jit(solution)/shard_map/psum | solution.py:848
  129.5 0.5 slice_bitcast_fusion
  130.0 0.5 slice_bitcast_fusion.1
  130.5 0.6 slice.28
  131.1 0.6 slice.26
  131.7 0.7 copy.20
  (13 shorter events, 0.0 us)
Async XLA Ops:
  1.4 1.0 copy-start
  2.5 0.9 copy-start.2
  3.4 0.9 copy-start.3
  4.3 0.9 copy-start.4
  5.2 0.7 copy-start.5
  5.9 0.7 copy-start.6
  6.6 0.7 copy-start.7
  7.3 0.7 copy-start.8
  7.9 0.7 copy-start.9
  11.6 24.7 %collective-permute-start.1 = (f32[8,32,128]{2,1,0:T(8,128)S(1)}, f32[8,32,128]{2,1,0:T(8,128)S(1)}, u32[]{:S(2)}, u32[]{:S(2)}) collective-permute-start(f32[8,32,128]{2,1,0:T(8,128)S(1)} %get-tuple-element.37.own), channel_id=1, source_target_pairs={{1,0},{2,1},{3,2},{4,3},{5,4},{6,5},{7,6},{0,7},{9,8},{10,9},{11,1... | collective-permute-start | bytes 393224 | tf_op jit(solution)/shard_map/ppermute | solution.py:799
  17.6 18.6 %collective-permute-start = (f32[8,32,128]{2,1,0:T(8,128)S(1)}, f32[8,32,128]{2,1,0:T(8,128)S(1)}, u32[]{:S(2)}, u32[]{:S(2)}) collective-permute-start(f32[8,32,128]{2,1,0:T(8,128)S(1)} %get-tuple-element.37.own), channel_id=1, source_target_pairs={{0,1},{1,2},{2,3},{3,4},{4,5},{5,6},{6,7},{7,0},{8,9},{9,10},{10,1... | collective-permute-start | bytes 393224 | tf_op jit(solution)/shard_map/ppermute | solution.py:798
  17.6 18.6 %copy-start.1 = (f32[1,4,256,128]{3,2,1,0:T(8,128)S(1)}, f32[1,4,256,128]{3,2,1,0:T(8,128)}, u32[]{:S(2)}) copy-start(f32[1,4,256,128]{3,2,1,0:T(8,128)} %cot.3) | copy-start | bytes 1572868
  34.9 1.3 %copy-start.10 = (bf16[16,256,256]{2,1,0:T(8,128)(2,1)}, bf16[16,256,256]{2,1,0:T(8,128)(2,1)S(1)}, u32[]{:S(2)}) copy-start(bf16[16,256,256]{2,1,0:T(8,128)(2,1)S(1)} %get-tuple-element.44.h1_hi) | copy-start | bytes 6291460
where the time goes:
time: 133 us; the launch traced here: 132 us
  Pallas kernels  72.9 us (55%)
  blocking collectives  40.5 us (30%)
  local copies, waits for them, and re-layouts  12.2 us (9%)
  starting transfers between devices  6.05 us (5%)
    pallas_call x3, Pallas kernels, call(): pl.pallas_call(kernel, out_shape=outs, in_specs=in_spaces or whole(len(op...  72.9 us
    psum x1, blocking collectives, body(): totals = lax.psum(g_weights, ('traj', 'tx', 'ty'))  40.5 us
    unnamed x24, local copies, waits for them, and re-layouts  9.95 us
    ppermute x1, starting transfers between devices, body(): lax.ppermute(rim, axes, [((i + 1) % ring, i) for i in range(ring)])  6.05 us
  transfers between devices with their start and end apart: 2, of which 0 were waited for; matrix products, arithmetic and copies ran while one was open for 0% of the time, Pallas kernels for 13%

commit v1 on v0

--- a/solution.py
+++ b/solution.py
@@ -14,9 +14,9 @@
 FACES = 8
 SEG = 16
 RIM = 4
-PAIR = 2
+PAIR = 4
 ONES = 16
-VMEM_BYTES = 48 * 2**20
+VMEM_BYTES = 32 * 2**20
 
 
 def dot(a, b):
@@ -354,24 +354,33 @@
 
 
 def pack_kernel(den, mom, tra, cot, w_in, b_in, w_mid, b_mid, w_out, b_out,
-                rim, first_x, first_y, first_bias, mid, mid_bias, out, out_bias,
-                out_back, mid_back, first_x_back, first_y_back):
+                rim, state, cots, first_x, first_y, first_bias, mid, mid_bias, out, out_bias,
+                out_back, mid_back, first_x_back, first_y_back, *scratch):
+    *small, sems = scratch
     nx, ny = den.shape[1:]
     segs = ny // SEG
     rows = nx // segs
-    hid = w_in.shape[0]
-    planes = [den.at[0], mom.at[0, 0], mom.at[0, 1], tra.at[0]] + [cot.at[0, c] for c in range(4)]
-    lane = lax.broadcasted_iota(jnp.int32, (FACES, ny), 1)
-    for v, plane in enumerate(planes):
-        for at in range(0, rows, FACES):
-            total = jnp.zeros((FACES, ny), F32)
-            for s in range(segs):
-                first = s * SEG + RIM
-                moved = turn(plane[pl.ds(s * rows + at, FACES), :], first + RIM, 1)
-                total = jnp.where((lane >= first) & (lane < first + 2 * RIM), moved, total)
-            rim[v, pl.ds(at, FACES), :] = total
-
-    wi, wm, wo = split3(w_in[...]), split3(w_mid[...]), split3(w_out[...])
+    hid = w_in.shape[1]
+    copies = [
+        pltpu.make_async_copy(source, target, sems.at[k])
+        for k, (source, target) in enumerate(
+            list(zip([w_in, b_in, w_mid, b_mid, w_out, b_out], small))
+            + [
+                (den.at[0], state.at[0]),
+                (mom.at[0], state.at[pl.ds(1, 2)]),
+                (tra.at[0], state.at[3]),
+                (cot.at[0], cots),
+            ]
+        )
+    ]
+    for one in copies:
+        one.start()
+    for one in copies[:6]:
+        one.wait()
+    w_in, b_in, w_mid, b_mid, w_out, b_out = small
+    eye = pick((hid, hid), lambda q, n: q == n)
+    wi = [dot_nt(eye, level).astype(BF16) for level in split3(w_in[...])]
+    wm, wo = split3(w_mid[...]), split3(w_out[...])
     lanes = out_bias.shape[1]
     first_x[...] = build_first_x(wi, b_in[...], hid)
     first_y[...] = build_first_y(wi, hid)
@@ -385,13 +394,22 @@
     first_x_back[...] = build_first_x_back(wi, hid)
     first_y_back[...] = build_first_y_back(wi, hid)
 
+    for one in copies[6:]:
+        one.wait()
+    lane = lane_index(ny)
+    for v in range(8):
+        plane = state.at[v] if v < 4 else cots.at[v - 4]
+        for at in range(0, rows, FACES):
+            total = jnp.zeros((FACES, ny), F32)
+            for s in range(segs):
+                first = s * SEG + RIM
+                moved = turn(plane[pl.ds(s * rows + at, FACES), :], first + RIM, 1)
+                total = jnp.where((lane >= first) & (lane < first + 2 * RIM), moved, total)
+            rim[v, pl.ds(at, FACES), :] = total
+
 
 def row_block(at):
     return pl.ds(pl.multiple_of(at * FACES, FACES), FACES)
-
-
-def state_planes(den, mom, tra):
-    return [den.at[0], mom.at[0, 0], mom.at[0, 1], tra.at[0]]
 
 
 def x_tiles(planes, group, groups):
@@ -416,32 +434,20 @@
     return plane_rows - courant * (upper - lower)
 
 
-def x_forward_kernel(den, mom, tra, first_x, mid, mid_bias, out, out_bias,
-                     middle, h1_hi, h1_lo, h2_hi, h2_lo, gates_out,
-                     flux, kept, kept_gates, sems):
-    nx, ny = den.shape[1:]
+def x_forward_kernel(state, first_x, mid, mid_bias, out, out_bias,
+                     middle, h1_hi, h1_lo, h2_hi, h2_lo, gates_out, flux):
+    nx, ny = state.shape[1:]
     groups = nx // FACES
     half = groups // PAIR
     hid = mid.shape[0] // 4
     x_weights = (first_x, None, mid, mid_bias, out, out_bias)
-    planes = state_planes(den, mom, tra)
-    targets = [h1_hi, h1_lo, h2_hi, h2_lo]
-
-    def copies(step):
-        all_of = [
-            pltpu.make_async_copy(kept.at[k, step], target.at[step], sems.at[k, step])
-            for k, target in enumerate(targets)
-        ]
-        return all_of + [pltpu.make_async_copy(kept_gates.at[step], gates_out.at[step], sems.at[4, step])]
+    planes = [state.at[c] for c in range(4)]
 
     def step_of(step, _):
         tiles = pair_tiles(planes, step, half)
         h1_pair, h2_pair, gates, fluxes = x_forward(tiles, x_weights, hid)
-        for k, value in enumerate(h1_pair + h2_pair):
-            kept[k, step] = value
-        kept_gates[step] = gates
-        for one in copies(step):
-            one.start()
+        for target, value in zip((h1_hi, h1_lo, h2_hi, h2_lo, gates_out), h1_pair + h2_pair + (gates,)):
+            target[step] = value
         for c in range(4):
             for k in range(PAIR):
                 flux[c, row_block(step + k * half + 1), :] = fluxes[c][:, k * ny : (k + 1) * ny]
@@ -458,13 +464,6 @@
         return 0
 
     lax.fori_loop(0, groups, update, 0)
-
-    def finish(step, _):
-        for one in copies(step):
-            one.wait()
-        return 0
-
-    lax.fori_loop(0, half, finish, 0)
 
 
 def y_order(planes):
@@ -530,14 +529,14 @@
     return exact(pick((24, shape[0]), sel, F32), exact(jnp.where(keep, acc, 0.0), fold))
 
 
-def back_kernel(den, mom, tra, cot, middle, own, from_left, from_right,
+def back_kernel(state, cot, middle, own, from_left, from_right,
                 first_x, first_y, first_bias, mid, mid_bias, out, out_bias,
                 out_back, mid_back, first_x_back, first_y_back,
                 h1_hi, h1_lo, h2_hi, h2_lo, gates_in,
                 g_den, g_mom, g_tra, g_weights,
                 rim_state, rim_cot, rim_flux, rim_middle, rim_grad, d_middle,
-                kept, kept_gates, acc_x, acc_y, acc_mid, acc_out, acc_out_bias, sems):
-    nx, ny = den.shape[1:]
+                acc_x, acc_y, acc_mid, acc_out, acc_out_bias):
+    nx, ny = state.shape[1:]
     groups = nx // FACES
     half = groups // PAIR
     hid = mid.shape[0] // 4
@@ -546,13 +545,6 @@
     rim_rows = nx // segs
     rim_groups = rim_rows // FACES
     rim_half = rim_groups // PAIR
-
-    fetches = [
-        pltpu.make_async_copy(source, kept.at[k], sems.at[k])
-        for k, source in enumerate([h1_hi, h1_lo, h2_hi, h2_lo])
-    ] + [pltpu.make_async_copy(gates_in, kept_gates, sems.at[4])]
-    for one in fetches:
-        one.start()
 
     for acc in (acc_x, acc_y, acc_mid, acc_out, acc_out_bias):
         acc[...] = jnp.zeros(acc.shape, F32)
@@ -652,7 +644,7 @@
                 cells[1][c].append(value)
                 cells[2][c].append(turn(jnp.where(lane < 1, low, value), -1, 1))
                 cells[3][c].append(turn(low, -2, 1))
-                value = cot[0, c, rows, :]
+                value = cot[c, rows, :]
                 rim_value = rim_cot[c, rim_at, :]
                 low = jnp.where(lane < 1, pltpu.roll(rim_value, to_low, 1), value)
                 cots[0][c].append(value)
@@ -679,23 +671,21 @@
                     pltpu.roll(rim_value, to_low, 1),
                     jnp.where(lane == ny - 1, pltpu.roll(rim_value, to_high, 1), 0.0),
                 )
-                d_middle[c, rows, :] = cot[0, c, rows, :] + gathered[c] + from_rim
+                d_middle[c, rows, :] = cot[c, rows, :] + gathered[c] + from_rim
         return 0
 
     lax.fori_loop(0, half, main_y, 0)
 
-    for one in fetches:
-        one.wait()
-    planes = state_planes(den, mom, tra)
-    grads = state_planes(g_den, g_mom, g_tra)
+    planes = [state.at[c] for c in range(4)]
+    grads = [g_den.at[0], g_mom.at[0, 0], g_mom.at[0, 1], g_tra.at[0]]
     d_planes = [d_middle.at[c] for c in range(4)]
 
     def main_x(step, carry):
         tiles = pair_tiles(planes, step, half)
         d_tiles = pair_tiles(d_planes, step, half)
-        gates = kept_gates[step]
-        h1_pair = (kept[0, step], kept[1, step])
-        h2_pair = (kept[2, step], kept[3, step])
+        gates = gates_in[step]
+        h1_pair = (h1_hi[step], h1_lo[step])
+        h2_pair = (h2_hi[step], h2_lo[step])
         h1 = h1_pair[0].astype(F32) + h1_pair[1].astype(F32)
         h2 = h2_pair[0].astype(F32) + h2_pair[1].astype(F32)
         cells = x_cells(tiles)
@@ -727,26 +717,40 @@
             at = (k + 1) % PAIR * half * FACES
             grads[c][pl.ds(at, FACES), :] += last[c][:, k * ny : (k + 1) * ny]
 
-    g_weights[...] = jnp.zeros(g_weights.shape, F32)
     eye = pick((hid, hid), lambda q, n: q == n, F32)
     grad_first = fold_first_x(acc_x[...], hid) + fold_first_y(acc_y[...], hid)
-    g_weights[0:hid, 0:16] = exact_nt(eye, grad_first[:16])
     both = acc_mid[...]
     grad_mid = both[:hid, :hid] + both[:hid, hid:] + both[hid : 2 * hid, :hid]
-    g_weights[hid : 2 * hid, 0:hid] = exact_nt(eye, grad_mid)
     grad_mid_bias = both[2 * hid :, :hid] + both[2 * hid :, hid:]
     r, c = rows_cols(acc_out.shape)
     fold = pick((acc_out.shape[1], hid), lambda q, n: (q % hid) == n, F32)
     rows = pick((8, 64), lambda q, n: (n >> 3) == q, F32)
-    g_weights[2 * hid : 2 * hid + 8, 0:hid] = exact(
-        rows, exact(jnp.where((r & 7) == (c // hid), acc_out[...], 0.0), fold)
-    )
+    grad_out = exact(rows, exact(jnp.where((r & 7) == (c // hid), acc_out[...], 0.0), fold))
     out_bias_rows = exact_nt(jnp.ones((8, acc_out_bias.shape[1]), F32), acc_out_bias[...])
+    grad_out_bias = exact_nt(out_bias_rows, pick((hid, 64), lambda q, n: (n >> 3) == q, F32))
     r, c = rows_cols((8, hid))
-    g_weights[2 * hid + 8 : 2 * hid + 16, 0:hid] = jnp.where(
-        r == 0, grad_first[16:24], jnp.where(r == 1, grad_mid_bias[:8], 0.0)
-    )
-    g_weights[2 * hid + 16 : 2 * hid + 24, 0:8] = exact_nt(out_bias_rows, rows)
+    biases = jnp.where(
+        r == 0,
+        grad_first[16:24],
+        jnp.where(r == 1, jnp.broadcast_to(grad_mid_bias[:1], (8, hid)), jnp.where(r == 2, grad_out_bias, 0.0)),
+    )
+    width = g_weights.shape[1]
+    beside = stack([grad_first[:16], grad_out, biases])
+    g_weights[...] = exact(
+        exact_nt(eye, grad_mid), pick((hid, width), lambda q, n: n == q, F32)
+    ) + exact(beside, pick((hid, width), lambda q, n: n == q + hid, F32))
+
+
+def finish_kernel(one, other, g_w_in, g_b_in, g_w_mid, g_b_mid, g_w_out, g_b_out):
+    hid = g_w_mid.shape[0]
+    total = one[...] + other[...]
+    g_w_mid[...] = total[:, :hid]
+    beside = total[:, hid : 2 * hid]
+    g_w_in[...] = beside[:16]
+    g_w_out[...] = beside[16:24]
+    g_b_in[...] = beside[24:25]
+    g_b_mid[...] = beside[25:26]
+    g_b_out[...] = beside[26:27, :8]
 
 
 def whole(count, space=pltpu.VMEM):
@@ -765,7 +769,17 @@
     )(*operands)
 
 
-def body(ring, density, momentum, tracer, cotangent, w_in, b_in, w_mid, b_mid, w_out, b_out):
+def others(values, axis, size):
+    return [lax.ppermute(values, axis, [(i, i ^ k) for i in range(size)]) for k in range(1, size)]
+
+
+def tree_sum(parts):
+    while len(parts) > 1:
+        parts = [parts[k] + parts[k + 1] for k in range(0, len(parts), 2)]
+    return parts[0]
+
+
+def body(sizes, density, momentum, tracer, cotangent, w_in, b_in, w_mid, b_mid, w_out, b_out):
     nx, ny = density.shape[1:]
     hid = w_in.shape[0]
     wide = FACES * hid
@@ -774,12 +788,18 @@
     lanes = PAIR * ny
     segs = ny // SEG
     rim_rows = nx // segs
+    ring = sizes["tx"] * sizes["ty"]
     shape = jax.ShapeDtypeStruct
 
-    rim, *matrices = call(
+    operands = [
+        density, momentum, tracer, cotangent, w_in.T, b_in[None], w_mid, b_mid[None], w_out, b_out[None]
+    ]
+    rim, state, cots, *matrices = call(
         pack_kernel,
         [
             shape((8, rim_rows, ny), F32),
+            shape((4, nx, ny), F32),
+            shape((4, nx, ny), F32),
             shape((wide, 6 * 64 + ONES), BF16),
             shape((wide, 6 * 128), BF16),
             shape((wide, lanes), F32),
@@ -792,25 +812,21 @@
             shape((128, 2 * wide), BF16),
             shape((256, 2 * wide), BF16),
         ],
-        [density, momentum, tracer, cotangent, w_in, b_in[None], w_mid, b_mid[None], w_out, b_out[None]],
+        operands,
+        in_spaces=whole(10, pltpu.HBM),
+        scratch=[pltpu.VMEM(one.shape, F32) for one in operands[4:]] + [pltpu.SemaphoreType.DMA((10,))],
     )
     axes = ("tx", "ty")
     from_left = lax.ppermute(rim, axes, [(i, (i + 1) % ring) for i in range(ring)])
     from_right = lax.ppermute(rim, axes, [((i + 1) % ring, i) for i in range(ring)])
 
-    middle, h1_hi, h1_lo, h2_hi, h2_lo, gates = call(
+    middle, *kept = call(
         x_forward_kernel,
         [shape((4, nx, ny), F32)]
         + [shape((half, wide, lanes), BF16)] * 4
         + [shape((half, 64, lanes), F32)],
-        [density, momentum, tracer, matrices[0]] + matrices[3:7],
-        out_spaces=whole(1) + whole(5, pl.ANY),
-        scratch=[
-            pltpu.VMEM((4, nx + FACES, ny), F32),
-            pltpu.VMEM((4, half, wide, lanes), BF16),
-            pltpu.VMEM((half, 64, lanes), F32),
-            pltpu.SemaphoreType.DMA((5, half)),
-        ],
+        [state, matrices[0]] + matrices[3:7],
+        scratch=[pltpu.VMEM((4, nx + FACES, ny), F32)],
         flops=10**10,
         moved=10**7,
     )
@@ -820,12 +836,9 @@
             shape(density.shape, F32),
             shape(momentum.shape, F32),
             shape(tracer.shape, F32),
-            shape((2 * hid + 24, 128), F32),
+            shape((hid, 128), F32),
         ],
-        [density, momentum, tracer, cotangent, middle, rim, from_left, from_right]
-        + matrices
-        + [h1_hi, h1_lo, h2_hi, h2_lo, gates],
-        in_spaces=whole(19) + whole(5, pl.ANY),
+        [state, cots, middle, rim, from_left, from_right] + matrices + kept,
         scratch=[
             pltpu.VMEM((4, rim_rows + FACES, ny), F32),
             pltpu.VMEM((4, rim_rows, ny), F32),
@@ -833,38 +846,38 @@
             pltpu.VMEM((4, rim_rows, ny), F32),
             pltpu.VMEM((4, rim_rows, ny), F32),
             pltpu.VMEM((4, nx, ny), F32),
-            pltpu.VMEM((4, half, wide, lanes), BF16),
-            pltpu.VMEM((half, 64, lanes), F32),
             pltpu.VMEM((64 + ONES, wide), F32),
             pltpu.VMEM((128 + ONES, wide), F32),
             pltpu.VMEM((2 * hid + ONES, 2 * hid), F32),
             pltpu.VMEM((64, wide), F32),
             pltpu.VMEM((64, lanes), F32),
-            pltpu.SemaphoreType.DMA((5,)),
         ],
         flops=4 * 10**10,
         moved=2 * 10**7,
     )
-    totals = lax.psum(g_weights, ("traj", "tx", "ty"))
-    return (
-        g_den,
-        g_mom,
-        g_tra,
-        totals[:hid, :16],
-        totals[2 * hid + 8, :hid],
-        totals[hid : 2 * hid, :hid],
-        totals[2 * hid + 9, :hid],
-        totals[2 * hid : 2 * hid + 8, :hid],
-        totals[2 * hid + 16, :8],
-    )
+    totals = tree_sum([g_weights] + others(g_weights, "traj", sizes["traj"]))
+    totals = tree_sum([totals] + others(totals, "ty", sizes["ty"]))
+    parts = [totals] + others(totals, "tx", sizes["tx"])
+    g_w_in, g_b_in, g_w_mid, g_b_mid, g_w_out, g_b_out = call(
+        finish_kernel,
+        [
+            shape((w_in.shape[1], hid), F32),
+            shape((1, hid), F32),
+            shape(w_mid.shape, F32),
+            shape((1, hid), F32),
+            shape(w_out.shape, F32),
+            shape((1, b_out.shape[0]), F32),
+        ],
+        [tree_sum(parts[: len(parts) // 2]), tree_sum(parts[len(parts) // 2 :])],
+    )
+    return (g_den, g_mom, g_tra, g_w_in.T, g_b_in[0], g_w_mid, g_b_mid[0], g_w_out, g_b_out[0])
 
 
 def solution(mesh):
     flow = P("traj", None, ("tx", "ty"))
     deep = P("traj", None, None, ("tx", "ty"))
-    ring = mesh.shape["tx"] * mesh.shape["ty"]
     return jax.shard_map(
-        functools.partial(body, ring),
+        functools.partial(body, dict(mesh.shape)),
         mesh=mesh,
         in_specs=(flow, deep, flow, deep) + (P(),) * 6,
         out_specs=(flow, deep, flow) + (P(),) * 6,

time: 133 us -> 80 us (0.60)
  blocking collectives: 40.5 us -> 0 us
  Pallas kernels: 72.9 us -> 48.5 us
  waiting for transfers between devices: 0.01 us -> 8.51 us
  starting transfers between devices: 6.05 us -> 14 us
  local copies, waits for them, and re-layouts: 12.2 us -> 7.86 us
    psum x1 -> x0, blocking collectives: 40.5 us -> none  [body(): totals = lax.psum(g_weights, ('traj', 'tx', 'ty'))]
    pallas_call x3 -> x4, Pallas kernels: 72.9 us -> 48.5 us  [call(): pl.pallas_call(kernel, out_shape=outs, in_specs=in_spaces or whole(len(op...]
    ppermute x0 -> x7, waiting for transfers between devices: none -> 8.25 us  [others(): lax.ppermute(values, axis, [(i, i ^ k) for i in range(size)])]
    ppermute x0 -> x7, starting transfers between devices: none -> 7.91 us  [others(): lax.ppermute(values, axis, [(i, i ^ k) for i in range(size)])]
    unnamed x24 -> x20, local copies, waits for them, and re-layouts: 9.95 us -> 7.86 us
  transfers between devices with their start and end apart: 2 -> 9, of which waited for: 0 -> 6; matrix products, arithmetic and copies ran while one was open for 0% -> 0% of each run, Pallas kernels for 13% -> 9%
where the time goes in v1:
time: 80 us; the launch traced here: 79.6 us
  Pallas kernels  48.5 us (61%)
  starting transfers between devices  14 us (18%)
  waiting for transfers between devices  8.51 us (11%)
  local copies, waits for them, and re-layouts  7.86 us (10%)
    pallas_call x4, Pallas kernels, call(): pl.pallas_call(kernel, out_shape=outs, in_specs=in_spaces or whole(len(op...  48.5 us
    ppermute x7, waiting for transfers between devices, others(): lax.ppermute(values, axis, [(i, i ^ k) for i in range(size)])  8.25 us
    ppermute x7, starting transfers between devices, others(): lax.ppermute(values, axis, [(i, i ^ k) for i in range(size)])  7.91 us
    unnamed x20, local copies, waits for them, and re-layouts  7.86 us
    ppermute x1, starting transfers between devices, body(): lax.ppermute(rim, axes, [((i + 1) % ring, i) for i in range(ring)])  6.05 us
  transfers between devices with their start and end apart: 9, of which 6 were waited for; matrix products, arithmetic and copies ran while one was open for 0% of the time, Pallas kernels for 9%

profile of v1, /device:TPU:0, one launch (start us, length us, event | category | flops | bytes accessed | tf_op | source)
XLA Modules:
  0.0 79.6 jit_solution(11994412998403762061)
XLA Ops:
  0.7 1.0 %copy-done = f32[1,4,256,128]{3,2,1,0:T(8,128)S(1)} copy-done((f32[1,4,256,128]{3,2,1,0:T(8,128)S(1)}, f32[1,4,256,128]{3,2,1,0:T(8,128)}, u32[]{:S(2)}) %copy-start) | copy-done | bytes 524312
  1.7 0.9 %copy-done.1 = f32[1,2,256,128]{3,2,1,0:T(8,128)S(1)} copy-done((f32[1,2,256,128]{3,2,1,0:T(8,128)S(1)}, f32[1,2,256,128]{3,2,1,0:T(8,128)}, u32[]{:S(2)}) %copy-start.1) | copy-done | bytes 262168
  2.6 0.9 %copy-done.2 = f32[1,256,128]{2,1,0:T(8,128)S(1)} copy-done((f32[1,256,128]{2,1,0:T(8,128)S(1)}, f32[1,256,128]{2,1,0:T(8,128)}, u32[]{:S(2)}) %copy-start.2) | copy-done | bytes 131096
  3.5 0.9 %copy-done.3 = f32[1,256,128]{2,1,0:T(8,128)S(1)} copy-done((f32[1,256,128]{2,1,0:T(8,128)S(1)}, f32[1,256,128]{2,1,0:T(8,128)}, u32[]{:S(2)}) %copy-start.3) | copy-done | bytes 131096
  4.5 0.7 copy-done.4
  5.2 0.7 copy-done.5
  5.9 0.7 copy-done.6
  6.6 0.7 copy-done.7
  7.2 0.7 copy-done.8
  7.9 0.7 copy-done.9
  8.5 4.0 %shard_map.169 = (f32[8,32,128]{2,1,0:T(8,128)S(1)}, f32[4,256,128]{2,1,0:T(8,128)S(1)}, f32[4,256,128]{2,1,0:T(8,128)S(1)}, bf16[256,400]{1,0:T(8,128)(2,1)S(1)...) custom-call(f32[1,256,128]{2,1,0:T(8,128)S(1)} %copy-done.2, ...), custom_call_target="tpu_custom_call" | custom-call | tf_op jit(solution)/shard_map/pallas_call | solution.py:761
  12.5 6.1 %collective-permute-start.1 = (f32[8,32,128]{2,1,0:T(8,128)S(1)}, f32[8,32,128]{2,1,0:T(8,128)S(1)}, u32[]{:S(2)}, u32[]{:S(2)}) collective-permute-start(f32[8,32,128]{2,1,0:T(8,128)S(1)} %get-tuple-element.47.own), channel_id=1, source_target_pairs={{1,0},{2,1},{3,2},{4,3},{5,4},{6,5},{7,6},{0,7},{9,8},{10,9},{11,1... | collective-permute-start | bytes 393224 | tf_op jit(solution)/shard_map/ppermute | solution.py:821
  18.6 7.4 %shard_map.170 = (f32[4,256,128]{2,1,0:T(8,128)S(1)}, bf16[8,256,512]{2,1,0:T(8,128)(2,1)S(1)}, bf16[8,256,512]{2,1,0:T(8,128)(2,1)S(1)}, bf16[8,256,512]{2,1,0:...) custom-call(f32[4,256,128]{2,1,0:T(8,128)S(1)} %get-tuple-element.39.state, ...), custom_call_target="tpu_custom_call" | custom-call | flops 10000000000 | bytes 10000000 | tf_op jit(solution)/shard_map/pallas_call | solution.py:761
  26.2 36.5 %shard_map.171 = (f32[1,256,128]{2,1,0:T(8,128)}, f32[1,2,256,128]{3,2,1,0:T(8,128)}, f32[1,256,128]{2,1,0:T(8,128)}, f32[32,128]{1,0:T(8,128)S(1)}) custom-call(f32[4,256,128]{2,1,0:T(8,128)S(1)} %get-tuple-element.39.state, f32[4,256,128]{2,1,0:T(8,128)S(1)} %get-tuple-element.40.cot, f32[4,256,128]{2,1,0:T(8,128)S(1)} %get-tuple-element.46.middle, ...), custom_call_target="tpu_custom_call" | custom-call | flops 40000000000 | bytes 20000000 | tf_op jit(solution)/shard_map/pallas_call | solution.py:761
  63.1 1.1 %collective-permute-start.3 = (f32[32,128]{1,0:T(8,128)S(1)}, f32[32,128]{1,0:T(8,128)S(1)}, u32[]{:S(2)}, u32[]{:S(2)}) collective-permute-start(f32[32,128]{1,0:T(8,128)S(1)} %get-tuple-element.62), channel_id=1, source_target_pairs={{0,16},{8,24},{16,0},{24,8},{1,17},{9,25},{17,1},{25,9},{2,18},{10... | collective-permute-start | bytes 49160 | tf_op jit(solution)/shard_map/ppermute | solution.py:773
  64.6 1.4 %collective-permute-done.4 = f32[32,128]{1,0:T(8,128)S(1)} collective-permute-done((f32[32,128]{1,0:T(8,128)S(1)}, f32[32,128]{1,0:T(8,128)S(1)}, u32[]{:S(2)}, u32[]{:S(2)}) %collective-permute-start.4) | collective-permute-done | bytes 16416 | tf_op jit(solution)/shard_map/ppermute | solution.py:773
  66.0 0.9 %collective-permute-done.3 = f32[32,128]{1,0:T(8,128)S(1)} collective-permute-done((f32[32,128]{1,0:T(8,128)S(1)}, f32[32,128]{1,0:T(8,128)S(1)}, u32[]{:S(2)}, u32[]{:S(2)}) %collective-permute-start.3) | collective-permute-done | bytes 16416 | tf_op jit(solution)/shard_map/ppermute | solution.py:773
  66.9 3.6 %collective-permute-start.7 = (f32[32,128]{1,0:T(8,128)S(1)}, f32[32,128]{1,0:T(8,128)S(1)}, u32[]{:S(2)}, u32[]{:S(2)}) collective-permute-start(f32[32,128]{1,0:T(8,128)S(1)} %add_add_fusion.1), channel_id=1, source_target_pairs={{0,3},{1,2},{2,1},{3,0},{4,7},{5,6},{6,5},{7,4},{8,11},{9,10},{10,... | collective-permute-start | bytes 49160 | tf_op jit(solution)/shard_map/ppermute | solution.py:773
  70.4 0.9 %collective-permute-start.5 = (f32[32,128]{1,0:T(8,128)S(1)}, f32[32,128]{1,0:T(8,128)S(1)}, u32[]{:S(2)}, u32[]{:S(2)}) collective-permute-start(f32[32,128]{1,0:T(8,128)S(1)} %add_add_fusion.1), channel_id=1, source_target_pairs={{0,1},{1,0},{2,3},{3,2},{4,5},{5,4},{6,7},{7,6},{8,9},{9,8},{10,11... | collective-permute-start | bytes 49160 | tf_op jit(solution)/shard_map/ppermute | solution.py:773
  71.3 1.1 %collective-permute-done.7 = f32[32,128]{1,0:T(8,128)S(1)} collective-permute-done((f32[32,128]{1,0:T(8,128)S(1)}, f32[32,128]{1,0:T(8,128)S(1)}, u32[]{:S(2)}, u32[]{:S(2)}) %collective-permute-start.7) | collective-permute-done | bytes 16416 | tf_op jit(solution)/shard_map/ppermute | solution.py:773
  72.5 2.6 %collective-permute-done.6 = f32[32,128]{1,0:T(8,128)S(1)} collective-permute-done((f32[32,128]{1,0:T(8,128)S(1)}, f32[32,128]{1,0:T(8,128)S(1)}, u32[]{:S(2)}, u32[]{:S(2)}) %collective-permute-start.6) | collective-permute-done | bytes 16416 | tf_op jit(solution)/shard_map/ppermute | solution.py:773
  75.1 1.6 %collective-permute-start.8 = (f32[32,128]{1,0:T(8,128)S(1)}, f32[32,128]{1,0:T(8,128)S(1)}, u32[]{:S(2)}, u32[]{:S(2)}) collective-permute-start(f32[32,128]{1,0:T(8,128)S(1)} %add_add_fusion.one), channel_id=1, source_target_pairs={{0,4},{4,0},{1,5},{5,1},{2,6},{6,2},{3,7},{7,3},{8,12},{12,8},{9,1... | collective-permute-start | bytes 49160 | tf_op jit(solution)/shard_map/ppermute | solution.py:773
  76.7 2.2 %collective-permute-done.8.other = f32[32,128]{1,0:T(8,128)S(1)} collective-permute-done((f32[32,128]{1,0:T(8,128)S(1)}, f32[32,128]{1,0:T(8,128)S(1)}, u32[]{:S(2)}, u32[]{:S(2)}) %collective-permute-start.8) | collective-permute-done | bytes 16416 | tf_op jit(solution)/shard_map/ppermute | solution.py:773
  78.9 0.7 shard_map.172
  (20 shorter events, 1.1 us)
Async XLA Ops:
  0.6 1.0 %copy-start = (f32[1,4,256,128]{3,2,1,0:T(8,128)S(1)}, f32[1,4,256,128]{3,2,1,0:T(8,128)}, u32[]{:S(2)}) copy-start(f32[1,4,256,128]{3,2,1,0:T(8,128)} %cot.1) | copy-start | bytes 1572868
  1.7 0.9 %copy-start.1 = (f32[1,2,256,128]{3,2,1,0:T(8,128)S(1)}, f32[1,2,256,128]{3,2,1,0:T(8,128)}, u32[]{:S(2)}) copy-start(f32[1,2,256,128]{3,2,1,0:T(8,128)} %mom.1) | copy-start | bytes 786436
  2.6 0.9 %copy-start.2 = (f32[1,256,128]{2,1,0:T(8,128)S(1)}, f32[1,256,128]{2,1,0:T(8,128)}, u32[]{:S(2)}) copy-start(f32[1,256,128]{2,1,0:T(8,128)} %den.1) | copy-start | bytes 393220
  3.5 0.9 %copy-start.3 = (f32[1,256,128]{2,1,0:T(8,128)S(1)}, f32[1,256,128]{2,1,0:T(8,128)}, u32[]{:S(2)}) copy-start(f32[1,256,128]{2,1,0:T(8,128)} %tra.1) | copy-start | bytes 393220
  4.4 0.7 copy-start.4
  5.2 0.7 copy-start.5
  5.9 0.7 copy-start.6
  6.6 0.7 copy-start.7
  7.2 0.7 copy-start.8
  7.9 0.7 copy-start.9
  12.5 13.4 %collective-permute-start.1 = (f32[8,32,128]{2,1,0:T(8,128)S(1)}, f32[8,32,128]{2,1,0:T(8,128)S(1)}, u32[]{:S(2)}, u32[]{:S(2)}) collective-permute-start(f32[8,32,128]{2,1,0:T(8,128)S(1)} %get-tuple-element.47.own), channel_id=1, source_target_pairs={{1,0},{2,1},{3,2},{4,3},{5,4},{6,5},{7,6},{0,7},{9,8},{10,9},{11,1... | collective-permute-start | bytes 393224 | tf_op jit(solution)/shard_map/ppermute | solution.py:821
  18.6 7.7 %collective-permute-start = (f32[8,32,128]{2,1,0:T(8,128)S(1)}, f32[8,32,128]{2,1,0:T(8,128)S(1)}, u32[]{:S(2)}, u32[]{:S(2)}) collective-permute-start(f32[8,32,128]{2,1,0:T(8,128)S(1)} %get-tuple-element.47.own), channel_id=1, source_target_pairs={{0,1},{1,2},{2,3},{3,4},{4,5},{5,6},{6,7},{7,0},{8,9},{9,10},{10,1... | collective-permute-start | bytes 393224 | tf_op jit(solution)/shard_map/ppermute | solution.py:820
  62.7 3.3 %collective-permute-start.4 = (f32[32,128]{1,0:T(8,128)S(1)}, f32[32,128]{1,0:T(8,128)S(1)}, u32[]{:S(2)}, u32[]{:S(2)}) collective-permute-start(f32[32,128]{1,0:T(8,128)S(1)} %get-tuple-element.62), channel_id=1, source_target_pairs={{0,24},{8,16},{16,8},{24,0},{1,25},{9,17},{17,9},{25,1},{2,26},{10... | collective-permute-start | bytes 49160 | tf_op jit(solution)/shard_map/ppermute | solution.py:773
  63.1 3.7 %collective-permute-start.3 = (f32[32,128]{1,0:T(8,128)S(1)}, f32[32,128]{1,0:T(8,128)S(1)}, u32[]{:S(2)}, u32[]{:S(2)}) collective-permute-start(f32[32,128]{1,0:T(8,128)S(1)} %get-tuple-element.62), channel_id=1, source_target_pairs={{0,16},{8,24},{16,0},{24,8},{1,17},{9,25},{17,1},{25,9},{2,18},{10... | collective-permute-start | bytes 49160 | tf_op jit(solution)/shard_map/ppermute | solution.py:773
  64.2 2.6 %collective-permute-start.2 = (f32[32,128]{1,0:T(8,128)S(1)}, f32[32,128]{1,0:T(8,128)S(1)}, u32[]{:S(2)}, u32[]{:S(2)}) collective-permute-start(f32[32,128]{1,0:T(8,128)S(1)} %get-tuple-element.62), channel_id=1, source_target_pairs={{0,8},{8,0},{16,24},{24,16},{1,9},{9,1},{17,25},{25,17},{2,10},{10... | collective-permute-start | bytes 49160 | tf_op jit(solution)/shard_map/ppermute | solution.py:773
  66.9 5.6 %collective-permute-start.7 = (f32[32,128]{1,0:T(8,128)S(1)}, f32[32,128]{1,0:T(8,128)S(1)}, u32[]{:S(2)}, u32[]{:S(2)}) collective-permute-start(f32[32,128]{1,0:T(8,128)S(1)} %add_add_fusion.1), channel_id=1, source_target_pairs={{0,3},{1,2},{2,1},{3,0},{4,7},{5,6},{6,5},{7,4},{8,11},{9,10},{10,... | collective-permute-start | bytes 49160 | tf_op jit(solution)/shard_map/ppermute | solution.py:773
  70.4 4.6 %collective-permute-start.6 = (f32[32,128]{1,0:T(8,128)S(1)}, f32[32,128]{1,0:T(8,128)S(1)}, u32[]{:S(2)}, u32[]{:S(2)}) collective-permute-start(f32[32,128]{1,0:T(8,128)S(1)} %add_add_fusion.1), channel_id=1, source_target_pairs={{0,2},{1,3},{2,0},{3,1},{4,6},{5,7},{6,4},{7,5},{8,10},{9,11},{10,... | collective-permute-start | bytes 49160 | tf_op jit(solution)/shard_map/ppermute | solution.py:773
  70.4 4.6 %collective-permute-start.5 = (f32[32,128]{1,0:T(8,128)S(1)}, f32[32,128]{1,0:T(8,128)S(1)}, u32[]{:S(2)}, u32[]{:S(2)}) collective-permute-start(f32[32,128]{1,0:T(8,128)S(1)} %add_add_fusion.1), channel_id=1, source_target_pairs={{0,1},{1,0},{2,3},{3,2},{4,5},{5,4},{6,7},{7,6},{8,9},{9,8},{10,11... | collective-permute-start | bytes 49160 | tf_op jit(solution)/shard_map/ppermute | solution.py:773
  75.1 3.8 %collective-permute-start.8 = (f32[32,128]{1,0:T(8,128)S(1)}, f32[32,128]{1,0:T(8,128)S(1)}, u32[]{:S(2)}, u32[]{:S(2)}) collective-permute-start(f32[32,128]{1,0:T(8,128)S(1)} %add_add_fusion.one), channel_id=1, source_target_pairs={{0,4},{4,0},{1,5},{5,1},{2,6},{6,2},{3,7},{7,3},{8,12},{12,8},{9,1... | collective-permute-start | bytes 49160 | tf_op jit(solution)/shard_map/ppermute | solution.py:773

commit v2 on v1

--- a/solution.py
+++ b/solution.py
@@ -14,7 +14,8 @@
 FACES = 8
 SEG = 16
 RIM = 4
-PAIR = 4
+PAIR = 8
+RIM_PAIR = 4
 ONES = 16
 VMEM_BYTES = 32 * 2**20
 
@@ -221,14 +222,14 @@
     if first_bias_ref is None:
         h1 = jnp.tanh(dot(first_ref[...], stack(stacked(first) + [jnp.ones((ONES, width), BF16)])))
     else:
-        h1 = jnp.tanh(dot(first_ref[...], stack(stacked(first))) + first_bias_ref[...])
+        h1 = jnp.tanh(dot(first_ref[...], stack(stacked(first))) + first_bias_ref[:, :width])
     h1_parts = split3(h1)
     block = 2 * hid
     parts = []
     for at in range(0, FACES * hid, block):
         high, middle, low = (p[at : at + block] for p in h1_parts)
         both = dot(mid_ref[...], stack([high, middle, low, high]))
-        parts.append(jnp.tanh(both[:block] + both[block:] + mid_bias_ref[...]))
+        parts.append(jnp.tanh(both[:block] + both[block:] + mid_bias_ref[:, :width]))
     h2 = stack(parts)
     h2_parts = split3(h2)
     rows = 8 * FACES
@@ -236,7 +237,7 @@
     b = dot(out_ref[: 2 * rows, :], h2_parts[1])
     c = dot(out_ref[:rows, :], h2_parts[2])
     gates = jnp.tanh(
-        ((a[2 * rows :] + b[rows:] + c) + (a[rows : 2 * rows] + b[:rows])) + a[:rows] + out_bias_ref[...]
+        ((a[2 * rows :] + b[rows:] + c) + (a[rows : 2 * rows] + b[:rows])) + a[:rows] + out_bias_ref[:, :width]
     )
     return h1, h1_parts[:2], h2, h2_parts[:2], gates
 
@@ -264,17 +265,19 @@
     acc_in, acc_mid, acc_out, acc_out_bias = acc
     width = d3_full.shape[1]
     ones = jnp.ones((ONES, width), BF16)
-    nothing = jnp.zeros((ONES, width), BF16)
-    acc_in[...] += dot_nt(
-        side([stack([first[0], ones]), stack([first[0], ones]), stack([first[1], nothing])]),
-        side([d1[0], d1[1], d1[0]]),
-    )
+    rows = first[0].shape[0]
+    high = dot_nt(stack([first[0], ones, first[1]]), d1[0])
+    low = dot_nt(stack([first[0], ones]), d1[1])
+    acc_in[...] += high[: rows + ONES] + low
+    acc_in[:rows, :] += high[rows + ONES :]
     lefts, rights = [], []
     for at in range(0, FACES * hid, hid):
         lefts.append(stack([h1[0][at : at + hid], h1[1][at : at + hid], ones]))
         rights.append(stack([d2[0][at : at + hid], d2[1][at : at + hid]]))
     acc_mid[...] += dot_nt(side(lefts), side(rights))
-    acc_out[...] += dot_nt(side([d3[0], d3[0], d3[1]]), side([h2[0], h2[1], h2[0]]))
+    rows = d3[0].shape[0]
+    high = dot_nt(stack([d3[0], d3[1]]), h2[0])
+    acc_out[...] += high[:rows] + high[rows:] + dot_nt(d3[0], h2[1])
     acc_out_bias[...] += d3_full
 
 
@@ -544,7 +547,7 @@
     segs = ny // SEG
     rim_rows = nx // segs
     rim_groups = rim_rows // FACES
-    rim_half = rim_groups // PAIR
+    rim_half = rim_groups // RIM_PAIR
 
     for acc in (acc_x, acc_y, acc_mid, acc_out, acc_out_bias):
         acc[...] = jnp.zeros(acc.shape, F32)
@@ -580,12 +583,12 @@
                 ])
                 for c in range(4)
             ]
-            for k in range(PAIR)
+            for k in range(RIM_PAIR)
         ]
         tiles = [side([one[c] for one in sets]) for c in range(4)]
         fluxes = x_forward(tiles, x_weights, hid)[3]
         for c in range(4):
-            for k in range(PAIR):
+            for k in range(RIM_PAIR):
                 rim_flux[c, row_block(step + k * rim_half + 1), :] = fluxes[c][:, k * ny : (k + 1) * ny]
         return 0
 
@@ -598,13 +601,13 @@
             rim_middle[c, rows, :] = update_cells(rim_state[c, rows, :], both)
 
     refs = ((first_y, first_bias, mid, mid_bias, out, out_bias), out_back, mid_back, first_y_back)
-    spot_wide = lane_index(PAIR * ny) & (SEG - 1)
+    spot_wide = lane_index(RIM_PAIR * ny) & (SEG - 1)
     rim_faces = (spot_wide == RIM - 2) | (spot_wide == RIM - 1) | (spot_wide == 3 * RIM)
 
     def rim_back(step, _):
         cells = [[[] for _ in range(4)] for _ in range(4)]
         cots = [[[] for _ in range(4)] for _ in range(2)]
-        for k in range(PAIR):
+        for k in range(RIM_PAIR):
             rows = row_block(step + k * rim_half)
             for c in range(4):
                 value = rim_middle[c, rows, :]
@@ -616,7 +619,7 @@
         cells = [y_order([side(one) for one in row]) for row in cells]
         cots = [y_order([side(one) for one in row]) for row in cots]
         parts, _ = y_step(cells, cots, rim_faces, refs, hid)
-        for k in range(PAIR):
+        for k in range(RIM_PAIR):
             own_parts = [[one[:, k * ny : (k + 1) * ny] for one in row] for row in parts]
             gathered = y_order(y_gather(own_parts, ny))
             for c in range(4):
@@ -812,7 +815,7 @@
             shape((128, 2 * wide), BF16),
             shape((256, 2 * wide), BF16),
         ],
-        operands,
+        [pltpu.with_memory_space_constraint(one, pltpu.HBM) for one in operands],
         in_spaces=whole(10, pltpu.HBM),
         scratch=[pltpu.VMEM(one.shape, F32) for one in operands[4:]] + [pltpu.SemaphoreType.DMA((10,))],
     )

time: 80 us -> 62.9 us (0.79)
  Pallas kernels: 48.5 us -> 39.5 us
  local copies, waits for them, and re-layouts: 7.86 us -> 0 us
    pallas_call x4, Pallas kernels: 48.5 us -> 39.5 us  [call(): pl.pallas_call(kernel, out_shape=outs, in_specs=in_spaces or whole(len(op...]
    unnamed x20 -> x0, local copies, waits for them, and re-layouts: 7.86 us -> none
    ppermute x1, waiting for transfers between devices: 0.26 us -> 2.19 us  [body(): lax.ppermute(rim, axes, [(i, (i + 1) % ring) for i in range(ring)])]
    ppermute x7, waiting for transfers between devices: 8.25 us -> 6.33 us  [others(): lax.ppermute(values, axis, [(i, i ^ k) for i in range(size)])]
where the time goes in v2:
time: 62.9 us; the launch traced here: 62.7 us
  Pallas kernels  39.5 us (63%)
  starting transfers between devices  14 us (22%)
  waiting for transfers between devices  8.52 us (14%)
  between operations  0.69 us (1%)
    pallas_call x4, Pallas kernels, call(): pl.pallas_call(kernel, out_shape=outs, in_specs=in_spaces or whole(len(op...  39.5 us
    ppermute x7, starting transfers between devices, others(): lax.ppermute(values, axis, [(i, i ^ k) for i in range(size)])  7.9 us
    ppermute x7, waiting for transfers between devices, others(): lax.ppermute(values, axis, [(i, i ^ k) for i in range(size)])  6.33 us
    ppermute x1, starting transfers between devices, body(): lax.ppermute(rim, axes, [((i + 1) % ring, i) for i in range(ring)])  6.06 us
    ppermute x1, waiting for transfers between devices, body(): lax.ppermute(rim, axes, [(i, (i + 1) % ring) for i in range(ring)])  2.19 us
  transfers between devices with their start and end apart: 9, of which 6 were waited for; matrix products, arithmetic and copies ran while one was open for 0% of the time, Pallas kernels for 9%

profile of v2, /device:TPU:0, one launch (start us, length us, event | category | flops | bytes accessed | tf_op | source)
XLA Modules:
  0.0 62.7 jit_solution(14929932111615233138)
XLA Ops:
  0.6 4.3 %shard_map.169 = (f32[8,32,128]{2,1,0:T(8,128)S(1)}, f32[4,256,128]{2,1,0:T(8,128)S(1)}, f32[4,256,128]{2,1,0:T(8,128)S(1)}, bf16[256,400]{1,0:T(8,128)(2,1)S(1)...) custom-call(f32[1,256,128]{2,1,0:T(8,128)} %den.1, ...), custom_call_target="tpu_custom_call" | custom-call | tf_op jit(solution)/shard_map/pallas_call | solution.py:764
  4.9 6.1 %collective-permute-start.1 = (f32[8,32,128]{2,1,0:T(8,128)S(1)}, f32[8,32,128]{2,1,0:T(8,128)S(1)}, u32[]{:S(2)}, u32[]{:S(2)}) collective-permute-start(f32[8,32,128]{2,1,0:T(8,128)S(1)} %get-tuple-element.47.own), channel_id=1, source_target_pairs={{1,0},{2,1},{3,2},{4,3},{5,4},{6,5},{7,6},{0,7},{9,8},{10,9},{11,1... | collective-permute-start | bytes 393224 | tf_op jit(solution)/shard_map/ppermute | solution.py:824
  11.0 0.0 collective-permute-start
  11.0 5.5 %shard_map.170 = (f32[4,256,128]{2,1,0:T(8,128)S(1)}, bf16[4,256,1024]{2,1,0:T(8,128)(2,1)S(1)}, bf16[4,256,1024]{2,1,0:T(8,128)(2,1)S(1)}, bf16[4,256,1024]{2,1...) custom-call(f32[4,256,128]{2,1,0:T(8,128)S(1)} %get-tuple-element.39.state, ...), custom_call_target="tpu_custom_call" | custom-call | flops 10000000000 | bytes 10000000 | tf_op jit(solution)/shard_map/pallas_call | solution.py:764
  16.5 0.0 collective-permute-done.1.from_right
  16.5 2.2 %collective-permute-done.from_left = f32[8,32,128]{2,1,0:T(8,128)S(1)} collective-permute-done((f32[8,32,128]{2,1,0:T(8,128)S(1)}, f32[8,32,128]{2,1,0:T(8,128)S(1)}, u32[]{:S(2)}, u32[]{:S(2)}) %collective-permute-start) | collective-permute-done | bytes 131104 | tf_op jit(solution)/shard_map/ppermute | solution.py:823
  18.7 29.1 %shard_map.171 = (f32[1,256,128]{2,1,0:T(8,128)}, f32[1,2,256,128]{3,2,1,0:T(8,128)}, f32[1,256,128]{2,1,0:T(8,128)}, f32[32,128]{1,0:T(8,128)S(1)}) custom-call(f32[4,256,128]{2,1,0:T(8,128)S(1)} %get-tuple-element.39.state, f32[4,256,128]{2,1,0:T(8,128)S(1)} %get-tuple-element.40.cot, f32[4,256,128]{2,1,0:T(8,128)S(1)} %get-tuple-element.46.middle, ...), custom_call_target="tpu_custom_call" | custom-call | flops 40000000000 | bytes 20000000 | tf_op jit(solution)/shard_map/pallas_call | solution.py:764
  47.8 0.0 collective-permute-start.4
  47.8 1.5 %collective-permute-start.3 = (f32[32,128]{1,0:T(8,128)S(1)}, f32[32,128]{1,0:T(8,128)S(1)}, u32[]{:S(2)}, u32[]{:S(2)}) collective-permute-start(f32[32,128]{1,0:T(8,128)S(1)} %get-tuple-element.62), channel_id=1, source_target_pairs={{0,16},{8,24},{16,0},{24,8},{1,17},{9,25},{17,1},{25,9},{2,18},{10... | collective-permute-start | bytes 49160 | tf_op jit(solution)/shard_map/ppermute | solution.py:776
  49.3 0.3 collective-permute-start.2
  49.6 1.4 %collective-permute-done.4 = f32[32,128]{1,0:T(8,128)S(1)} collective-permute-done((f32[32,128]{1,0:T(8,128)S(1)}, f32[32,128]{1,0:T(8,128)S(1)}, u32[]{:S(2)}, u32[]{:S(2)}) %collective-permute-start.4) | collective-permute-done | bytes 16416 | tf_op jit(solution)/shard_map/ppermute | solution.py:776
  51.1 0.5 collective-permute-done.3
  51.5 0.0 collective-permute-done.2
  51.5 2.0 %collective-permute-start.7 = (f32[32,128]{1,0:T(8,128)S(1)}, f32[32,128]{1,0:T(8,128)S(1)}, u32[]{:S(2)}, u32[]{:S(2)}) collective-permute-start(f32[32,128]{1,0:T(8,128)S(1)} %add_add_fusion.1), channel_id=1, source_target_pairs={{0,3},{1,2},{2,1},{3,0},{4,7},{5,6},{6,5},{7,4},{8,11},{9,10},{10,... | collective-permute-start | bytes 49160 | tf_op jit(solution)/shard_map/ppermute | solution.py:776
  53.5 0.0 collective-permute-start.6
  53.6 2.4 %collective-permute-start.5 = (f32[32,128]{1,0:T(8,128)S(1)}, f32[32,128]{1,0:T(8,128)S(1)}, u32[]{:S(2)}, u32[]{:S(2)}) collective-permute-start(f32[32,128]{1,0:T(8,128)S(1)} %add_add_fusion.1), channel_id=1, source_target_pairs={{0,1},{1,0},{2,3},{3,2},{4,5},{5,4},{6,7},{7,6},{8,9},{9,8},{10,11... | collective-permute-start | bytes 49160 | tf_op jit(solution)/shard_map/ppermute | solution.py:776
  56.0 1.3 %collective-permute-done.7 = f32[32,128]{1,0:T(8,128)S(1)} collective-permute-done((f32[32,128]{1,0:T(8,128)S(1)}, f32[32,128]{1,0:T(8,128)S(1)}, u32[]{:S(2)}, u32[]{:S(2)}) %collective-permute-start.7) | collective-permute-done | bytes 16416 | tf_op jit(solution)/shard_map/ppermute | solution.py:776
  57.2 0.9 %collective-permute-done.6 = f32[32,128]{1,0:T(8,128)S(1)} collective-permute-done((f32[32,128]{1,0:T(8,128)S(1)}, f32[32,128]{1,0:T(8,128)S(1)}, u32[]{:S(2)}, u32[]{:S(2)}) %collective-permute-start.6) | collective-permute-done | bytes 16416 | tf_op jit(solution)/shard_map/ppermute | solution.py:776
  58.2 0.0 collective-permute-done.5
  58.2 1.6 %collective-permute-start.8 = (f32[32,128]{1,0:T(8,128)S(1)}, f32[32,128]{1,0:T(8,128)S(1)}, u32[]{:S(2)}, u32[]{:S(2)}) collective-permute-start(f32[32,128]{1,0:T(8,128)S(1)} %add_add_fusion.one), channel_id=1, source_target_pairs={{0,4},{4,0},{1,5},{5,1},{2,6},{6,2},{3,7},{7,3},{8,12},{12,8},{9,1... | collective-permute-start | bytes 49160 | tf_op jit(solution)/shard_map/ppermute | solution.py:776
  59.8 2.2 %collective-permute-done.8.other = f32[32,128]{1,0:T(8,128)S(1)} collective-permute-done((f32[32,128]{1,0:T(8,128)S(1)}, f32[32,128]{1,0:T(8,128)S(1)}, u32[]{:S(2)}, u32[]{:S(2)}) %collective-permute-start.8) | collective-permute-done | bytes 16416 | tf_op jit(solution)/shard_map/ppermute | solution.py:776
  62.0 0.7 %shard_map.172 = (f32[16,32]{1,0:T(8,128)}, f32[1,32]{1,0:T(1,128)}, f32[32,32]{1,0:T(8,128)}, f32[1,32]{1,0:T(1,128)}, f32[8,32]{1,0:T(8,128)}, /*index=5*/f32[1,8]{1,0:T(1,128)}) custom-call(f32[32,128]{1,0:T(8,128)S(1)} %add_add_fusion.one, f32[32,128]{1,0:T(8,128)S(1)} %collective-permute-done.8.other), custom_call_target="tpu_custom_call" | custom-call | tf_op jit(solution)/shard_map/pallas_call | solution.py:764
  (2 shorter events, 0.0 us)
Async XLA Ops:
  4.9 11.5 %collective-permute-start.1 = (f32[8,32,128]{2,1,0:T(8,128)S(1)}, f32[8,32,128]{2,1,0:T(8,128)S(1)}, u32[]{:S(2)}, u32[]{:S(2)}) collective-permute-start(f32[8,32,128]{2,1,0:T(8,128)S(1)} %get-tuple-element.47.own), channel_id=1, source_target_pairs={{1,0},{2,1},{3,2},{4,3},{5,4},{6,5},{7,6},{0,7},{9,8},{10,9},{11,1... | collective-permute-start | bytes 393224 | tf_op jit(solution)/shard_map/ppermute | solution.py:824
  11.0 7.7 %collective-permute-start = (f32[8,32,128]{2,1,0:T(8,128)S(1)}, f32[8,32,128]{2,1,0:T(8,128)S(1)}, u32[]{:S(2)}, u32[]{:S(2)}) collective-permute-start(f32[8,32,128]{2,1,0:T(8,128)S(1)} %get-tuple-element.47.own), channel_id=1, source_target_pairs={{0,1},{1,2},{2,3},{3,4},{4,5},{5,6},{6,7},{7,0},{8,9},{9,10},{10,1... | collective-permute-start | bytes 393224 | tf_op jit(solution)/shard_map/ppermute | solution.py:823
  47.8 3.3 %collective-permute-start.4 = (f32[32,128]{1,0:T(8,128)S(1)}, f32[32,128]{1,0:T(8,128)S(1)}, u32[]{:S(2)}, u32[]{:S(2)}) collective-permute-start(f32[32,128]{1,0:T(8,128)S(1)} %get-tuple-element.62), channel_id=1, source_target_pairs={{0,24},{8,16},{16,8},{24,0},{1,25},{9,17},{17,9},{25,1},{2,26},{10... | collective-permute-start | bytes 49160 | tf_op jit(solution)/shard_map/ppermute | solution.py:776
  47.8 3.8 %collective-permute-start.3 = (f32[32,128]{1,0:T(8,128)S(1)}, f32[32,128]{1,0:T(8,128)S(1)}, u32[]{:S(2)}, u32[]{:S(2)}) collective-permute-start(f32[32,128]{1,0:T(8,128)S(1)} %get-tuple-element.62), channel_id=1, source_target_pairs={{0,16},{8,24},{16,0},{24,8},{1,17},{9,25},{17,1},{25,9},{2,18},{10... | collective-permute-start | bytes 49160 | tf_op jit(solution)/shard_map/ppermute | solution.py:776
  49.3 2.3 %collective-permute-start.2 = (f32[32,128]{1,0:T(8,128)S(1)}, f32[32,128]{1,0:T(8,128)S(1)}, u32[]{:S(2)}, u32[]{:S(2)}) collective-permute-start(f32[32,128]{1,0:T(8,128)S(1)} %get-tuple-element.62), channel_id=1, source_target_pairs={{0,8},{8,0},{16,24},{24,16},{1,9},{9,1},{17,25},{25,17},{2,10},{10... | collective-permute-start | bytes 49160 | tf_op jit(solution)/shard_map/ppermute | solution.py:776
  51.5 5.7 %collective-permute-start.7 = (f32[32,128]{1,0:T(8,128)S(1)}, f32[32,128]{1,0:T(8,128)S(1)}, u32[]{:S(2)}, u32[]{:S(2)}) collective-permute-start(f32[32,128]{1,0:T(8,128)S(1)} %add_add_fusion.1), channel_id=1, source_target_pairs={{0,3},{1,2},{2,1},{3,0},{4,7},{5,6},{6,5},{7,4},{8,11},{9,10},{10,... | collective-permute-start | bytes 49160 | tf_op jit(solution)/shard_map/ppermute | solution.py:776
  53.5 4.6 %collective-permute-start.6 = (f32[32,128]{1,0:T(8,128)S(1)}, f32[32,128]{1,0:T(8,128)S(1)}, u32[]{:S(2)}, u32[]{:S(2)}) collective-permute-start(f32[32,128]{1,0:T(8,128)S(1)} %add_add_fusion.1), channel_id=1, source_target_pairs={{0,2},{1,3},{2,0},{3,1},{4,6},{5,7},{6,4},{7,5},{8,10},{9,11},{10,... | collective-permute-start | bytes 49160 | tf_op jit(solution)/shard_map/ppermute | solution.py:776
  53.6 4.6 %collective-permute-start.5 = (f32[32,128]{1,0:T(8,128)S(1)}, f32[32,128]{1,0:T(8,128)S(1)}, u32[]{:S(2)}, u32[]{:S(2)}) collective-permute-start(f32[32,128]{1,0:T(8,128)S(1)} %add_add_fusion.1), channel_id=1, source_target_pairs={{0,1},{1,0},{2,3},{3,2},{4,5},{5,4},{6,7},{7,6},{8,9},{9,8},{10,11... | collective-permute-start | bytes 49160 | tf_op jit(solution)/shard_map/ppermute | solution.py:776
  58.2 3.8 %collective-permute-start.8 = (f32[32,128]{1,0:T(8,128)S(1)}, f32[32,128]{1,0:T(8,128)S(1)}, u32[]{:S(2)}, u32[]{:S(2)}) collective-permute-start(f32[32,128]{1,0:T(8,128)S(1)} %add_add_fusion.one), channel_id=1, source_target_pairs={{0,4},{4,0},{1,5},{5,1},{2,6},{6,2},{3,7},{7,3},{8,12},{12,8},{9,1... | collective-permute-start | bytes 49160 | tf_op jit(solution)/shard_map/ppermute | solution.py:776

commit v3 on v2

--- a/solution.py
+++ b/solution.py
@@ -56,6 +56,14 @@
     return lax.broadcasted_iota(jnp.int32, shape, 0), lax.broadcasted_iota(jnp.int32, shape, 1)
 
 
+def quot(values, n):
+    return values >> (n.bit_length() - 1) if n & (n - 1) == 0 else values // n
+
+
+def rest(values, n):
+    return values & (n - 1) if n & (n - 1) == 0 else values % n
+
+
 def pick(shape, test, dtype=BF16):
     r, c = rows_cols(shape)
     return jnp.where(test(r, c), 1.0, 0.0).astype(dtype)
@@ -100,13 +108,13 @@
             for lev in range(3)
         ]
         part = place(None, w, rights)
-        total = total + jnp.where((c & 15) - (r // hid) == s, stack([part] * FACES), 0.0)
+        total = total + jnp.where((c & 15) - (quot(r, hid)) == s, stack([part] * FACES), 0.0)
     levels = split3(b)
     at, _ = rows_cols((cols, hid))
     rows = jnp.zeros((cols, hid), F32)
     for lev in range(3):
         rows = jnp.where(at == 384 + lev, jnp.broadcast_to(levels[lev].astype(F32), (cols, hid)), rows)
-    bias = dot_nt(pick((wide, hid), lambda q, n: (q % hid) == n), rows.astype(BF16))
+    bias = dot_nt(pick((wide, hid), lambda q, n: (rest(q, hid)) == n), rows.astype(BF16))
     return (jnp.where(c < 384, total, 0.0) + bias).astype(BF16)
 
 
@@ -118,7 +126,7 @@
         pick((16, cols), lambda q, n: (level_of(n >> 7) == lev) & (q == ((n & 127) >> 3))) for lev in range(3)
     ]
     part = place(None, w, rights)
-    return jnp.where((c & 7) == (r // hid), stack([part] * FACES), 0.0).astype(BF16)
+    return jnp.where((c & 7) == (quot(r, hid)), stack([part] * FACES), 0.0).astype(BF16)
 
 
 def build_mid(w, hid):
@@ -131,8 +139,8 @@
             def inner(q, n):
                 at = jnp.full(n.shape, -1, jnp.int32)
                 for k, level in enumerate(levels):
-                    at = jnp.where(n // block == k, level, at)
-                return (at == lev) & ((n % hid) == q)
+                    at = jnp.where(quot(n, block) == k, level, at)
+                return (at == lev) & ((rest(n, hid)) == q)
 
             return inner
 
@@ -140,7 +148,7 @@
 
     upper = place(None, w, rights((0, 0, 0, 2)))
     lower = place(None, w, rights((1, 1, -1, -1)))
-    keep = ((r % block) // hid) == ((c % block) // hid)
+    keep = (quot(rest(r, block), hid)) == (quot(rest(c, block), hid))
     return jnp.where(keep, stack([upper, upper, lower, lower]), 0.0).astype(BF16)
 
 
@@ -150,20 +158,20 @@
     r, c = rows_cols(shape)
     eye = pick((hid, hid), lambda q, n: q == n)
     rights = [
-        pick((hid, 3 * block), lambda q, n: ((n // block == 1) == (lev == 1)) & ((n % hid) == q))
+        pick((hid, 3 * block), lambda q, n: ((quot(n, block) == 1) == (lev == 1)) & ((rest(n, hid)) == q))
         for lev in range(2)
     ]
     part = place(lambda v: dot_nt(eye, v), w[:2], rights)
-    return jnp.where((r // hid) == ((c % block) // hid), stack([part] * 2), 0.0).astype(BF16)
+    return jnp.where((quot(r, hid)) == (quot(rest(c, block), hid)), stack([part] * 2), 0.0).astype(BF16)
 
 
 def build_out(w, hid):
     wide = FACES * hid
     shape = (64, wide)
     r, c = rows_cols(shape)
-    right = pick((hid, wide), lambda q, n: (n % hid) == q)
+    right = pick((hid, wide), lambda q, n: (rest(n, hid)) == q)
     left = pick((64, 8), lambda q, n: (q >> 3) == n)
-    keep = (r & 7) == (c // hid)
+    keep = (r & 7) == (quot(c, hid))
     return stack([jnp.where(keep, dot(dot(left, v).astype(BF16), right), 0.0) for v in w]).astype(BF16)
 
 
@@ -176,20 +184,20 @@
     wide = FACES * hid
     shape = (wide, 192)
     r, c = rows_cols(shape)
-    left = pick((wide, hid), lambda q, n: (q % hid) == n)
+    left = pick((wide, hid), lambda q, n: (rest(q, hid)) == n)
 
     rights = [
         pick((8, 192), lambda q, n: (((n >> 6) == 1) == (lev == 1)) & (((n & 63) >> 3) == q)) for lev in range(2)
     ]
     part = place(lambda v: dot_nt(left, v), w[:2], rights)
-    return jnp.where((r // hid) == (c & 7), part, 0.0).astype(BF16)
+    return jnp.where((quot(r, hid)) == (c & 7), part, 0.0).astype(BF16)
 
 
 def build_first_x_back(w, hid):
     wide = FACES * hid
     shape = (128, 2 * wide)
     r, c = rows_cols(shape)
-    right = pick((hid, 2 * wide), lambda q, n: (n % hid) == q)
+    right = pick((hid, 2 * wide), lambda q, n: (rest(n, hid)) == q)
     total = jnp.zeros(shape, F32)
     for s in range(4):
         left = pick((128, 16), lambda q, n: n == 4 * s + ((q & 63) >> 4))
@@ -198,7 +206,7 @@
             return dot(dot_nt(left, values).astype(BF16), right)
 
         value = jnp.where(r < 64, one(w[0]), jnp.where(c < wide, one(w[1]), 0.0))
-        total = total + jnp.where((r & 15) - ((c % wide) // hid) == s, value, 0.0)
+        total = total + jnp.where((r & 15) - (quot(rest(c, wide), hid)) == s, value, 0.0)
     return total.astype(BF16)
 
 
@@ -206,14 +214,18 @@
     wide = FACES * hid
     shape = (256, 2 * wide)
     r, c = rows_cols(shape)
-    right = pick((hid, 2 * wide), lambda q, n: (n % hid) == q)
+    right = pick((hid, 2 * wide), lambda q, n: (rest(n, hid)) == q)
     left = pick((256, 16), lambda q, n: n == ((q & 127) >> 3))
 
     def one(values):
         return dot(dot_nt(left, values).astype(BF16), right)
 
     value = jnp.where(r < 128, one(w[0]), jnp.where(c < wide, one(w[1]), 0.0))
-    return jnp.where((r & 7) == ((c % wide) // hid), value, 0.0).astype(BF16)
+    return jnp.where((r & 7) == (quot(rest(c, wide), hid)), value, 0.0).astype(BF16)
+
+
+def spread(bias_ref, width):
+    return side([bias_ref[...]] * (width // bias_ref.shape[1]))
 
 
 def limiter_forward(first, weights, hid):
@@ -222,14 +234,14 @@
     if first_bias_ref is None:
         h1 = jnp.tanh(dot(first_ref[...], stack(stacked(first) + [jnp.ones((ONES, width), BF16)])))
     else:
-        h1 = jnp.tanh(dot(first_ref[...], stack(stacked(first))) + first_bias_ref[:, :width])
+        h1 = jnp.tanh(dot(first_ref[...], stack(stacked(first))) + spread(first_bias_ref, width))
     h1_parts = split3(h1)
     block = 2 * hid
     parts = []
     for at in range(0, FACES * hid, block):
         high, middle, low = (p[at : at + block] for p in h1_parts)
         both = dot(mid_ref[...], stack([high, middle, low, high]))
-        parts.append(jnp.tanh(both[:block] + both[block:] + mid_bias_ref[:, :width]))
+        parts.append(jnp.tanh(both[:block] + both[block:] + spread(mid_bias_ref, width)))
     h2 = stack(parts)
     h2_parts = split3(h2)
     rows = 8 * FACES
@@ -237,22 +249,33 @@
     b = dot(out_ref[: 2 * rows, :], h2_parts[1])
     c = dot(out_ref[:rows, :], h2_parts[2])
     gates = jnp.tanh(
-        ((a[2 * rows :] + b[rows:] + c) + (a[rows : 2 * rows] + b[:rows])) + a[:rows] + out_bias_ref[:, :width]
+        ((a[2 * rows :] + b[rows:] + c) + (a[rows : 2 * rows] + b[:rows])) + a[:rows] + spread(out_bias_ref, width)
     )
     return h1, h1_parts[:2], h2, h2_parts[:2], gates
 
 
-def limiter_backward(d3, h1, h2, out_back_ref, mid_back_ref, hid):
+def limiter_backward(d3, h1, h2, h1_pair, h2_pair, out_back_ref, mid_back_ref, acc, hid):
     d3_hi, d3_lo = split(d3)
-    d2 = dot(out_back_ref[...], stack([d3_hi, d3_hi, d3_lo])) * (1.0 - h2 * h2)
-    d2_hi, d2_lo = split(d2)
+    dh2 = dot(out_back_ref[...], stack([d3_hi, d3_hi, d3_lo]))
+    if acc is not None:
+        rows = d3.shape[0]
+        high = dot_nt(stack([d3_hi, d3_lo]), h2_pair[0])
+        acc[2][...] += high[:rows] + high[rows:] + dot_nt(d3_hi, h2_pair[1])
+        acc[3][...] += d3
+    d2_hi, d2_lo = split(dh2 * (1.0 - h2 * h2))
     block = 2 * hid
     parts = []
     for at in range(0, FACES * hid, block):
         hi, lo = d2_hi[at : at + block], d2_lo[at : at + block]
         parts.append(dot(mid_back_ref[...], stack([hi, hi, lo])))
-    d1 = stack(parts) * (1.0 - h1 * h1)
-    return (d3_hi, d3_lo), (d2_hi, d2_lo), split(d1)
+    if acc is not None:
+        ones = jnp.ones((ONES, d3.shape[1]), BF16)
+        lefts, rights = [], []
+        for at in range(0, FACES * hid, hid):
+            lefts.append(stack([h1_pair[0][at : at + hid], h1_pair[1][at : at + hid], ones]))
+            rights.append(stack([d2_hi[at : at + hid], d2_lo[at : at + hid]]))
+        acc[1][...] += dot_nt(side(lefts), side(rights))
+    return split(stack(parts) * (1.0 - h1 * h1))
 
 
 def first_backward(d1, back_ref):
@@ -261,24 +284,13 @@
     return both[:half] + both[half:]
 
 
-def add_weight_grads(first, h1, h2, d1, d2, d3, d3_full, acc, hid):
-    acc_in, acc_mid, acc_out, acc_out_bias = acc
-    width = d3_full.shape[1]
-    ones = jnp.ones((ONES, width), BF16)
+def add_first_grads(first, d1, acc_in):
+    ones = jnp.ones((ONES, d1[0].shape[1]), BF16)
     rows = first[0].shape[0]
     high = dot_nt(stack([first[0], ones, first[1]]), d1[0])
     low = dot_nt(stack([first[0], ones]), d1[1])
     acc_in[...] += high[: rows + ONES] + low
     acc_in[:rows, :] += high[rows + ONES :]
-    lefts, rights = [], []
-    for at in range(0, FACES * hid, hid):
-        lefts.append(stack([h1[0][at : at + hid], h1[1][at : at + hid], ones]))
-        rights.append(stack([d2[0][at : at + hid], d2[1][at : at + hid]]))
-    acc_mid[...] += dot_nt(side(lefts), side(rights))
-    rows = d3[0].shape[0]
-    high = dot_nt(stack([d3[0], d3[1]]), h2[0])
-    acc_out[...] += high[:rows] + high[rows:] + dot_nt(d3[0], h2[1])
-    acc_out_bias[...] += d3_full
 
 
 def edge_states(cells, gates):
@@ -387,9 +399,9 @@
     lanes = out_bias.shape[1]
     first_x[...] = build_first_x(wi, b_in[...], hid)
     first_y[...] = build_first_y(wi, hid)
-    first_bias[...] = spread_bias(b_in[...], FACES * hid, lanes, lambda q: q % hid)
+    first_bias[...] = spread_bias(b_in[...], FACES * hid, lanes, lambda q: rest(q, hid))
     mid[...] = build_mid(wm, hid)
-    mid_bias[...] = spread_bias(b_mid[...], 2 * hid, lanes, lambda q: q % hid)
+    mid_bias[...] = spread_bias(b_mid[...], 2 * hid, lanes, lambda q: rest(q, hid))
     out[...] = build_out(wo, hid)
     out_bias[...] = spread_bias(b_out[...], 64, lanes, lambda q: q >> 3)
     out_back[...] = build_out_back(wo, hid)
@@ -477,7 +489,7 @@
     return lax.broadcasted_iota(jnp.int32, (FACES, width), 1)
 
 
-def y_step(cells, cots, halo_mask, refs, hid):
+def y_step(cells, cots, halo_mask, refs, acc, hid):
     weights, out_back, mid_back, first_y_back = refs
     window = split3(stack([cells[s][c] for s in range(4) for c in range(4)]))
     h1, h1_pair, h2, h2_pair, gates = limiter_forward(window, weights, hid)
@@ -488,13 +500,14 @@
         d_left = [jnp.where(halo_mask, d, 0.0) for d in d_left]
         d_right = [jnp.where(halo_mask, d, 0.0) for d in d_right]
     d3_full, direct = edge_backward(cells, gates, d_left, d_right)
-    d3, d2, d1 = limiter_backward(d3_full, h1, h2, out_back, mid_back, hid)
+    d1 = limiter_backward(d3_full, h1, h2, h1_pair, h2_pair, out_back, mid_back, acc, hid)
     d_window = first_backward(d1, first_y_back)
-    parts = [
+    if acc is not None:
+        add_first_grads(window, d1, acc[0])
+    return [
         [d_window[FACES * (4 * s + c) : FACES * (4 * s + c + 1)] + direct[s][c] for c in range(4)]
         for s in range(4)
     ]
-    return parts, (window, h1_pair, h2_pair, d1, d2, d3, d3_full)
 
 
 def y_gather(parts, ny):
@@ -511,23 +524,25 @@
 def fold_first_x(acc, hid):
     shape = acc.shape
     r, c = rows_cols(shape)
-    fold = pick((shape[1], hid), lambda q, n: (q % hid) == n, F32)
-    total = jnp.zeros((24, hid), F32)
-    for s in range(4):
-        keep = ((r & 15) - (c // hid) == s) & (r < 64)
-        sel = lambda q, n: (n < 64) & (q == 4 * s + (n >> 4))
-        if s == 0:
-            keep = keep | (r >= 64)
-            sel = lambda q, n: ((n < 64) & (q == (n >> 4))) | ((n == 64) & (q == 16))
-        total = total + exact(pick((24, shape[0]), sel, F32), exact(jnp.where(keep, acc, 0.0), fold))
-    return total
+    fold = pick((shape[1], hid), lambda q, n: rest(n - q, hid) == 0, F32)
+    face = quot(c, hid)
+    parts = [
+        jnp.where((((r & 15) - face) == s) & (r < 64) | (r >= 64) & (s == 0), acc, 0.0)[: 80 if s == 0 else 64]
+        for s in range(4)
+    ]
+    folded = exact(stack(parts), fold)
+    def test(q, n):
+        at = jnp.where(n < 64, n, n - ONES)
+        return ((n < 64) | (n >= 64 + ONES)) & (q == (at >> 4)) | (n == 64) & (q == 16)
+
+    return exact(pick((24, folded.shape[0]), test, F32), folded)
 
 
 def fold_first_y(acc, hid):
     shape = acc.shape
     r, c = rows_cols(shape)
-    fold = pick((shape[1], hid), lambda q, n: (q % hid) == n, F32)
-    keep = ((r & 7) == (c // hid)) | (r >= 128)
+    fold = pick((shape[1], hid), lambda q, n: (rest(q, hid)) == n, F32)
+    keep = ((r & 7) == (quot(c, hid))) | (r >= 128)
     sel = lambda q, n: ((n < 128) & (q == (n >> 3))) | ((n == 128) & (q == 16))
     return exact(pick((24, shape[0]), sel, F32), exact(jnp.where(keep, acc, 0.0), fold))
 
@@ -618,7 +633,7 @@
                     cots[s][c].append(turn(value, -s, 1))
         cells = [y_order([side(one) for one in row]) for row in cells]
         cots = [y_order([side(one) for one in row]) for row in cots]
-        parts, _ = y_step(cells, cots, rim_faces, refs, hid)
+        parts = y_step(cells, cots, rim_faces, refs, None, hid)
         for k in range(RIM_PAIR):
             own_parts = [[one[:, k * ny : (k + 1) * ny] for one in row] for row in parts]
             gathered = y_order(y_gather(own_parts, ny))
@@ -654,10 +669,7 @@
                 cots[1][c].append(turn(low, -1, 1))
         cells = [y_order([side(one) for one in row]) for row in cells]
         cots = [y_order([side(one) for one in row]) for row in cots]
-        parts, (window, h1_pair, h2_pair, d1, d2, d3, d3_full) = y_step(cells, cots, None, refs, hid)
-        add_weight_grads(
-            window, h1_pair, h2_pair, d1, d2, d3, d3_full, (acc_y, acc_mid, acc_out, acc_out_bias), hid
-        )
+        parts = y_step(cells, cots, None, refs, (acc_y, acc_mid, acc_out, acc_out_bias), hid)
         for k in range(PAIR):
             group = step + k * half
             rows = row_block(group)
@@ -696,12 +708,11 @@
         d_flux = [courant * (turn(d, -2, 0)[:FACES] - turn(d, -1, 0)[:FACES]) for d in d_tiles]
         d_left, d_right = face_flux_backward(left, right, d_flux)
         d3_full, direct = edge_backward(cells, gates, d_left, d_right)
-        d3, d2, d1 = limiter_backward(d3_full, h1, h2, out_back, mid_back, hid)
+        d1 = limiter_backward(
+            d3_full, h1, h2, h1_pair, h2_pair, out_back, mid_back, (acc_x, acc_mid, acc_out, acc_out_bias), hid
+        )
         d_window = first_backward(d1, first_x_back)
-        add_weight_grads(
-            split(stack(tiles)), h1_pair, h2_pair, d1, d2, d3, d3_full,
-            (acc_x, acc_mid, acc_out, acc_out_bias), hid,
-        )
+        add_first_grads(split(stack(tiles)), d1, acc_x)
         later = []
         for c in range(4):
             total = d_window[2 * FACES * c : 2 * FACES * (c + 1)]
@@ -726,9 +737,9 @@
     grad_mid = both[:hid, :hid] + both[:hid, hid:] + both[hid : 2 * hid, :hid]
     grad_mid_bias = both[2 * hid :, :hid] + both[2 * hid :, hid:]
     r, c = rows_cols(acc_out.shape)
-    fold = pick((acc_out.shape[1], hid), lambda q, n: (q % hid) == n, F32)
+    fold = pick((acc_out.shape[1], hid), lambda q, n: (rest(q, hid)) == n, F32)
     rows = pick((8, 64), lambda q, n: (n >> 3) == q, F32)
-    grad_out = exact(rows, exact(jnp.where((r & 7) == (c // hid), acc_out[...], 0.0), fold))
+    grad_out = exact(rows, exact(jnp.where((r & 7) == (quot(c, hid)), acc_out[...], 0.0), fold))
     out_bias_rows = exact_nt(jnp.ones((8, acc_out_bias.shape[1]), F32), acc_out_bias[...])
     grad_out_bias = exact_nt(out_bias_rows, pick((hid, 64), lambda q, n: (n >> 3) == q, F32))
     r, c = rows_cols((8, hid))
@@ -737,23 +748,22 @@
         grad_first[16:24],
         jnp.where(r == 1, jnp.broadcast_to(grad_mid_bias[:1], (8, hid)), jnp.where(r == 2, grad_out_bias, 0.0)),
     )
-    width = g_weights.shape[1]
-    beside = stack([grad_first[:16], grad_out, biases])
-    g_weights[...] = exact(
-        exact_nt(eye, grad_mid), pick((hid, width), lambda q, n: n == q, F32)
-    ) + exact(beside, pick((hid, width), lambda q, n: n == q + hid, F32))
-
-
-def finish_kernel(one, other, g_w_in, g_b_in, g_w_mid, g_b_mid, g_w_out, g_b_out):
+    g_weights[...] = jnp.zeros(g_weights.shape, F32)
+    g_weights[:, :hid] = stack([exact_nt(eye, grad_mid), grad_first[:16], grad_out, biases])
+
+
+def finish_kernel(parts, g_w_in, g_b_in, g_w_mid, g_b_mid, g_w_out, g_b_out):
     hid = g_w_mid.shape[0]
-    total = one[...] + other[...]
-    g_w_mid[...] = total[:, :hid]
-    beside = total[:, hid : 2 * hid]
-    g_w_in[...] = beside[:16]
-    g_w_out[...] = beside[16:24]
-    g_b_in[...] = beside[24:25]
-    g_b_mid[...] = beside[25:26]
-    g_b_out[...] = beside[26:27, :8]
+    found = [parts[k] for k in range(parts.shape[0])]
+    while len(found) > 1:
+        found = [found[k] + found[k + 1] if k + 1 < len(found) else found[k] for k in range(0, len(found), 2)]
+    total = found[0][:, :hid]
+    g_w_mid[...] = total[:hid]
+    g_w_in[...] = total[hid : hid + 16]
+    g_w_out[...] = total[hid + 16 : hid + 24]
+    g_b_in[...] = total[hid + 24 : hid + 25]
+    g_b_mid[...] = total[hid + 25 : hid + 26]
+    g_b_out[...] = total[hid + 26 : hid + 27, :8]
 
 
 def whole(count, space=pltpu.VMEM):
@@ -805,11 +815,11 @@
             shape((4, nx, ny), F32),
             shape((wide, 6 * 64 + ONES), BF16),
             shape((wide, 6 * 128), BF16),
-            shape((wide, lanes), F32),
+            shape((wide, ny), F32),
             shape((4 * hid, 8 * hid), BF16),
-            shape((2 * hid, lanes), F32),
+            shape((2 * hid, ny), F32),
             shape((192, wide), BF16),
-            shape((64, lanes), F32),
+            shape((64, ny), F32),
             shape((wide, 192), BF16),
             shape((2 * hid, 6 * hid), BF16),
             shape((128, 2 * wide), BF16),
@@ -839,7 +849,7 @@
             shape(density.shape, F32),
             shape(momentum.shape, F32),
             shape(tracer.shape, F32),
-            shape((hid, 128), F32),
+            shape((2 * hid, 128), F32),
         ],
         [state, cots, middle, rim, from_left, from_right] + matrices + kept,
         scratch=[
@@ -858,9 +868,7 @@
         flops=4 * 10**10,
         moved=2 * 10**7,
     )
-    totals = tree_sum([g_weights] + others(g_weights, "traj", sizes["traj"]))
-    totals = tree_sum([totals] + others(totals, "ty", sizes["ty"]))
-    parts = [totals] + others(totals, "tx", sizes["tx"])
+    everyone = lax.all_gather(g_weights, ("traj", "tx", "ty"))
     g_w_in, g_b_in, g_w_mid, g_b_mid, g_w_out, g_b_out = call(
         finish_kernel,
         [
@@ -871,7 +879,7 @@
             shape(w_out.shape, F32),
             shape((1, b_out.shape[0]), F32),
         ],
-        [tree_sum(parts[: len(parts) // 2]), tree_sum(parts[len(parts) // 2 :])],
+        [everyone],
     )
     return (g_den, g_mom, g_tra, g_w_in.T, g_b_in[0], g_w_mid, g_b_mid[0], g_w_out, g_b_out[0])
 

time: 62.9 us -> 114 us (1.81)
  waiting for transfers between devices: 8.52 us -> 55.4 us
  between operations: 0.69 us -> 14.1 us
  starting transfers between devices: 14 us -> 6.1 us
  Pallas kernels: 39.5 us -> 36.7 us
  local copies, waits for them, and re-layouts: 0 us -> 1.22 us
    all_gather x0 -> x1, waiting for transfers between devices: none -> 53.1 us  [body(): everyone = lax.all_gather(g_weights, ('traj', 'tx', 'ty'))]
    ppermute x7 -> x0, starting transfers between devices: 7.9 us -> none  [others(): lax.ppermute(values, axis, [(i, i ^ k) for i in range(size)])]
    ppermute x7 -> x0, waiting for transfers between devices: 6.33 us -> none  [others(): lax.ppermute(values, axis, [(i, i ^ k) for i in range(size)])]
    pallas_call x4, Pallas kernels: 39.5 us -> 36.7 us  [call(): pl.pallas_call(kernel, out_shape=outs, in_specs=in_spaces or whole(len(op...]
    unnamed x0 -> x2, local copies, waits for them, and re-layouts: none -> 1.22 us
  transfers between devices with their start and end apart: 9 -> 3, of which waited for: 6 -> 2; matrix products, arithmetic and copies ran while one was open for 0% -> 0% of each run, Pallas kernels for 9% -> 5%
where the time goes in v3:
time: 114 us; the launch traced here: 113 us
  waiting for transfers between devices  55.4 us (49%)
  Pallas kernels  36.7 us (32%)
  between operations  14.1 us (12%)
  starting transfers between devices  6.1 us (5%)
  local copies, waits for them, and re-layouts  1.22 us (1%)
    all_gather x1, waiting for transfers between devices, body(): everyone = lax.all_gather(g_weights, ('traj', 'tx', 'ty'))  53.1 us
    pallas_call x4, Pallas kernels, call(): pl.pallas_call(kernel, out_shape=outs, in_specs=in_spaces or whole(len(op...  36.7 us
    ppermute x1, starting transfers between devices, body(): lax.ppermute(rim, axes, [((i + 1) % ring, i) for i in range(ring)])  6.06 us
  transfers between devices with their start and end apart: 3, of which 2 were waited for; matrix products, arithmetic and copies ran while one was open for 0% of the time, Pallas kernels for 5%

profile of v3, /device:TPU:0, one launch (start us, length us, event | category | flops | bytes accessed | tf_op | source)
XLA Modules:
  0.0 113.4 jit_solution(17923980355678396418)
XLA Ops:
  7.2 0.0 all-gather.3.cloned.1.call-start
  7.2 4.1 %shard_map.169 = (f32[8,32,128]{2,1,0:T(8,128)S(1)}, f32[4,256,128]{2,1,0:T(8,128)S(1)}, f32[4,256,128]{2,1,0:T(8,128)S(1)}, bf16[256,400]{1,0:T(8,128)(2,1)S(1)...) custom-call(f32[1,256,128]{2,1,0:T(8,128)} %den.1, ...), custom_call_target="tpu_custom_call" | custom-call | tf_op jit(solution)/shard_map/pallas_call | solution.py:774
  11.4 6.1 %collective-permute-start.1 = (f32[8,32,128]{2,1,0:T(8,128)S(1)}, f32[8,32,128]{2,1,0:T(8,128)S(1)}, u32[]{:S(2)}, u32[]{:S(2)}) collective-permute-start(f32[8,32,128]{2,1,0:T(8,128)S(1)} %get-tuple-element.47.own), channel_id=1, source_target_pairs={{1,0},{2,1},{3,2},{4,3},{5,4},{6,5},{7,6},{0,7},{9,8},{10,9},{11,1... | collective-permute-start | bytes 393224 | tf_op jit(solution)/shard_map/ppermute | solution.py:834
  17.4 0.0 collective-permute-start
  17.4 5.4 %shard_map.170 = (f32[4,256,128]{2,1,0:T(8,128)S(1)}, bf16[4,256,1024]{2,1,0:T(8,128)(2,1)S(1)}, bf16[4,256,1024]{2,1,0:T(8,128)(2,1)S(1)}, bf16[4,256,1024]{2,1...) custom-call(f32[4,256,128]{2,1,0:T(8,128)S(1)} %get-tuple-element.39.state, ...), custom_call_target="tpu_custom_call" | custom-call | flops 10000000000 | bytes 10000000 | tf_op jit(solution)/shard_map/pallas_call | solution.py:774
  22.8 0.0 collective-permute-done.1.from_right
  22.9 2.2 %collective-permute-done.from_left = f32[8,32,128]{2,1,0:T(8,128)S(1)} collective-permute-done((f32[8,32,128]{2,1,0:T(8,128)S(1)}, f32[8,32,128]{2,1,0:T(8,128)S(1)}, u32[]{:S(2)}, u32[]{:S(2)}) %collective-permute-start) | collective-permute-done | bytes 131104 | tf_op jit(solution)/shard_map/ppermute | solution.py:833
  25.1 26.5 %shard_map.171 = (f32[1,256,128]{2,1,0:T(8,128)}, f32[1,2,256,128]{3,2,1,0:T(8,128)}, f32[1,256,128]{2,1,0:T(8,128)}, f32[64,128]{1,0:T(8,128)}) custom-call(f32[4,256,128]{2,1,0:T(8,128)S(1)} %get-tuple-element.39.state, f32[4,256,128]{2,1,0:T(8,128)S(1)} %get-tuple-element.40.cot, f32[4,256,128]{2,1,0:T(8,128)S(1)} %get-tuple-element.46.middle, ...), custom_call_target="tpu_custom_call" | custom-call | flops 40000000000 | bytes 20000000 | tf_op jit(solution)/shard_map/pallas_call | solution.py:774
  51.6 0.0 all-gather.3.cloned.1.call-update
  51.6 53.1 %all-gather.3.cloned.1.call-done = f32[2048,128]{1,0:T(8,128)} async-done(((f32[64,128]{1,0:T(8,128)}), f32[2048,128]{1,0:T(8,128)}) %all-gather.3.cloned.1.call-update) | async-done | bytes 1048592 | tf_op jit(solution)/shard_map/all_gather | solution.py:871
  104.7 0.0 copy-start
  104.7 1.2 %copy-done = f32[2048,128]{1,0:T(8,128)S(1)} copy-done((f32[2048,128]{1,0:T(8,128)S(1)}, f32[2048,128]{1,0:T(8,128)}, u32[]{:S(2)}) %copy-start) | copy-done | bytes 1048600
  105.9 0.7 shard_map.172
Async XLA Ops:
  7.2 97.5 %all-gather.3.cloned.1.call-start = ((), (), s32[]{:S(2)}) async-start(), calls=%async_computation | async-start | bytes 1081344 | tf_op jit(solution)/shard_map/all_gather | solution.py:871
  11.4 11.5 %collective-permute-start.1 = (f32[8,32,128]{2,1,0:T(8,128)S(1)}, f32[8,32,128]{2,1,0:T(8,128)S(1)}, u32[]{:S(2)}, u32[]{:S(2)}) collective-permute-start(f32[8,32,128]{2,1,0:T(8,128)S(1)} %get-tuple-element.47.own), channel_id=1, source_target_pairs={{1,0},{2,1},{3,2},{4,3},{5,4},{6,5},{7,6},{0,7},{9,8},{10,9},{11,1... | collective-permute-start | bytes 393224 | tf_op jit(solution)/shard_map/ppermute | solution.py:834
  17.4 7.7 %collective-permute-start = (f32[8,32,128]{2,1,0:T(8,128)S(1)}, f32[8,32,128]{2,1,0:T(8,128)S(1)}, u32[]{:S(2)}, u32[]{:S(2)}) collective-permute-start(f32[8,32,128]{2,1,0:T(8,128)S(1)} %get-tuple-element.47.own), channel_id=1, source_target_pairs={{0,1},{1,2},{2,3},{3,4},{4,5},{5,6},{6,7},{7,0},{8,9},{9,10},{10,1... | collective-permute-start | bytes 393224 | tf_op jit(solution)/shard_map/ppermute | solution.py:833
  104.7 1.2 %copy-start = (f32[2048,128]{1,0:T(8,128)S(1)}, f32[2048,128]{1,0:T(8,128)}, u32[]{:S(2)}) copy-start(f32[2048,128]{1,0:T(8,128)} %all-gather.3.cloned.1.call-done) | copy-start | bytes 3145732
Sparse Core Ops, SparseCore 0:
  51.7 52.9 all-gather.2

commit v4 on v3

--- a/solution.py
+++ b/solution.py
@@ -77,15 +77,6 @@
     return jnp.concatenate(parts, 1)
 
 
-def place(left, levels, rights):
-    total = None
-    for values, right in zip(levels, rights):
-        values = values if left is None else left(values).astype(BF16)
-        part = dot(values, right)
-        total = part if total is None else total + part
-    return total
-
-
 STACKED = (0, 0, 0, 1, 1, 2)
 
 
@@ -97,131 +88,115 @@
     return jnp.where(block < 3, 0, jnp.where(block < 5, 1, 2))
 
 
-def build_first_x(w, b, hid):
-    wide, cols = FACES * hid, 6 * 64 + ONES
-    shape = (wide, cols)
-    r, c = rows_cols(shape)
-    total = jnp.zeros(shape, F32)
+def choose(values, levels):
+    parts = [part.astype(F32) for part in split3(values)]
+    total = jnp.zeros(values.shape, F32)
+    for k, part in enumerate(parts):
+        total = jnp.where(levels == k, part, total)
+    return total
+
+
+def build_first(w, b, hid):
+    x_cols, y_cols, step = 6 * 64 + ONES, 6 * 128, 512
+
+    def source(q, n):
+        s = n >> 9
+        m = n & (step - 1)
+        in_x = (s < 4) & (m < 384) & (q == 4 * s + ((m >> 4) & 3))
+        in_y = (n >= 4 * step) & (q == (((n - 4 * step) & 127) >> 3))
+        return in_x | in_y
+
+    spread_out = exact(w, pick((16, 4 * step + y_cols), source, F32))
+    _, n = rows_cols(spread_out.shape)
+    block = jnp.where(n < 4 * step, (n & (step - 1)) >> 6, (n - 4 * step) >> 7)
+    spread_out = choose(spread_out, level_of(block))
+
+    at, _ = rows_cols((x_cols, hid))
+    rows = jnp.zeros((x_cols, hid), F32)
+    for k, level in enumerate(split3(b)):
+        rows = jnp.where(at == 384 + k, jnp.broadcast_to(level.astype(F32), (x_cols, hid)), rows)
+    bias = dot_nt(pick((hid, hid), lambda q, n: q == n), rows.astype(BF16))
+
+    r, c = rows_cols((FACES * hid, x_cols))
+    shift = jnp.where(c < 384, (c & 15) - quot(r, hid), -1)
+    first_x = stack([bias] * FACES)
     for s in range(4):
-        rights = [
-            pick((16, cols), lambda q, n: (n < 384) & (level_of(n >> 6) == lev) & (q == 4 * s + ((n >> 4) & 3)))
-            for lev in range(3)
-        ]
-        part = place(None, w, rights)
-        total = total + jnp.where((c & 15) - (quot(r, hid)) == s, stack([part] * FACES), 0.0)
-    levels = split3(b)
-    at, _ = rows_cols((cols, hid))
-    rows = jnp.zeros((cols, hid), F32)
-    for lev in range(3):
-        rows = jnp.where(at == 384 + lev, jnp.broadcast_to(levels[lev].astype(F32), (cols, hid)), rows)
-    bias = dot_nt(pick((wide, hid), lambda q, n: (rest(q, hid)) == n), rows.astype(BF16))
-    return (jnp.where(c < 384, total, 0.0) + bias).astype(BF16)
-
-
-def build_first_y(w, hid):
-    wide, cols = FACES * hid, 6 * 128
-    shape = (wide, cols)
-    r, c = rows_cols(shape)
-    rights = [
-        pick((16, cols), lambda q, n: (level_of(n >> 7) == lev) & (q == ((n & 127) >> 3))) for lev in range(3)
-    ]
-    part = place(None, w, rights)
-    return jnp.where((c & 7) == (quot(r, hid)), stack([part] * FACES), 0.0).astype(BF16)
+        part = spread_out[:, s * step : s * step + x_cols]
+        first_x = jnp.where(shift == s, stack([part] * FACES), first_x)
+    r, c = rows_cols((FACES * hid, y_cols))
+    first_y = jnp.where((c & 7) == quot(r, hid), stack([spread_out[:, 4 * step :]] * FACES), 0.0)
+    return first_x.astype(BF16), first_y.astype(BF16)
+
+
+def build_first_back(w_t, hid):
+    wide = FACES * hid
+
+    def source(q, n):
+        in_x = (q < 512) & (n == 4 * (q >> 7) + ((q & 63) >> 4))
+        in_y = (q >= 512) & (n == (((q - 512) & 127) >> 3))
+        return in_x | in_y
+
+    rows = exact(pick((512 + 256, 16), source, F32), w_t)
+    right = pick((hid, 2 * wide), lambda q, n: rest(n, hid) == q)
+    high, low = (dot(part, right) for part in split(rows))
+    r, c = rows_cols(high.shape)
+    is_low = jnp.where(r < 512, r & 64, (r - 512) & 128) > 0
+    value = jnp.where(is_low, jnp.where(c < wide, low, 0.0), high)
+    face = quot(rest(c, wide), hid)
+    r, c = r[:128], c[:128]
+    shift = (r & 15) - face[:128]
+    back_x = jnp.zeros((128, 2 * wide), F32)
+    for s in range(4):
+        back_x = jnp.where(shift == s, value[128 * s : 128 * (s + 1)], back_x)
+    r, _ = rows_cols((256, 2 * wide))
+    back_y = jnp.where((r & 7) == face[512:], value[512:], 0.0)
+    return back_x.astype(BF16), back_y.astype(BF16)
 
 
 def build_mid(w, hid):
     block = 2 * hid
-    shape = (2 * block, 4 * block)
-    r, c = rows_cols(shape)
-
-    def rights(levels):
-        def test(lev):
-            def inner(q, n):
-                at = jnp.full(n.shape, -1, jnp.int32)
-                for k, level in enumerate(levels):
-                    at = jnp.where(quot(n, block) == k, level, at)
-                return (at == lev) & ((rest(n, hid)) == q)
-
-            return inner
-
-        return [pick((hid, 4 * block), test(lev)) for lev in range(3)]
-
-    upper = place(None, w, rights((0, 0, 0, 2)))
-    lower = place(None, w, rights((1, 1, -1, -1)))
-    keep = (quot(rest(r, block), hid)) == (quot(rest(c, block), hid))
+    tiled = exact(w, pick((hid, 4 * block), lambda q, n: rest(n, hid) == q, F32))
+    _, n = rows_cols(tiled.shape)
+    upper = choose(tiled, jnp.where(n < 3 * block, 0, 2))
+    lower = choose(tiled, jnp.where(n < 2 * block, 1, -1))
+    r, c = rows_cols((2 * block, 4 * block))
+    keep = quot(rest(r, block), hid) == quot(rest(c, block), hid)
     return jnp.where(keep, stack([upper, upper, lower, lower]), 0.0).astype(BF16)
 
 
 def build_mid_back(w, hid):
     block = 2 * hid
-    shape = (block, 3 * block)
-    r, c = rows_cols(shape)
-    eye = pick((hid, hid), lambda q, n: q == n)
-    rights = [
-        pick((hid, 3 * block), lambda q, n: ((quot(n, block) == 1) == (lev == 1)) & ((rest(n, hid)) == q))
-        for lev in range(2)
-    ]
-    part = place(lambda v: dot_nt(eye, v), w[:2], rights)
-    return jnp.where((quot(r, hid)) == (quot(rest(c, block), hid)), stack([part] * 2), 0.0).astype(BF16)
+    turned = exact_nt(pick((hid, hid), lambda q, n: q == n, F32), w)
+    tiled = exact(turned, pick((hid, 3 * block), lambda q, n: rest(n, hid) == q, F32))
+    _, n = rows_cols(tiled.shape)
+    tiled = choose(tiled, jnp.where(quot(n, block) == 1, 1, 0))
+    r, c = rows_cols((block, 3 * block))
+    keep = quot(r, hid) == quot(rest(c, block), hid)
+    return jnp.where(keep, stack([tiled] * 2), 0.0).astype(BF16)
 
 
 def build_out(w, hid):
     wide = FACES * hid
-    shape = (64, wide)
-    r, c = rows_cols(shape)
-    right = pick((hid, wide), lambda q, n: (rest(n, hid)) == q)
-    left = pick((64, 8), lambda q, n: (q >> 3) == n)
-    keep = (r & 7) == (quot(c, hid))
-    return stack([jnp.where(keep, dot(dot(left, v).astype(BF16), right), 0.0) for v in w]).astype(BF16)
-
-
-def spread_bias(b, rows, lanes, unit):
-    n = b.shape[1]
-    return exact_nt(pick((rows, n), lambda q, m: unit(q) == m, F32), jnp.broadcast_to(b, (lanes, n)))
+    rows = exact(pick((64, 8), lambda q, n: (q >> 3) == n, F32), w)
+    tiled = dot(stack(list(split3(rows))), pick((hid, wide), lambda q, n: rest(n, hid) == q))
+    r, c = rows_cols(tiled.shape)
+    return jnp.where((r & 7) == quot(c, hid), tiled, 0.0).astype(BF16)
 
 
 def build_out_back(w, hid):
     wide = FACES * hid
-    shape = (wide, 192)
-    r, c = rows_cols(shape)
-    left = pick((wide, hid), lambda q, n: (rest(q, hid)) == n)
-
-    rights = [
-        pick((8, 192), lambda q, n: (((n >> 6) == 1) == (lev == 1)) & (((n & 63) >> 3) == q)) for lev in range(2)
-    ]
-    part = place(lambda v: dot_nt(left, v), w[:2], rights)
-    return jnp.where((quot(r, hid)) == (c & 7), part, 0.0).astype(BF16)
-
-
-def build_first_x_back(w, hid):
-    wide = FACES * hid
-    shape = (128, 2 * wide)
-    r, c = rows_cols(shape)
-    right = pick((hid, 2 * wide), lambda q, n: (rest(n, hid)) == q)
-    total = jnp.zeros(shape, F32)
-    for s in range(4):
-        left = pick((128, 16), lambda q, n: n == 4 * s + ((q & 63) >> 4))
-
-        def one(values):
-            return dot(dot_nt(left, values).astype(BF16), right)
-
-        value = jnp.where(r < 64, one(w[0]), jnp.where(c < wide, one(w[1]), 0.0))
-        total = total + jnp.where((r & 15) - (quot(rest(c, wide), hid)) == s, value, 0.0)
-    return total.astype(BF16)
-
-
-def build_first_y_back(w, hid):
-    wide = FACES * hid
-    shape = (256, 2 * wide)
-    r, c = rows_cols(shape)
-    right = pick((hid, 2 * wide), lambda q, n: (rest(n, hid)) == q)
-    left = pick((256, 16), lambda q, n: n == ((q & 127) >> 3))
-
-    def one(values):
-        return dot(dot_nt(left, values).astype(BF16), right)
-
-    value = jnp.where(r < 128, one(w[0]), jnp.where(c < wide, one(w[1]), 0.0))
-    return jnp.where((r & 7) == (quot(rest(c, wide), hid)), value, 0.0).astype(BF16)
+    turned = exact_nt(pick((hid, hid), lambda q, n: q == n, F32), w)
+    tiled = exact(turned, pick((8, 192), lambda q, n: ((n & 63) >> 3) == q, F32))
+    _, n = rows_cols(tiled.shape)
+    tiled = choose(tiled, jnp.where((n >> 6) == 1, 1, 0))
+    r, c = rows_cols((wide, 192))
+    return jnp.where(quot(r, hid) == (c & 7), stack([tiled] * FACES), 0.0).astype(BF16)
+
+
+def spread_bias(b, lanes, copies):
+    n = b.shape[1]
+    rows = exact_nt(pick((n, n), lambda q, m: q == m, F32), jnp.broadcast_to(b, (lanes, n)))
+    return stack([rows] * copies)
 
 
 def spread(bias_ref, width):
@@ -393,21 +368,19 @@
     for one in copies[:6]:
         one.wait()
     w_in, b_in, w_mid, b_mid, w_out, b_out = small
-    eye = pick((hid, hid), lambda q, n: q == n)
-    wi = [dot_nt(eye, level).astype(BF16) for level in split3(w_in[...])]
-    wm, wo = split3(w_mid[...]), split3(w_out[...])
     lanes = out_bias.shape[1]
-    first_x[...] = build_first_x(wi, b_in[...], hid)
-    first_y[...] = build_first_y(wi, hid)
-    first_bias[...] = spread_bias(b_in[...], FACES * hid, lanes, lambda q: rest(q, hid))
-    mid[...] = build_mid(wm, hid)
-    mid_bias[...] = spread_bias(b_mid[...], 2 * hid, lanes, lambda q: rest(q, hid))
-    out[...] = build_out(wo, hid)
-    out_bias[...] = spread_bias(b_out[...], 64, lanes, lambda q: q >> 3)
-    out_back[...] = build_out_back(wo, hid)
-    mid_back[...] = build_mid_back(wm, hid)
-    first_x_back[...] = build_first_x_back(wi, hid)
-    first_y_back[...] = build_first_y_back(wi, hid)
+    w_in_rows = exact_nt(pick((hid, hid), lambda q, n: q == n, F32), w_in[...])
+    first_x[...], first_y[...] = build_first(w_in_rows, b_in[...], hid)
+    first_bias[...] = spread_bias(b_in[...], lanes, FACES)
+    mid[...] = build_mid(w_mid[...], hid)
+    mid_bias[...] = spread_bias(b_mid[...], lanes, 2)
+    out[...] = build_out(w_out[...], hid)
+    out_bias[...] = exact_nt(
+        pick((64, 8), lambda q, n: (q >> 3) == n, F32), jnp.broadcast_to(b_out[...], (lanes, 8))
+    )
+    out_back[...] = build_out_back(w_out[...], hid)
+    mid_back[...] = build_mid_back(w_mid[...], hid)
+    first_x_back[...], first_y_back[...] = build_first_back(w_in[...], hid)
 
     for one in copies[6:]:
         one.wait()
@@ -521,16 +494,19 @@
     return out
 
 
-def fold_first_x(acc, hid):
-    shape = acc.shape
-    r, c = rows_cols(shape)
-    fold = pick((shape[1], hid), lambda q, n: rest(n - q, hid) == 0, F32)
-    face = quot(c, hid)
+def fold_faces(rows, hid, lanes):
+    fold = pick((rows.shape[1], lanes), lambda q, n: (rest(n - q, hid) == 0) & (n >= hid) & (n < 2 * hid), F32)
+    return exact(rows, fold)
+
+
+def fold_first_x(acc, hid, lanes):
+    r, c = rows_cols(acc.shape)
+    shift = jnp.where(r < 64, (r & 15) - quot(c, hid), -1)
     parts = [
-        jnp.where((((r & 15) - face) == s) & (r < 64) | (r >= 64) & (s == 0), acc, 0.0)[: 80 if s == 0 else 64]
-        for s in range(4)
+        jnp.where((shift == s) | (r >= 64) & (s == 0), acc, 0.0)[: 64 + ONES if s == 0 else 64] for s in range(4)
     ]
-    folded = exact(stack(parts), fold)
+    folded = fold_faces(stack(parts), hid, lanes)
+
     def test(q, n):
         at = jnp.where(n < 64, n, n - ONES)
         return ((n < 64) | (n >= 64 + ONES)) & (q == (at >> 4)) | (n == 64) & (q == 16)
@@ -538,16 +514,14 @@
     return exact(pick((24, folded.shape[0]), test, F32), folded)
 
 
-def fold_first_y(acc, hid):
-    shape = acc.shape
-    r, c = rows_cols(shape)
-    fold = pick((shape[1], hid), lambda q, n: (rest(q, hid)) == n, F32)
-    keep = ((r & 7) == (quot(c, hid))) | (r >= 128)
+def fold_first_y(acc, hid, lanes):
+    r, c = rows_cols(acc.shape)
+    keep = ((r & 7) == quot(c, hid)) | (r >= 128)
     sel = lambda q, n: ((n < 128) & (q == (n >> 3))) | ((n == 128) & (q == 16))
-    return exact(pick((24, shape[0]), sel, F32), exact(jnp.where(keep, acc, 0.0), fold))
-
-
-def back_kernel(state, cot, middle, own, from_left, from_right,
+    return exact(pick((24, acc.shape[0]), sel, F32), fold_faces(jnp.where(keep, acc, 0.0), hid, lanes))
+
+
+def back_kernel(odd, state, cot, middle, own, from_first, from_second,
                 first_x, first_y, first_bias, mid, mid_bias, out, out_bias,
                 out_back, mid_back, first_x_back, first_y_back,
                 h1_hi, h1_lo, h2_hi, h2_lo, gates_in,
@@ -569,17 +543,19 @@
 
     lane = lane_index(ny)
     spot = lane & (SEG - 1)
+    is_odd = jnp.full((FACES, ny), odd[0], jnp.int32) == 1
     for v in range(8):
         for g in range(rim_groups):
             rows = pl.ds(g * FACES, FACES)
-            mine = own[v, rows, :]
+            mine, first, second = own[v, rows, :], from_first[v, rows, :], from_second[v, rows, :]
+            left, right = jnp.where(is_odd, first, second), jnp.where(is_odd, second, first)
             value = jnp.where(
                 spot < RIM,
-                turn(from_left[v, rows, :], -RIM, 1),
+                turn(left, -RIM, 1),
                 jnp.where(
                     spot < 2 * RIM,
                     turn(mine, -RIM, 1),
-                    jnp.where(spot < 3 * RIM, turn(mine, RIM, 1), turn(from_right[v, rows, :], RIM, 1)),
+                    jnp.where(spot < 3 * RIM, turn(mine, RIM, 1), turn(right, RIM, 1)),
                 ),
             )
             if v < 4:
@@ -731,39 +707,37 @@
             at = (k + 1) % PAIR * half * FACES
             grads[c][pl.ds(at, FACES), :] += last[c][:, k * ny : (k + 1) * ny]
 
-    eye = pick((hid, hid), lambda q, n: q == n, F32)
-    grad_first = fold_first_x(acc_x[...], hid) + fold_first_y(acc_y[...], hid)
+    lanes = g_weights.shape[1]
+    grad_first = fold_first_x(acc_x[...], hid, lanes) + fold_first_y(acc_y[...], hid, lanes)
     both = acc_mid[...]
     grad_mid = both[:hid, :hid] + both[:hid, hid:] + both[hid : 2 * hid, :hid]
+    grad_mid = exact_nt(
+        pick((hid, hid), lambda q, n: q == n, F32), stack([grad_mid, jnp.zeros((lanes - hid, hid), F32)])
+    )
     grad_mid_bias = both[2 * hid :, :hid] + both[2 * hid :, hid:]
     r, c = rows_cols(acc_out.shape)
-    fold = pick((acc_out.shape[1], hid), lambda q, n: (rest(q, hid)) == n, F32)
-    rows = pick((8, 64), lambda q, n: (n >> 3) == q, F32)
-    grad_out = exact(rows, exact(jnp.where((r & 7) == (quot(c, hid)), acc_out[...], 0.0), fold))
+    grad_out = exact(
+        pick((8, 64), lambda q, n: (n >> 3) == q, F32),
+        fold_faces(jnp.where((r & 7) == quot(c, hid), acc_out[...], 0.0), hid, lanes),
+    )
     out_bias_rows = exact_nt(jnp.ones((8, acc_out_bias.shape[1]), F32), acc_out_bias[...])
-    grad_out_bias = exact_nt(out_bias_rows, pick((hid, 64), lambda q, n: (n >> 3) == q, F32))
-    r, c = rows_cols((8, hid))
-    biases = jnp.where(
-        r == 0,
-        grad_first[16:24],
-        jnp.where(r == 1, jnp.broadcast_to(grad_mid_bias[:1], (8, hid)), jnp.where(r == 2, grad_out_bias, 0.0)),
-    )
-    g_weights[...] = jnp.zeros(g_weights.shape, F32)
-    g_weights[:, :hid] = stack([exact_nt(eye, grad_mid), grad_first[:16], grad_out, biases])
-
-
-def finish_kernel(parts, g_w_in, g_b_in, g_w_mid, g_b_mid, g_w_out, g_b_out):
+    grad_out_bias = exact_nt(out_bias_rows, pick((lanes, 64), lambda q, n: (n >> 3) == q - hid, F32))
+    r, c = rows_cols((8, lanes))
+    biases = jnp.where(r == 0, grad_first[16:24], jnp.where(r == 1, grad_out_bias, 0.0))
+    g_weights[:hid, :] = grad_mid + stack([grad_first[:16], grad_out, biases])
+    g_weights[hid:, :] = jnp.zeros((8, lanes), F32)
+    g_weights[hid:, :hid] = grad_mid_bias[:8]
+
+
+def finish_kernel(total, g_w_in, g_b_in, g_w_mid, g_b_mid, g_w_out, g_b_out):
     hid = g_w_mid.shape[0]
-    found = [parts[k] for k in range(parts.shape[0])]
-    while len(found) > 1:
-        found = [found[k] + found[k + 1] if k + 1 < len(found) else found[k] for k in range(0, len(found), 2)]
-    total = found[0][:, :hid]
-    g_w_mid[...] = total[:hid]
-    g_w_in[...] = total[hid : hid + 16]
-    g_w_out[...] = total[hid + 16 : hid + 24]
-    g_b_in[...] = total[hid + 24 : hid + 25]
-    g_b_mid[...] = total[hid + 25 : hid + 26]
-    g_b_out[...] = total[hid + 26 : hid + 27, :8]
+    g_w_mid[...] = total[:hid, :hid]
+    beside = total[:hid, hid : 2 * hid]
+    g_w_in[...] = beside[:16]
+    g_w_out[...] = beside[16:24]
+    g_b_in[...] = beside[24:25]
+    g_b_out[...] = beside[25:26, :8]
+    g_b_mid[...] = total[hid : hid + 1, :hid]
 
 
 def whole(count, space=pltpu.VMEM):
@@ -782,14 +756,14 @@
     )(*operands)
 
 
-def others(values, axis, size):
-    return [lax.ppermute(values, axis, [(i, i ^ k) for i in range(size)]) for k in range(1, size)]
-
-
-def tree_sum(parts):
-    while len(parts) > 1:
-        parts = [parts[k] + parts[k + 1] for k in range(0, len(parts), 2)]
-    return parts[0]
+def sum_all(values, sizes):
+    for axis, size in sizes.items():
+        if size & (size - 1):
+            values = lax.psum(values, axis)
+            continue
+        for k in range(size.bit_length() - 1):
+            values = values + lax.ppermute(values, axis, [(i, i ^ (1 << k)) for i in range(size)])
+    return values
 
 
 def body(sizes, density, momentum, tracer, cotangent, w_in, b_in, w_mid, b_mid, w_out, b_out):
@@ -830,8 +804,9 @@
         scratch=[pltpu.VMEM(one.shape, F32) for one in operands[4:]] + [pltpu.SemaphoreType.DMA((10,))],
     )
     axes = ("tx", "ty")
-    from_left = lax.ppermute(rim, axes, [(i, (i + 1) % ring) for i in range(ring)])
-    from_right = lax.ppermute(rim, axes, [((i + 1) % ring, i) for i in range(ring)])
+    swaps = [[(i, (i + 1 if (i + first) % 2 == 0 else i - 1) % ring) for i in range(ring)] for first in range(2)]
+    from_first, from_second = (lax.ppermute(rim, axes, swap) for swap in swaps)
+    odd = (lax.axis_index(axes) % 2).astype(jnp.int32).reshape(1)
 
     middle, *kept = call(
         x_forward_kernel,
@@ -849,9 +824,10 @@
             shape(density.shape, F32),
             shape(momentum.shape, F32),
             shape(tracer.shape, F32),
-            shape((2 * hid, 128), F32),
+            shape((hid + 8, 128), F32),
         ],
-        [state, cots, middle, rim, from_left, from_right] + matrices + kept,
+        [odd, state, cots, middle, rim, from_first, from_second] + matrices + kept,
+        in_spaces=whole(1, pltpu.SMEM) + whole(6 + len(matrices) + len(kept)),
         scratch=[
             pltpu.VMEM((4, rim_rows + FACES, ny), F32),
             pltpu.VMEM((4, rim_rows, ny), F32),
@@ -868,7 +844,7 @@
         flops=4 * 10**10,
         moved=2 * 10**7,
     )
-    everyone = lax.all_gather(g_weights, ("traj", "tx", "ty"))
+    total = sum_all(g_weights, sizes)
     g_w_in, g_b_in, g_w_mid, g_b_mid, g_w_out, g_b_out = call(
         finish_kernel,
         [
@@ -879,7 +855,7 @@
             shape(w_out.shape, F32),
             shape((1, b_out.shape[0]), F32),
         ],
-        [everyone],
+        [total],
     )
     return (g_den, g_mom, g_tra, g_w_in.T, g_b_in[0], g_w_mid, g_b_mid[0], g_w_out, g_b_out[0])
 

time: 114 us -> 74.7 us (0.66)
  waiting for transfers between devices: 55.4 us -> 12.4 us
  between operations: 14.1 us -> 0.69 us
  local copies, waits for them, and re-layouts: 1.22 us -> 14 us
  starting transfers between devices: 6.1 us -> 10.9 us
    all_gather x1 -> x0, waiting for transfers between devices: 53.1 us -> none  [body(): everyone = lax.all_gather(g_weights, ('traj', 'tx', 'ty'))]
    unnamed x2 -> x20, local copies, waits for them, and re-layouts: 1.22 us -> 14 us
    ppermute x2 -> x7, waiting for transfers between devices: 2.25 us -> 12.4 us  [the longest x5 12.4 us: sum_all(): lax.ppermute(values, axis, [(i, i ^ 1 << k) for i in range(size)])]
    ppermute x2 -> x7, starting transfers between devices: 6.06 us -> 10.9 us  [the longest x2 6.07 us: body(): from_first, from_second = (lax.ppermute(rim, axes, swap) for swap in swaps)]
  transfers between devices with their start and end apart: 3 -> 7, of which waited for: 2 -> 5; matrix products, arithmetic and copies ran while one was open for 0% -> 0% of each run, Pallas kernels for 5% -> 7%
where the time goes in v4:
time: 74.7 us; the launch traced here: 74.4 us
  Pallas kernels  36.4 us (49%)
  local copies, waits for them, and re-layouts  14 us (19%)
  waiting for transfers between devices  12.4 us (17%)
  starting transfers between devices  10.9 us (15%)
    pallas_call x4, Pallas kernels, call(): pl.pallas_call(kernel, out_shape=outs, in_specs=in_spaces or whole(len(op...  36.4 us
    unnamed x20, local copies, waits for them, and re-layouts  14 us
    ppermute x5, waiting for transfers between devices, sum_all(): lax.ppermute(values, axis, [(i, i ^ 1 << k) for i in range(size)])  12.4 us
    ppermute x2, starting transfers between devices, body(): from_first, from_second = (lax.ppermute(rim, axes, swap) for swap in swaps)  6.07 us
    ppermute x5, starting transfers between devices, sum_all(): lax.ppermute(values, axis, [(i, i ^ 1 << k) for i in range(size)])  4.83 us
  transfers between devices with their start and end apart: 7, of which 5 were waited for; matrix products, arithmetic and copies ran while one was open for 0% of the time, Pallas kernels for 7%

profile of v4, /device:TPU:0, one launch (start us, length us, event | category | flops | bytes accessed | tf_op | source)
XLA Modules:
  0.0 74.4 jit_solution(4322579492599044338)
XLA Ops:
  0.6 3.8 %shard_map.169 = (f32[8,32,128]{2,1,0:T(8,128)S(1)}, f32[4,256,128]{2,1,0:T(8,128)S(1)}, f32[4,256,128]{2,1,0:T(8,128)S(1)}, bf16[256,400]{1,0:T(8,128)(2,1)S(1)...) custom-call(f32[1,256,128]{2,1,0:T(8,128)} %den.1, ...), custom_call_target="tpu_custom_call" | custom-call | tf_op jit(solution)/shard_map/pallas_call | solution.py:748
  4.4 6.1 %collective-permute-start.1 = (f32[8,32,128]{2,1,0:T(8,128)S(1)}, f32[8,32,128]{2,1,0:T(8,128)S(1)}, u32[]{:S(2)}, u32[]{:S(2)}) collective-permute-start(f32[8,32,128]{2,1,0:T(8,128)S(1)} %get-tuple-element.47.own), channel_id=1, source_target_pairs={{0,7},{1,2},{2,1},{3,4},{4,3},{5,6},{6,5},{7,0},{8,15},{9,10},{10,... | collective-permute-start | bytes 393224 | tf_op jit(solution)/shard_map/ppermute | solution.py:808
  10.5 5.4 %shard_map.170 = (f32[4,256,128]{2,1,0:T(8,128)S(1)}, bf16[4,256,1024]{2,1,0:T(8,128)(2,1)S(1)}, bf16[4,256,1024]{2,1,0:T(8,128)(2,1)S(1)}, bf16[4,256,1024]{2,1...) custom-call(f32[4,256,128]{2,1,0:T(8,128)S(1)} %get-tuple-element.39.state, ...), custom_call_target="tpu_custom_call" | custom-call | flops 10000000000 | bytes 10000000 | tf_op jit(solution)/shard_map/pallas_call | solution.py:748
  15.9 1.3 %copy-done = bf16[4,256,1024]{2,1,0:T(8,128)(2,1)} copy-done((bf16[4,256,1024]{2,1,0:T(8,128)(2,1)}, bf16[4,256,1024]{2,1,0:T(8,128)(2,1)S(1)}, u32[]{:S(2)}) %copy-start) | copy-done | bytes 2097176
  17.3 1.3 %copy-done.2 = bf16[4,256,1024]{2,1,0:T(8,128)(2,1)} copy-done((bf16[4,256,1024]{2,1,0:T(8,128)(2,1)}, bf16[4,256,1024]{2,1,0:T(8,128)(2,1)S(1)}, u32[]{:S(2)}) %copy-start.2) | copy-done | bytes 2097176
  18.6 1.4 %copy-done.4 = bf16[4,256,1024]{2,1,0:T(8,128)(2,1)} copy-done((bf16[4,256,1024]{2,1,0:T(8,128)(2,1)}, bf16[4,256,1024]{2,1,0:T(8,128)(2,1)S(1)}, u32[]{:S(2)}) %copy-start.4) | copy-done | bytes 2097176
  19.9 1.4 %copy-done.6 = bf16[4,256,1024]{2,1,0:T(8,128)(2,1)} copy-done((bf16[4,256,1024]{2,1,0:T(8,128)(2,1)}, bf16[4,256,1024]{2,1,0:T(8,128)(2,1)S(1)}, u32[]{:S(2)}) %copy-start.6) | copy-done | bytes 2097176
  21.3 1.1 %copy-done.8 = f32[4,64,1024]{2,1,0:T(8,128)} copy-done((f32[4,64,1024]{2,1,0:T(8,128)}, f32[4,64,1024]{2,1,0:T(8,128)S(1)}, u32[]{:S(2)}) %copy-start.8) | copy-done | bytes 1048600
  22.4 1.6 %copy-done.1 = bf16[4,256,1024]{2,1,0:T(8,128)(2,1)S(1)} copy-done((bf16[4,256,1024]{2,1,0:T(8,128)(2,1)S(1)}, bf16[4,256,1024]{2,1,0:T(8,128)(2,1)}, u32[]{:S(2)}) %copy-start.1) | copy-done | bytes 2097176
  23.9 1.6 %copy-done.3 = bf16[4,256,1024]{2,1,0:T(8,128)(2,1)S(1)} copy-done((bf16[4,256,1024]{2,1,0:T(8,128)(2,1)S(1)}, bf16[4,256,1024]{2,1,0:T(8,128)(2,1)}, u32[]{:S(2)}) %copy-start.3) | copy-done | bytes 2097176
  25.5 1.6 %copy-done.5 = bf16[4,256,1024]{2,1,0:T(8,128)(2,1)S(1)} copy-done((bf16[4,256,1024]{2,1,0:T(8,128)(2,1)S(1)}, bf16[4,256,1024]{2,1,0:T(8,128)(2,1)}, u32[]{:S(2)}) %copy-start.5) | copy-done | bytes 2097176
  27.1 1.6 %copy-done.7 = bf16[4,256,1024]{2,1,0:T(8,128)(2,1)S(1)} copy-done((bf16[4,256,1024]{2,1,0:T(8,128)(2,1)S(1)}, bf16[4,256,1024]{2,1,0:T(8,128)(2,1)}, u32[]{:S(2)}) %copy-start.7) | copy-done | bytes 2097176
  28.7 1.2 %copy-done.9 = f32[4,64,1024]{2,1,0:T(8,128)S(1)} copy-done((f32[4,64,1024]{2,1,0:T(8,128)S(1)}, f32[4,64,1024]{2,1,0:T(8,128)}, u32[]{:S(2)}) %copy-start.9) | copy-done | bytes 1048600
  29.9 26.5 %shard_map.171 = (f32[1,256,128]{2,1,0:T(8,128)}, f32[1,2,256,128]{3,2,1,0:T(8,128)}, f32[1,256,128]{2,1,0:T(8,128)}, f32[40,128]{1,0:T(8,128)S(1)}) custom-call(s32[1]{0:T(128)} %bitcast.odd, f32[4,256,128]{2,1,0:T(8,128)S(1)} %get-tuple-element.39.state, f32[4,256,128]{2,1,0:T(8,128)S(1)} %get-tuple-element.40.cot, ...), custom_call_target="tpu_custom_call" | custom-call | flops 40000000000 | bytes 20000000 | tf_op jit(solution)/shard_map/pallas_call | solution.py:748
  56.5 1.2 %collective-permute-done.2 = f32[40,128]{1,0:T(8,128)S(1)} collective-permute-done((f32[40,128]{1,0:T(8,128)S(1)}, f32[40,128]{1,0:T(8,128)S(1)}, u32[]{:S(2)}, u32[]{:S(2)}) %collective-permute-start.2) | collective-permute-done | bytes 20512 | tf_op jit(solution)/shard_map/ppermute | solution.py:765
  57.7 1.5 %collective-permute-start.3 = (f32[40,128]{1,0:T(8,128)S(1)}, f32[40,128]{1,0:T(8,128)S(1)}, u32[]{:S(2)}, u32[]{:S(2)}) collective-permute-start(f32[40,128]{1,0:T(8,128)S(1)} %add.24), channel_id=1, source_target_pairs={{0,16},{8,24},{16,0},{24,8},{1,17},{9,25},{17,1},{25,9},{2,18},{10... | collective-permute-start | bytes 61448 | tf_op jit(solution)/shard_map/ppermute | solution.py:765
  59.2 2.3 %collective-permute-done.3 = f32[40,128]{1,0:T(8,128)S(1)} collective-permute-done((f32[40,128]{1,0:T(8,128)S(1)}, f32[40,128]{1,0:T(8,128)S(1)}, u32[]{:S(2)}, u32[]{:S(2)}) %collective-permute-start.3) | collective-permute-done | bytes 20512 | tf_op jit(solution)/shard_map/ppermute | solution.py:765
  61.5 0.5 collective-permute-start.4
  62.0 3.3 %collective-permute-done.4 = f32[40,128]{1,0:T(8,128)S(1)} collective-permute-done((f32[40,128]{1,0:T(8,128)S(1)}, f32[40,128]{1,0:T(8,128)S(1)}, u32[]{:S(2)}, u32[]{:S(2)}) %collective-permute-start.4) | collective-permute-done | bytes 20512 | tf_op jit(solution)/shard_map/ppermute | solution.py:765
  65.2 2.0 %collective-permute-start.5 = (f32[40,128]{1,0:T(8,128)S(1)}, f32[40,128]{1,0:T(8,128)S(1)}, u32[]{:S(2)}, u32[]{:S(2)}) collective-permute-start(f32[40,128]{1,0:T(8,128)S(1)} %add.26), channel_id=1, source_target_pairs={{0,1},{1,0},{2,3},{3,2},{4,5},{5,4},{6,7},{7,6},{8,9},{9,8},{10,11... | collective-permute-start | bytes 61448 | tf_op jit(solution)/shard_map/ppermute | solution.py:765
  67.3 1.8 %collective-permute-done.5 = f32[40,128]{1,0:T(8,128)S(1)} collective-permute-done((f32[40,128]{1,0:T(8,128)S(1)}, f32[40,128]{1,0:T(8,128)S(1)}, u32[]{:S(2)}, u32[]{:S(2)}) %collective-permute-start.5) | collective-permute-done | bytes 20512 | tf_op jit(solution)/shard_map/ppermute | solution.py:765
  69.0 0.8 %collective-permute-start.6 = (f32[40,128]{1,0:T(8,128)S(1)}, f32[40,128]{1,0:T(8,128)S(1)}, u32[]{:S(2)}, u32[]{:S(2)}) collective-permute-start(f32[40,128]{1,0:T(8,128)S(1)} %add.27), channel_id=1, source_target_pairs={{0,2},{1,3},{2,0},{3,1},{4,6},{5,7},{6,4},{7,5},{8,10},{9,11},{10,... | collective-permute-start | bytes 61448 | tf_op jit(solution)/shard_map/ppermute | solution.py:765
  69.8 3.9 %collective-permute-done.6 = f32[40,128]{1,0:T(8,128)S(1)} collective-permute-done((f32[40,128]{1,0:T(8,128)S(1)}, f32[40,128]{1,0:T(8,128)S(1)}, u32[]{:S(2)}, u32[]{:S(2)}) %collective-permute-start.6) | collective-permute-done | bytes 20512 | tf_op jit(solution)/shard_map/ppermute | solution.py:765
  73.7 0.7 shard_map.172
  (19 shorter events, 0.0 us)
Async XLA Ops:
  4.4 17.9 %collective-permute-start.1 = (f32[8,32,128]{2,1,0:T(8,128)S(1)}, f32[8,32,128]{2,1,0:T(8,128)S(1)}, u32[]{:S(2)}, u32[]{:S(2)}) collective-permute-start(f32[8,32,128]{2,1,0:T(8,128)S(1)} %get-tuple-element.47.own), channel_id=1, source_target_pairs={{0,7},{1,2},{2,1},{3,4},{4,3},{5,6},{6,5},{7,0},{8,15},{9,10},{10,... | collective-permute-start | bytes 393224 | tf_op jit(solution)/shard_map/ppermute | solution.py:808
  10.5 11.8 %collective-permute-start = (f32[8,32,128]{2,1,0:T(8,128)S(1)}, f32[8,32,128]{2,1,0:T(8,128)S(1)}, u32[]{:S(2)}, u32[]{:S(2)}) collective-permute-start(f32[8,32,128]{2,1,0:T(8,128)S(1)} %get-tuple-element.47.own), channel_id=1, source_target_pairs={{0,1},{1,0},{2,3},{3,2},{4,5},{5,4},{6,7},{7,6},{8,9},{9,8},{10,11... | collective-permute-start | bytes 393224 | tf_op jit(solution)/shard_map/ppermute | solution.py:808
  15.9 1.3 %copy-start = (bf16[4,256,1024]{2,1,0:T(8,128)(2,1)}, bf16[4,256,1024]{2,1,0:T(8,128)(2,1)S(1)}, u32[]{:S(2)}) copy-start(bf16[4,256,1024]{2,1,0:T(8,128)(2,1)S(1)} %get-tuple-element.54.h1_hi) | copy-start | bytes 6291460
  17.2 1.3 %copy-start.2 = (bf16[4,256,1024]{2,1,0:T(8,128)(2,1)}, bf16[4,256,1024]{2,1,0:T(8,128)(2,1)S(1)}, u32[]{:S(2)}) copy-start(bf16[4,256,1024]{2,1,0:T(8,128)(2,1)S(1)} %get-tuple-element.55.h1_lo) | copy-start | bytes 6291460
  18.6 1.4 %copy-start.4 = (bf16[4,256,1024]{2,1,0:T(8,128)(2,1)}, bf16[4,256,1024]{2,1,0:T(8,128)(2,1)S(1)}, u32[]{:S(2)}) copy-start(bf16[4,256,1024]{2,1,0:T(8,128)(2,1)S(1)} %get-tuple-element.56.h2_hi) | copy-start | bytes 6291460
  19.9 1.4 %copy-start.6 = (bf16[4,256,1024]{2,1,0:T(8,128)(2,1)}, bf16[4,256,1024]{2,1,0:T(8,128)(2,1)S(1)}, u32[]{:S(2)}) copy-start(bf16[4,256,1024]{2,1,0:T(8,128)(2,1)S(1)} %get-tuple-element.57.h2_lo) | copy-start | bytes 6291460
  21.3 1.1 %copy-start.8 = (f32[4,64,1024]{2,1,0:T(8,128)}, f32[4,64,1024]{2,1,0:T(8,128)S(1)}, u32[]{:S(2)}) copy-start(f32[4,64,1024]{2,1,0:T(8,128)S(1)} %get-tuple-element.58.gates_in) | copy-start | bytes 3145732
  22.4 1.6 %copy-start.1 = (bf16[4,256,1024]{2,1,0:T(8,128)(2,1)S(1)}, bf16[4,256,1024]{2,1,0:T(8,128)(2,1)}, u32[]{:S(2)}) copy-start(bf16[4,256,1024]{2,1,0:T(8,128)(2,1)} %copy-done) | copy-start | bytes 6291460
  23.9 1.6 %copy-start.3 = (bf16[4,256,1024]{2,1,0:T(8,128)(2,1)S(1)}, bf16[4,256,1024]{2,1,0:T(8,128)(2,1)}, u32[]{:S(2)}) copy-start(bf16[4,256,1024]{2,1,0:T(8,128)(2,1)} %copy-done.2) | copy-start | bytes 6291460
  25.5 1.6 %copy-start.5 = (bf16[4,256,1024]{2,1,0:T(8,128)(2,1)S(1)}, bf16[4,256,1024]{2,1,0:T(8,128)(2,1)}, u32[]{:S(2)}) copy-start(bf16[4,256,1024]{2,1,0:T(8,128)(2,1)} %copy-done.4) | copy-start | bytes 6291460
  27.1 1.6 %copy-start.7 = (bf16[4,256,1024]{2,1,0:T(8,128)(2,1)S(1)}, bf16[4,256,1024]{2,1,0:T(8,128)(2,1)}, u32[]{:S(2)}) copy-start(bf16[4,256,1024]{2,1,0:T(8,128)(2,1)} %copy-done.6) | copy-start | bytes 6291460
  28.7 1.2 %copy-start.9 = (f32[4,64,1024]{2,1,0:T(8,128)S(1)}, f32[4,64,1024]{2,1,0:T(8,128)}, u32[]{:S(2)}) copy-start(f32[4,64,1024]{2,1,0:T(8,128)} %copy-done.8) | copy-start | bytes 3145732
  56.5 1.2 %collective-permute-start.2 = (f32[40,128]{1,0:T(8,128)S(1)}, f32[40,128]{1,0:T(8,128)S(1)}, u32[]{:S(2)}, u32[]{:S(2)}) collective-permute-start(f32[40,128]{1,0:T(8,128)S(1)} %get-tuple-element.62), channel_id=1, source_target_pairs={{0,8},{8,0},{16,24},{24,16},{1,9},{9,1},{17,25},{25,17},{2,10},{10... | collective-permute-start | bytes 61448 | tf_op jit(solution)/shard_map/ppermute | solution.py:765
  57.7 3.8 %collective-permute-start.3 = (f32[40,128]{1,0:T(8,128)S(1)}, f32[40,128]{1,0:T(8,128)S(1)}, u32[]{:S(2)}, u32[]{:S(2)}) collective-permute-start(f32[40,128]{1,0:T(8,128)S(1)} %add.24), channel_id=1, source_target_pairs={{0,16},{8,24},{16,0},{24,8},{1,17},{9,25},{17,1},{25,9},{2,18},{10... | collective-permute-start | bytes 61448 | tf_op jit(solution)/shard_map/ppermute | solution.py:765
  61.5 3.8 %collective-permute-start.4 = (f32[40,128]{1,0:T(8,128)S(1)}, f32[40,128]{1,0:T(8,128)S(1)}, u32[]{:S(2)}, u32[]{:S(2)}) collective-permute-start(f32[40,128]{1,0:T(8,128)S(1)} %add.25), channel_id=1, source_target_pairs={{0,4},{4,0},{1,5},{5,1},{2,6},{6,2},{3,7},{7,3},{8,12},{12,8},{9,1... | collective-permute-start | bytes 61448 | tf_op jit(solution)/shard_map/ppermute | solution.py:765
  65.2 3.8 %collective-permute-start.5 = (f32[40,128]{1,0:T(8,128)S(1)}, f32[40,128]{1,0:T(8,128)S(1)}, u32[]{:S(2)}, u32[]{:S(2)}) collective-permute-start(f32[40,128]{1,0:T(8,128)S(1)} %add.26), channel_id=1, source_target_pairs={{0,1},{1,0},{2,3},{3,2},{4,5},{5,4},{6,7},{7,6},{8,9},{9,8},{10,11... | collective-permute-start | bytes 61448 | tf_op jit(solution)/shard_map/ppermute | solution.py:765
  69.0 4.7 %collective-permute-start.6 = (f32[40,128]{1,0:T(8,128)S(1)}, f32[40,128]{1,0:T(8,128)S(1)}, u32[]{:S(2)}, u32[]{:S(2)}) collective-permute-start(f32[40,128]{1,0:T(8,128)S(1)} %add.27), channel_id=1, source_target_pairs={{0,2},{1,3},{2,0},{3,1},{4,6},{5,7},{6,4},{7,5},{8,10},{9,11},{10,... | collective-permute-start | bytes 61448 | tf_op jit(solution)/shard_map/ppermute | solution.py:765

commit v5 on v4

--- a/solution.py
+++ b/solution.py
@@ -233,9 +233,7 @@
     d3_hi, d3_lo = split(d3)
     dh2 = dot(out_back_ref[...], stack([d3_hi, d3_hi, d3_lo]))
     if acc is not None:
-        rows = d3.shape[0]
-        high = dot_nt(stack([d3_hi, d3_lo]), h2_pair[0])
-        acc[2][...] += high[:rows] + high[rows:] + dot_nt(d3_hi, h2_pair[1])
+        acc[2][...] += dot_nt(stack(list(h2_pair)), stack([d3_hi, d3_lo]))
         acc[3][...] += d3
     d2_hi, d2_lo = split(dh2 * (1.0 - h2 * h2))
     block = 2 * hid
@@ -250,7 +248,7 @@
             lefts.append(stack([h1_pair[0][at : at + hid], h1_pair[1][at : at + hid], ones]))
             rights.append(stack([d2_hi[at : at + hid], d2_lo[at : at + hid]]))
         acc[1][...] += dot_nt(side(lefts), side(rights))
-    return split(stack(parts) * (1.0 - h1 * h1))
+    return stack(parts) * (1.0 - h1 * h1)
 
 
 def first_backward(d1, back_ref):
@@ -260,12 +258,13 @@
 
 
 def add_first_grads(first, d1, acc_in):
-    ones = jnp.ones((ONES, d1[0].shape[1]), BF16)
-    rows = first[0].shape[0]
-    high = dot_nt(stack([first[0], ones, first[1]]), d1[0])
-    low = dot_nt(stack([first[0], ones]), d1[1])
-    acc_in[...] += high[: rows + ONES] + low
-    acc_in[:rows, :] += high[rows + ONES :]
+    high, low = first[:2]
+    both = stack(list(d1))
+    if 2 * high.shape[0] + ONES <= acc_in.shape[1]:
+        ones = jnp.ones((ONES, high.shape[1]), BF16)
+        acc_in[:, : 2 * high.shape[0] + ONES] += dot_nt(both, stack([high, low, ones]))
+    else:
+        acc_in[...] += dot_nt(both, stack([high, low]))
 
 
 def edge_states(cells, gates):
@@ -473,10 +472,13 @@
         d_left = [jnp.where(halo_mask, d, 0.0) for d in d_left]
         d_right = [jnp.where(halo_mask, d, 0.0) for d in d_right]
     d3_full, direct = edge_backward(cells, gates, d_left, d_right)
-    d1 = limiter_backward(d3_full, h1, h2, h1_pair, h2_pair, out_back, mid_back, acc, hid)
+    d1_full = limiter_backward(d3_full, h1, h2, h1_pair, h2_pair, out_back, mid_back, acc, hid)
+    d1 = split(d1_full)
     d_window = first_backward(d1, first_y_back)
     if acc is not None:
         add_first_grads(window, d1, acc[0])
+        ny = acc[4].shape[1]
+        acc[4][...] += sum(d1_full[:, at : at + ny] for at in range(0, d1_full.shape[1], ny))
     return [
         [d_window[FACES * (4 * s + c) : FACES * (4 * s + c + 1)] + direct[s][c] for c in range(4)]
         for s in range(4)
@@ -494,40 +496,17 @@
     return out
 
 
-def fold_faces(rows, hid, lanes):
-    fold = pick((rows.shape[1], lanes), lambda q, n: (rest(n - q, hid) == 0) & (n >= hid) & (n < 2 * hid), F32)
-    return exact(rows, fold)
-
-
-def fold_first_x(acc, hid, lanes):
-    r, c = rows_cols(acc.shape)
-    shift = jnp.where(r < 64, (r & 15) - quot(c, hid), -1)
-    parts = [
-        jnp.where((shift == s) | (r >= 64) & (s == 0), acc, 0.0)[: 64 + ONES if s == 0 else 64] for s in range(4)
-    ]
-    folded = fold_faces(stack(parts), hid, lanes)
-
-    def test(q, n):
-        at = jnp.where(n < 64, n, n - ONES)
-        return ((n < 64) | (n >= 64 + ONES)) & (q == (at >> 4)) | (n == 64) & (q == 16)
-
-    return exact(pick((24, folded.shape[0]), test, F32), folded)
-
-
-def fold_first_y(acc, hid, lanes):
-    r, c = rows_cols(acc.shape)
-    keep = ((r & 7) == quot(c, hid)) | (r >= 128)
-    sel = lambda q, n: ((n < 128) & (q == (n >> 3))) | ((n == 128) & (q == 16))
-    return exact(pick((24, acc.shape[0]), sel, F32), fold_faces(jnp.where(keep, acc, 0.0), hid, lanes))
-
-
-def back_kernel(odd, state, cot, middle, own, from_first, from_second,
+def fold_rows(values, hid):
+    return sum(values[at : at + hid] for at in range(0, values.shape[0], hid))
+
+
+def back_kernel(state, cot, middle, own, from_first, from_second,
                 first_x, first_y, first_bias, mid, mid_bias, out, out_bias,
                 out_back, mid_back, first_x_back, first_y_back,
                 h1_hi, h1_lo, h2_hi, h2_lo, gates_in,
                 g_den, g_mom, g_tra, g_weights,
                 rim_state, rim_cot, rim_flux, rim_middle, rim_grad, d_middle,
-                acc_x, acc_y, acc_mid, acc_out, acc_out_bias):
+                acc_x, acc_y, acc_y_bias, acc_mid, acc_out, acc_out_bias):
     nx, ny = state.shape[1:]
     groups = nx // FACES
     half = groups // PAIR
@@ -538,12 +517,12 @@
     rim_groups = rim_rows // FACES
     rim_half = rim_groups // RIM_PAIR
 
-    for acc in (acc_x, acc_y, acc_mid, acc_out, acc_out_bias):
+    for acc in (acc_x, acc_y, acc_y_bias, acc_mid, acc_out, acc_out_bias):
         acc[...] = jnp.zeros(acc.shape, F32)
 
     lane = lane_index(ny)
     spot = lane & (SEG - 1)
-    is_odd = jnp.full((FACES, ny), odd[0], jnp.int32) == 1
+    is_odd = jnp.full((FACES, ny), lax.rem(lax.axis_index(("tx", "ty")), 2), jnp.int32) == 1
     for v in range(8):
         for g in range(rim_groups):
             rows = pl.ds(g * FACES, FACES)
@@ -645,7 +624,7 @@
                 cots[1][c].append(turn(low, -1, 1))
         cells = [y_order([side(one) for one in row]) for row in cells]
         cots = [y_order([side(one) for one in row]) for row in cots]
-        parts = y_step(cells, cots, None, refs, (acc_y, acc_mid, acc_out, acc_out_bias), hid)
+        parts = y_step(cells, cots, None, refs, (acc_y, acc_mid, acc_out, acc_out_bias, acc_y_bias), hid)
         for k in range(PAIR):
             group = step + k * half
             rows = row_block(group)
@@ -684,9 +663,10 @@
         d_flux = [courant * (turn(d, -2, 0)[:FACES] - turn(d, -1, 0)[:FACES]) for d in d_tiles]
         d_left, d_right = face_flux_backward(left, right, d_flux)
         d3_full, direct = edge_backward(cells, gates, d_left, d_right)
-        d1 = limiter_backward(
+        d1_full = limiter_backward(
             d3_full, h1, h2, h1_pair, h2_pair, out_back, mid_back, (acc_x, acc_mid, acc_out, acc_out_bias), hid
         )
+        d1 = split(d1_full)
         d_window = first_backward(d1, first_x_back)
         add_first_grads(split(stack(tiles)), d1, acc_x)
         later = []
@@ -708,23 +688,39 @@
             grads[c][pl.ds(at, FACES), :] += last[c][:, k * ny : (k + 1) * ny]
 
     lanes = g_weights.shape[1]
-    grad_first = fold_first_x(acc_x[...], hid, lanes) + fold_first_y(acc_y[...], hid, lanes)
     both = acc_mid[...]
     grad_mid = both[:hid, :hid] + both[:hid, hid:] + both[hid : 2 * hid, :hid]
     grad_mid = exact_nt(
         pick((hid, hid), lambda q, n: q == n, F32), stack([grad_mid, jnp.zeros((lanes - hid, hid), F32)])
     )
     grad_mid_bias = both[2 * hid :, :hid] + both[2 * hid :, hid:]
-    r, c = rows_cols(acc_out.shape)
-    grad_out = exact(
-        pick((8, 64), lambda q, n: (n >> 3) == q, F32),
-        fold_faces(jnp.where((r & 7) == quot(c, hid), acc_out[...], 0.0), hid, lanes),
+    r, c = rows_cols(acc_x.shape)
+    face = rest(quot(r, hid), FACES)
+    values = acc_x[...]
+    found = [fold_rows(jnp.where((c & 15) - face == s, values, 0.0)[:, :128], hid) for s in range(4)]
+    found.append(fold_rows(values[:, 128:], hid))
+    found.append(fold_rows(jnp.where((c & 7) == face, acc_y[...], 0.0), hid))
+    found.append(fold_rows(acc_y_bias[...], hid))
+    found.append(fold_rows(jnp.where((c[:, :128] & 7) == face[:, :128], acc_out[...], 0.0), hid))
+    found = side(found)
+
+    def source(q, n):
+        block = n >> 7
+        in_x = (block < 4) & (q == 4 * block + ((n & 63) >> 4))
+        in_y = (block >= 5) & (block < 7) & (q == ((n & 127) >> 3))
+        in_bias = ((n == 512) | (block == 7)) & (q == 24)
+        in_out = (block == 8) & (q == 16 + ((n & 63) >> 3))
+        return in_x | in_y | in_bias | in_out
+
+    beside = exact_nt(
+        pick((32, found.shape[1]), source, F32),
+        stack([jnp.zeros((hid, found.shape[1]), F32), found, jnp.zeros((lanes - 2 * hid, found.shape[1]), F32)]),
     )
     out_bias_rows = exact_nt(jnp.ones((8, acc_out_bias.shape[1]), F32), acc_out_bias[...])
     grad_out_bias = exact_nt(out_bias_rows, pick((lanes, 64), lambda q, n: (n >> 3) == q - hid, F32))
     r, c = rows_cols((8, lanes))
-    biases = jnp.where(r == 0, grad_first[16:24], jnp.where(r == 1, grad_out_bias, 0.0))
-    g_weights[:hid, :] = grad_mid + stack([grad_first[:16], grad_out, biases])
+    g_weights[:hid, :] = grad_mid + beside
+    g_weights[25:26, :] += grad_out_bias[:1]
     g_weights[hid:, :] = jnp.zeros((8, lanes), F32)
     g_weights[hid:, :hid] = grad_mid_bias[:8]
 
@@ -761,8 +757,10 @@
         if size & (size - 1):
             values = lax.psum(values, axis)
             continue
-        for k in range(size.bit_length() - 1):
-            values = values + lax.ppermute(values, axis, [(i, i ^ (1 << k)) for i in range(size)])
+        parts = [values] + [lax.ppermute(values, axis, [(i, i ^ k) for i in range(size)]) for k in range(1, size)]
+        while len(parts) > 1:
+            parts = [parts[k] + parts[k + 1] for k in range(0, len(parts), 2)]
+        values = parts[0]
     return values
 
 
@@ -806,7 +804,6 @@
     axes = ("tx", "ty")
     swaps = [[(i, (i + 1 if (i + first) % 2 == 0 else i - 1) % ring) for i in range(ring)] for first in range(2)]
     from_first, from_second = (lax.ppermute(rim, axes, swap) for swap in swaps)
-    odd = (lax.axis_index(axes) % 2).astype(jnp.int32).reshape(1)
 
     middle, *kept = call(
         x_forward_kernel,
@@ -826,8 +823,7 @@
             shape(tracer.shape, F32),
             shape((hid + 8, 128), F32),
         ],
-        [odd, state, cots, middle, rim, from_first, from_second] + matrices + kept,
-        in_spaces=whole(1, pltpu.SMEM) + whole(6 + len(matrices) + len(kept)),
+        [state, cots, middle, rim, from_first, from_second] + matrices + kept,
         scratch=[
             pltpu.VMEM((4, rim_rows + FACES, ny), F32),
             pltpu.VMEM((4, rim_rows, ny), F32),
@@ -835,10 +831,11 @@
             pltpu.VMEM((4, rim_rows, ny), F32),
             pltpu.VMEM((4, rim_rows, ny), F32),
             pltpu.VMEM((4, nx, ny), F32),
-            pltpu.VMEM((64 + ONES, wide), F32),
-            pltpu.VMEM((128 + ONES, wide), F32),
+            pltpu.VMEM((2 * wide, 256), F32),
+            pltpu.VMEM((2 * wide, 256), F32),
+            pltpu.VMEM((wide, ny), F32),
             pltpu.VMEM((2 * hid + ONES, 2 * hid), F32),
-            pltpu.VMEM((64, wide), F32),
+            pltpu.VMEM((2 * wide, 128), F32),
             pltpu.VMEM((64, lanes), F32),
         ],
         flops=4 * 10**10,

time: 74.7 us -> 58.8 us (0.79)
  local copies, waits for them, and re-layouts: 14 us -> 0 us
  waiting for transfers between devices: 12.4 us -> 8.62 us
  starting transfers between devices: 10.9 us -> 13.1 us
    unnamed x20 -> x0, local copies, waits for them, and re-layouts: 14 us -> none
    ppermute x5 -> x7, waiting for transfers between devices: 12.4 us -> 7.69 us  [sum_all(): lax.ppermute(values, axis, [(i, i ^ k) for i in range(size)])]
    ppermute x5 -> x7, starting transfers between devices: 4.83 us -> 6.99 us  [sum_all(): lax.ppermute(values, axis, [(i, i ^ k) for i in range(size)])]
    ppermute x2, waiting for transfers between devices: 0.01 us -> 0.93 us  [body(): from_first, from_second = (lax.ppermute(rim, axes, swap) for swap in swaps)]
  transfers between devices with their start and end apart: 7 -> 9, of which waited for: 5 -> 7; matrix products, arithmetic and copies ran while one was open for 0% -> 0% of each run, Pallas kernels for 7% -> 9%
where the time goes in v5:
time: 58.8 us; the launch traced here: 58.6 us
  Pallas kernels  36.2 us (62%)
  starting transfers between devices  13.1 us (22%)
  waiting for transfers between devices  8.62 us (15%)
  between operations  0.68 us (1%)
    pallas_call x4, Pallas kernels, call(): pl.pallas_call(kernel, out_shape=outs, in_specs=in_spaces or whole(len(op...  36.2 us
    ppermute x7, waiting for transfers between devices, sum_all(): lax.ppermute(values, axis, [(i, i ^ k) for i in range(size)])  7.69 us
    ppermute x7, starting transfers between devices, sum_all(): lax.ppermute(values, axis, [(i, i ^ k) for i in range(size)])  6.99 us
    ppermute x2, starting transfers between devices, body(): from_first, from_second = (lax.ppermute(rim, axes, swap) for swap in swaps)  6.07 us
  transfers between devices with their start and end apart: 9, of which 7 were waited for; matrix products, arithmetic and copies ran while one was open for 0% of the time, Pallas kernels for 9%

profile of v5, /device:TPU:0, one launch (start us, length us, event | category | flops | bytes accessed | tf_op | source)
XLA Modules:
  0.0 58.6 jit_solution(16814424201756767265)
XLA Ops:
  0.6 3.8 %shard_map.169 = (f32[8,32,128]{2,1,0:T(8,128)S(1)}, f32[4,256,128]{2,1,0:T(8,128)S(1)}, f32[4,256,128]{2,1,0:T(8,128)S(1)}, bf16[256,400]{1,0:T(8,128)(2,1)S(1)...) custom-call(f32[1,256,128]{2,1,0:T(8,128)} %den.1, ...), custom_call_target="tpu_custom_call" | custom-call | tf_op jit(solution)/shard_map/pallas_call | solution.py:744
  4.4 6.1 %collective-permute-start.1 = (f32[8,32,128]{2,1,0:T(8,128)S(1)}, f32[8,32,128]{2,1,0:T(8,128)S(1)}, u32[]{:S(2)}, u32[]{:S(2)}) collective-permute-start(f32[8,32,128]{2,1,0:T(8,128)S(1)} %get-tuple-element.47.own), channel_id=1, source_target_pairs={{0,7},{1,2},{2,1},{3,4},{4,3},{5,6},{6,5},{7,0},{8,15},{9,10},{10,... | collective-permute-start | bytes 393224 | tf_op jit(solution)/shard_map/ppermute | solution.py:806
  10.5 0.0 collective-permute-start
  10.5 5.4 %shard_map.170 = (f32[4,256,128]{2,1,0:T(8,128)S(1)}, bf16[4,256,1024]{2,1,0:T(8,128)(2,1)S(1)}, bf16[4,256,1024]{2,1,0:T(8,128)(2,1)S(1)}, bf16[4,256,1024]{2,1...) custom-call(f32[4,256,128]{2,1,0:T(8,128)S(1)} %get-tuple-element.39.state, ...), custom_call_target="tpu_custom_call" | custom-call | flops 10000000000 | bytes 10000000 | tf_op jit(solution)/shard_map/pallas_call | solution.py:744
  15.9 0.0 collective-permute-done.1.from_second
  15.9 0.9 %collective-permute-done.from_first = f32[8,32,128]{2,1,0:T(8,128)S(1)} collective-permute-done((f32[8,32,128]{2,1,0:T(8,128)S(1)}, f32[8,32,128]{2,1,0:T(8,128)S(1)}, u32[]{:S(2)}, u32[]{:S(2)}) %collective-permute-start) | collective-permute-done | bytes 131104 | tf_op jit(solution)/shard_map/ppermute | solution.py:806
  16.9 26.3 %shard_map.171 = (f32[1,256,128]{2,1,0:T(8,128)}, f32[1,2,256,128]{3,2,1,0:T(8,128)}, f32[1,256,128]{2,1,0:T(8,128)}, f32[40,128]{1,0:T(8,128)S(1)}) custom-call(f32[4,256,128]{2,1,0:T(8,128)S(1)} %get-tuple-element.39.state, f32[4,256,128]{2,1,0:T(8,128)S(1)} %get-tuple-element.40.cot, f32[4,256,128]{2,1,0:T(8,128)S(1)} %get-tuple-element.46.middle, ...), custom_call_target="tpu_custom_call" | custom-call | flops 40000000000 | bytes 20000000 | tf_op jit(solution)/shard_map/pallas_call | solution.py:744
  43.2 0.6 %collective-permute-start.4 = (f32[40,128]{1,0:T(8,128)S(1)}, f32[40,128]{1,0:T(8,128)S(1)}, u32[]{:S(2)}, u32[]{:S(2)}) collective-permute-start(f32[40,128]{1,0:T(8,128)S(1)} %get-tuple-element.62), channel_id=1, source_target_pairs={{0,24},{8,16},{16,8},{24,0},{1,25},{9,17},{17,9},{25,1},{2,26},{10... | collective-permute-start | bytes 61448 | tf_op jit(solution)/shard_map/ppermute | solution.py:760
  43.8 0.9 %collective-permute-start.3 = (f32[40,128]{1,0:T(8,128)S(1)}, f32[40,128]{1,0:T(8,128)S(1)}, u32[]{:S(2)}, u32[]{:S(2)}) collective-permute-start(f32[40,128]{1,0:T(8,128)S(1)} %get-tuple-element.62), channel_id=1, source_target_pairs={{0,16},{8,24},{16,0},{24,8},{1,17},{9,25},{17,1},{25,9},{2,18},{10... | collective-permute-start | bytes 61448 | tf_op jit(solution)/shard_map/ppermute | solution.py:760
  44.7 0.4 collective-permute-start.2
  45.0 1.6 %collective-permute-done.4 = f32[40,128]{1,0:T(8,128)S(1)} collective-permute-done((f32[40,128]{1,0:T(8,128)S(1)}, f32[40,128]{1,0:T(8,128)S(1)}, u32[]{:S(2)}, u32[]{:S(2)}) %collective-permute-start.4) | collective-permute-done | bytes 20512 | tf_op jit(solution)/shard_map/ppermute | solution.py:760
  46.6 1.2 %collective-permute-done.3 = f32[40,128]{1,0:T(8,128)S(1)} collective-permute-done((f32[40,128]{1,0:T(8,128)S(1)}, f32[40,128]{1,0:T(8,128)S(1)}, u32[]{:S(2)}, u32[]{:S(2)}) %collective-permute-start.3) | collective-permute-done | bytes 20512 | tf_op jit(solution)/shard_map/ppermute | solution.py:760
  47.8 0.0 collective-permute-done.2
  47.8 0.7 %collective-permute-start.5 = (f32[40,128]{1,0:T(8,128)S(1)}, f32[40,128]{1,0:T(8,128)S(1)}, u32[]{:S(2)}, u32[]{:S(2)}) collective-permute-start(f32[40,128]{1,0:T(8,128)S(1)} %add_add_fusion.1), channel_id=1, source_target_pairs={{0,4},{4,0},{1,5},{5,1},{2,6},{6,2},{3,7},{7,3},{8,12},{12,8},{9,1... | collective-permute-start | bytes 61448 | tf_op jit(solution)/shard_map/ppermute | solution.py:760
  48.5 3.1 %collective-permute-done.5 = f32[40,128]{1,0:T(8,128)S(1)} collective-permute-done((f32[40,128]{1,0:T(8,128)S(1)}, f32[40,128]{1,0:T(8,128)S(1)}, u32[]{:S(2)}, u32[]{:S(2)}) %collective-permute-start.5) | collective-permute-done | bytes 20512 | tf_op jit(solution)/shard_map/ppermute | solution.py:760
  51.6 1.0 %collective-permute-start.8 = (f32[40,128]{1,0:T(8,128)S(1)}, f32[40,128]{1,0:T(8,128)S(1)}, u32[]{:S(2)}, u32[]{:S(2)}) collective-permute-start(f32[40,128]{1,0:T(8,128)S(1)} %add.24), channel_id=1, source_target_pairs={{0,3},{1,2},{2,1},{3,0},{4,7},{5,6},{6,5},{7,4},{8,11},{9,10},{10,... | collective-permute-start | bytes 61448 | tf_op jit(solution)/shard_map/ppermute | solution.py:760
  52.6 1.4 %collective-permute-start.7 = (f32[40,128]{1,0:T(8,128)S(1)}, f32[40,128]{1,0:T(8,128)S(1)}, u32[]{:S(2)}, u32[]{:S(2)}) collective-permute-start(f32[40,128]{1,0:T(8,128)S(1)} %add.24), channel_id=1, source_target_pairs={{0,2},{1,3},{2,0},{3,1},{4,6},{5,7},{6,4},{7,5},{8,10},{9,11},{10,... | collective-permute-start | bytes 61448 | tf_op jit(solution)/shard_map/ppermute | solution.py:760
  54.1 1.9 %collective-permute-start.6 = (f32[40,128]{1,0:T(8,128)S(1)}, f32[40,128]{1,0:T(8,128)S(1)}, u32[]{:S(2)}, u32[]{:S(2)}) collective-permute-start(f32[40,128]{1,0:T(8,128)S(1)} %add.24), channel_id=1, source_target_pairs={{0,1},{1,0},{2,3},{3,2},{4,5},{5,4},{6,7},{7,6},{8,9},{9,8},{10,11... | collective-permute-start | bytes 61448 | tf_op jit(solution)/shard_map/ppermute | solution.py:760
  56.0 1.2 %collective-permute-done.8 = f32[40,128]{1,0:T(8,128)S(1)} collective-permute-done((f32[40,128]{1,0:T(8,128)S(1)}, f32[40,128]{1,0:T(8,128)S(1)}, u32[]{:S(2)}, u32[]{:S(2)}) %collective-permute-start.8) | collective-permute-done | bytes 20512 | tf_op jit(solution)/shard_map/ppermute | solution.py:760
  57.2 0.4 collective-permute-done.7
  57.7 0.2 collective-permute-done.6
  57.9 0.7 %shard_map.172 = (f32[16,32]{1,0:T(8,128)}, f32[1,32]{1,0:T(1,128)}, f32[32,32]{1,0:T(8,128)}, f32[1,32]{1,0:T(1,128)}, f32[8,32]{1,0:T(8,128)}, /*index=5*/f32[1,8]{1,0:T(1,128)}) custom-call(f32[40,128]{1,0:T(8,128)S(1)} %add_add_fusion.total), custom_call_target="tpu_custom_call" | custom-call | tf_op jit(solution)/shard_map/pallas_call | solution.py:744
  (3 shorter events, 0.0 us)
Async XLA Ops:
  4.4 11.5 %collective-permute-start.1 = (f32[8,32,128]{2,1,0:T(8,128)S(1)}, f32[8,32,128]{2,1,0:T(8,128)S(1)}, u32[]{:S(2)}, u32[]{:S(2)}) collective-permute-start(f32[8,32,128]{2,1,0:T(8,128)S(1)} %get-tuple-element.47.own), channel_id=1, source_target_pairs={{0,7},{1,2},{2,1},{3,4},{4,3},{5,6},{6,5},{7,0},{8,15},{9,10},{10,... | collective-permute-start | bytes 393224 | tf_op jit(solution)/shard_map/ppermute | solution.py:806
  10.5 6.3 %collective-permute-start = (f32[8,32,128]{2,1,0:T(8,128)S(1)}, f32[8,32,128]{2,1,0:T(8,128)S(1)}, u32[]{:S(2)}, u32[]{:S(2)}) collective-permute-start(f32[8,32,128]{2,1,0:T(8,128)S(1)} %get-tuple-element.47.own), channel_id=1, source_target_pairs={{0,1},{1,0},{2,3},{3,2},{4,5},{5,4},{6,7},{7,6},{8,9},{9,8},{10,11... | collective-permute-start | bytes 393224 | tf_op jit(solution)/shard_map/ppermute | solution.py:806
  43.2 3.4 %collective-permute-start.4 = (f32[40,128]{1,0:T(8,128)S(1)}, f32[40,128]{1,0:T(8,128)S(1)}, u32[]{:S(2)}, u32[]{:S(2)}) collective-permute-start(f32[40,128]{1,0:T(8,128)S(1)} %get-tuple-element.62), channel_id=1, source_target_pairs={{0,24},{8,16},{16,8},{24,0},{1,25},{9,17},{17,9},{25,1},{2,26},{10... | collective-permute-start | bytes 61448 | tf_op jit(solution)/shard_map/ppermute | solution.py:760
  43.8 4.0 %collective-permute-start.3 = (f32[40,128]{1,0:T(8,128)S(1)}, f32[40,128]{1,0:T(8,128)S(1)}, u32[]{:S(2)}, u32[]{:S(2)}) collective-permute-start(f32[40,128]{1,0:T(8,128)S(1)} %get-tuple-element.62), channel_id=1, source_target_pairs={{0,16},{8,24},{16,0},{24,8},{1,17},{9,25},{17,1},{25,9},{2,18},{10... | collective-permute-start | bytes 61448 | tf_op jit(solution)/shard_map/ppermute | solution.py:760
  44.7 3.1 %collective-permute-start.2 = (f32[40,128]{1,0:T(8,128)S(1)}, f32[40,128]{1,0:T(8,128)S(1)}, u32[]{:S(2)}, u32[]{:S(2)}) collective-permute-start(f32[40,128]{1,0:T(8,128)S(1)} %get-tuple-element.62), channel_id=1, source_target_pairs={{0,8},{8,0},{16,24},{24,16},{1,9},{9,1},{17,25},{25,17},{2,10},{10... | collective-permute-start | bytes 61448 | tf_op jit(solution)/shard_map/ppermute | solution.py:760
  47.8 3.8 %collective-permute-start.5 = (f32[40,128]{1,0:T(8,128)S(1)}, f32[40,128]{1,0:T(8,128)S(1)}, u32[]{:S(2)}, u32[]{:S(2)}) collective-permute-start(f32[40,128]{1,0:T(8,128)S(1)} %add_add_fusion.1), channel_id=1, source_target_pairs={{0,4},{4,0},{1,5},{5,1},{2,6},{6,2},{3,7},{7,3},{8,12},{12,8},{9,1... | collective-permute-start | bytes 61448 | tf_op jit(solution)/shard_map/ppermute | solution.py:760
  51.6 5.6 %collective-permute-start.8 = (f32[40,128]{1,0:T(8,128)S(1)}, f32[40,128]{1,0:T(8,128)S(1)}, u32[]{:S(2)}, u32[]{:S(2)}) collective-permute-start(f32[40,128]{1,0:T(8,128)S(1)} %add.24), channel_id=1, source_target_pairs={{0,3},{1,2},{2,1},{3,0},{4,7},{5,6},{6,5},{7,4},{8,11},{9,10},{10,... | collective-permute-start | bytes 61448 | tf_op jit(solution)/shard_map/ppermute | solution.py:760
  52.6 5.0 %collective-permute-start.7 = (f32[40,128]{1,0:T(8,128)S(1)}, f32[40,128]{1,0:T(8,128)S(1)}, u32[]{:S(2)}, u32[]{:S(2)}) collective-permute-start(f32[40,128]{1,0:T(8,128)S(1)} %add.24), channel_id=1, source_target_pairs={{0,2},{1,3},{2,0},{3,1},{4,6},{5,7},{6,4},{7,5},{8,10},{9,11},{10,... | collective-permute-start | bytes 61448 | tf_op jit(solution)/shard_map/ppermute | solution.py:760
  54.1 3.8 %collective-permute-start.6 = (f32[40,128]{1,0:T(8,128)S(1)}, f32[40,128]{1,0:T(8,128)S(1)}, u32[]{:S(2)}, u32[]{:S(2)}) collective-permute-start(f32[40,128]{1,0:T(8,128)S(1)} %add.24), channel_id=1, source_target_pairs={{0,1},{1,0},{2,3},{3,2},{4,5},{5,4},{6,7},{7,6},{8,9},{9,8},{10,11... | collective-permute-start | bytes 61448 | tf_op jit(solution)/shard_map/ppermute | solution.py:760

commit v6 on v5

--- a/solution.py
+++ b/solution.py
@@ -97,32 +97,32 @@
 
 
 def build_first(w, b, hid):
-    x_cols, y_cols, step = 6 * 64 + ONES, 6 * 128, 512
+    x_cols, y_cols, step = 6 * 32 + ONES, 6 * 128, 256
 
     def source(q, n):
-        s = n >> 9
+        s = n >> 8
         m = n & (step - 1)
-        in_x = (s < 4) & (m < 384) & (q == 4 * s + ((m >> 4) & 3))
+        in_x = (s < 4) & (m < 192) & (q == 4 * s + ((m & 31) >> 3))
         in_y = (n >= 4 * step) & (q == (((n - 4 * step) & 127) >> 3))
         return in_x | in_y
 
     spread_out = exact(w, pick((16, 4 * step + y_cols), source, F32))
     _, n = rows_cols(spread_out.shape)
-    block = jnp.where(n < 4 * step, (n & (step - 1)) >> 6, (n - 4 * step) >> 7)
+    block = jnp.where(n < 4 * step, (n & (step - 1)) >> 5, (n - 4 * step) >> 7)
     spread_out = choose(spread_out, level_of(block))
 
     at, _ = rows_cols((x_cols, hid))
     rows = jnp.zeros((x_cols, hid), F32)
     for k, level in enumerate(split3(b)):
-        rows = jnp.where(at == 384 + k, jnp.broadcast_to(level.astype(F32), (x_cols, hid)), rows)
+        rows = jnp.where(at == 192 + k, jnp.broadcast_to(level.astype(F32), (x_cols, hid)), rows)
     bias = dot_nt(pick((hid, hid), lambda q, n: q == n), rows.astype(BF16))
 
-    r, c = rows_cols((FACES * hid, x_cols))
-    shift = jnp.where(c < 384, (c & 15) - quot(r, hid), -1)
-    first_x = stack([bias] * FACES)
+    r, c = rows_cols((FACES // 2 * hid, x_cols))
+    shift = jnp.where(c < 192, (c & 7) - quot(r, hid), -1)
+    first_x = stack([bias] * (FACES // 2))
     for s in range(4):
         part = spread_out[:, s * step : s * step + x_cols]
-        first_x = jnp.where(shift == s, stack([part] * FACES), first_x)
+        first_x = jnp.where(shift == s, stack([part] * (FACES // 2)), first_x)
     r, c = rows_cols((FACES * hid, y_cols))
     first_y = jnp.where((c & 7) == quot(r, hid), stack([spread_out[:, 4 * step :]] * FACES), 0.0)
     return first_x.astype(BF16), first_y.astype(BF16)
@@ -132,24 +132,19 @@
     wide = FACES * hid
 
     def source(q, n):
-        in_x = (q < 512) & (n == 4 * (q >> 7) + ((q & 63) >> 4))
-        in_y = (q >= 512) & (n == (((q - 512) & 127) >> 3))
+        in_x = (q < 256) & (n == 4 * (q >> 6) + ((q & 63) >> 4))
+        in_y = (q >= 256) & (n == ((q - 256) >> 3))
         return in_x | in_y
 
-    rows = exact(pick((512 + 256, 16), source, F32), w_t)
-    right = pick((hid, 2 * wide), lambda q, n: rest(n, hid) == q)
-    high, low = (dot(part, right) for part in split(rows))
-    r, c = rows_cols(high.shape)
-    is_low = jnp.where(r < 512, r & 64, (r - 512) & 128) > 0
-    value = jnp.where(is_low, jnp.where(c < wide, low, 0.0), high)
-    face = quot(rest(c, wide), hid)
-    r, c = r[:128], c[:128]
-    shift = (r & 15) - face[:128]
-    back_x = jnp.zeros((128, 2 * wide), F32)
+    rows = exact(pick((256 + 128, 16), source, F32), w_t).astype(BF16)
+    value = dot(rows, pick((hid, wide), lambda q, n: rest(n, hid) == q))
+    r, c = rows_cols((64, wide))
+    shift = (r & 15) - quot(c, hid)
+    back_x = jnp.zeros((64, wide), F32)
     for s in range(4):
-        back_x = jnp.where(shift == s, value[128 * s : 128 * (s + 1)], back_x)
-    r, _ = rows_cols((256, 2 * wide))
-    back_y = jnp.where((r & 7) == face[512:], value[512:], 0.0)
+        back_x = jnp.where(shift == s, value[64 * s : 64 * (s + 1)], back_x)
+    r, c = rows_cols((128, wide))
+    back_y = jnp.where((r & 7) == quot(c, hid), value[256:], 0.0)
     return back_x.astype(BF16), back_y.astype(BF16)
 
 
@@ -205,11 +200,12 @@
 
 def limiter_forward(first, weights, hid):
     first_ref, first_bias_ref, mid_ref, mid_bias_ref, out_ref, out_bias_ref = weights
-    width = first[0].shape[1]
+    width = first[0][0].shape[1]
     if first_bias_ref is None:
-        h1 = jnp.tanh(dot(first_ref[...], stack(stacked(first) + [jnp.ones((ONES, width), BF16)])))
+        ones = [jnp.ones((ONES, width), BF16)]
+        h1 = stack([jnp.tanh(dot(first_ref[...], stack(stacked(one) + ones))) for one in first])
     else:
-        h1 = jnp.tanh(dot(first_ref[...], stack(stacked(first))) + spread(first_bias_ref, width))
+        h1 = jnp.tanh(dot(first_ref[...], stack(stacked(first[0]))) + spread(first_bias_ref, width))
     h1_parts = split3(h1)
     block = 2 * hid
     parts = []
@@ -244,17 +240,11 @@
     if acc is not None:
         ones = jnp.ones((ONES, d3.shape[1]), BF16)
         lefts, rights = [], []
-        for at in range(0, FACES * hid, hid):
-            lefts.append(stack([h1_pair[0][at : at + hid], h1_pair[1][at : at + hid], ones]))
-            rights.append(stack([d2_hi[at : at + hid], d2_lo[at : at + hid]]))
+        for at in range(0, FACES * hid, 2 * block):
+            lefts.append(stack([part[at : at + 2 * block] for part in h1_pair] + [ones]))
+            rights.append(stack([part[at : at + 2 * block] for part in (d2_hi, d2_lo)]))
         acc[1][...] += dot_nt(side(lefts), side(rights))
     return stack(parts) * (1.0 - h1 * h1)
-
-
-def first_backward(d1, back_ref):
-    both = dot(back_ref[...], stack([d1[0], d1[1]]))
-    half = both.shape[0] // 2
-    return both[:half] + both[half:]
 
 
 def add_first_grads(first, d1, acc_in):
@@ -343,7 +333,7 @@
 
 
 def pack_kernel(den, mom, tra, cot, w_in, b_in, w_mid, b_mid, w_out, b_out,
-                rim, state, cots, first_x, first_y, first_bias, mid, mid_bias, out, out_bias,
+                rim, to_first, to_second, state, cots, first_x, first_y, first_bias, mid, mid_bias, out, out_bias,
                 out_back, mid_back, first_x_back, first_y_back, *scratch):
     *small, sems = scratch
     nx, ny = den.shape[1:]
@@ -393,6 +383,22 @@
                 moved = turn(plane[pl.ds(s * rows + at, FACES), :], first + RIM, 1)
                 total = jnp.where((lane >= first) & (lane < first + 2 * RIM), moved, total)
             rim[v, pl.ds(at, FACES), :] = total
+    is_odd = odd_mask(ny)
+    spot = lane & (SEG - 1)
+    for v in range(8):
+        sides = []
+        for first in (2 * RIM, RIM):
+            total = jnp.zeros((FACES, ny), F32)
+            for g in range(rows // FACES):
+                moved = turn(rim[v, pl.ds(g * FACES, FACES), :], g * RIM - first, 1)
+                total = jnp.where((spot >= g * RIM) & (spot < (g + 1) * RIM), moved, total)
+            sides.append(total)
+        to_first[v] = jnp.where(is_odd, sides[0], sides[1])
+        to_second[v] = jnp.where(is_odd, sides[1], sides[0])
+
+
+def odd_mask(ny):
+    return jnp.full((FACES, ny), lax.rem(lax.axis_index(("tx", "ty")), 2), jnp.int32) == 1
 
 
 def row_block(at):
@@ -409,8 +415,13 @@
     return [side([one[c] for one in sets]) for c in range(len(planes))]
 
 
+def x_windows(tiles):
+    half = FACES // 2
+    return [split3(stack([turn(tile, -at, 0)[:FACES] for tile in tiles])) for at in (0, half)]
+
+
 def x_forward(tiles, weights, hid):
-    h1, h1_pair, h2, h2_pair, gates = limiter_forward(split3(stack(tiles)), weights, hid)
+    h1, h1_pair, h2, h2_pair, gates = limiter_forward(x_windows(tiles), weights, hid)
     cells = x_cells(tiles)
     return h1_pair, h2_pair, gates, face_flux(*edge_states(cells, gates))
 
@@ -464,7 +475,7 @@
 def y_step(cells, cots, halo_mask, refs, acc, hid):
     weights, out_back, mid_back, first_y_back = refs
     window = split3(stack([cells[s][c] for s in range(4) for c in range(4)]))
-    h1, h1_pair, h2, h2_pair, gates = limiter_forward(window, weights, hid)
+    h1, h1_pair, h2, h2_pair, gates = limiter_forward([window], weights, hid)
     left, right = edge_states(cells, gates)
     d_flux = [courant * (cots[1][c] - cots[0][c]) for c in range(4)]
     d_left, d_right = face_flux_backward(left, right, d_flux)
@@ -474,7 +485,7 @@
     d3_full, direct = edge_backward(cells, gates, d_left, d_right)
     d1_full = limiter_backward(d3_full, h1, h2, h1_pair, h2_pair, out_back, mid_back, acc, hid)
     d1 = split(d1_full)
-    d_window = first_backward(d1, first_y_back)
+    d_window = dot(first_y_back[...], d1[0])
     if acc is not None:
         add_first_grads(window, d1, acc[0])
         ny = acc[4].shape[1]
@@ -522,19 +533,19 @@
 
     lane = lane_index(ny)
     spot = lane & (SEG - 1)
-    is_odd = jnp.full((FACES, ny), lax.rem(lax.axis_index(("tx", "ty")), 2), jnp.int32) == 1
+    is_odd = odd_mask(ny)
     for v in range(8):
         for g in range(rim_groups):
             rows = pl.ds(g * FACES, FACES)
-            mine, first, second = own[v, rows, :], from_first[v, rows, :], from_second[v, rows, :]
+            mine, first, second = own[v, rows, :], from_first[v], from_second[v]
             left, right = jnp.where(is_odd, first, second), jnp.where(is_odd, second, first)
             value = jnp.where(
                 spot < RIM,
-                turn(left, -RIM, 1),
+                turn(left, -g * RIM, 1),
                 jnp.where(
                     spot < 2 * RIM,
                     turn(mine, -RIM, 1),
-                    jnp.where(spot < 3 * RIM, turn(mine, RIM, 1), turn(right, RIM, 1)),
+                    jnp.where(spot < 3 * RIM, turn(mine, RIM, 1), turn(right, (3 - g) * RIM, 1)),
                 ),
             )
             if v < 4:
@@ -667,7 +678,7 @@
             d3_full, h1, h2, h1_pair, h2_pair, out_back, mid_back, (acc_x, acc_mid, acc_out, acc_out_bias), hid
         )
         d1 = split(d1_full)
-        d_window = first_backward(d1, first_x_back)
+        d_window = dot(first_x_back[...], d1[0])
         add_first_grads(split(stack(tiles)), d1, acc_x)
         later = []
         for c in range(4):
@@ -688,12 +699,17 @@
             grads[c][pl.ds(at, FACES), :] += last[c][:, k * ny : (k + 1) * ny]
 
     lanes = g_weights.shape[1]
-    both = acc_mid[...]
-    grad_mid = both[:hid, :hid] + both[:hid, hid:] + both[hid : 2 * hid, :hid]
+    values = acc_mid[: 8 * hid, :]
+    r, c = rows_cols(values.shape)
+    same = rest(quot(r, hid), 4) == rest(quot(c, hid), 4)
+    values = fold_rows(jnp.where(same, values, 0.0), hid)
     grad_mid = exact_nt(
-        pick((hid, hid), lambda q, n: q == n, F32), stack([grad_mid, jnp.zeros((lanes - hid, hid), F32)])
-    )
-    grad_mid_bias = both[2 * hid :, :hid] + both[2 * hid :, hid:]
+        pick((hid, 8 * hid), lambda q, n: rest(n, hid) == q, F32),
+        stack([values, jnp.zeros((lanes - hid, 8 * hid), F32)]),
+    )
+    grad_mid_bias = exact(
+        acc_mid[8 * hid : 8 * hid + 8, :], pick((8 * hid, lanes), lambda q, n: rest(q, hid) == n, F32)
+    )
     r, c = rows_cols(acc_x.shape)
     face = rest(quot(r, hid), FACES)
     values = acc_x[...]
@@ -721,8 +737,7 @@
     r, c = rows_cols((8, lanes))
     g_weights[:hid, :] = grad_mid + beside
     g_weights[25:26, :] += grad_out_bias[:1]
-    g_weights[hid:, :] = jnp.zeros((8, lanes), F32)
-    g_weights[hid:, :hid] = grad_mid_bias[:8]
+    g_weights[hid:, :] = grad_mid_bias
 
 
 def finish_kernel(total, g_w_in, g_b_in, g_w_mid, g_b_mid, g_w_out, g_b_out):
@@ -753,11 +768,22 @@
 
 
 def sum_all(values, sizes):
-    for axis, size in sizes.items():
-        if size & (size - 1):
-            values = lax.psum(values, axis)
-            continue
-        parts = [values] + [lax.ppermute(values, axis, [(i, i ^ k) for i in range(size)]) for k in range(1, size)]
+    axes, size = tuple(sizes), 1
+    for one in sizes.values():
+        size *= one
+    if size & (size - 1):
+        return lax.psum(values, axes)
+    bits = [1 << k for k in range(size.bit_length() - 1)]
+    core = size // sizes["traj"]
+    others = [bit for bit in reversed(bits) if bit != core]
+    rounds = [[core]] * (core in bits) + [others[k : k + 2] for k in range(0, len(others), 2)]
+    for masks in rounds:
+        partners = [0]
+        for mask in masks:
+            partners = partners + [one ^ mask for one in partners]
+        parts = [
+            lax.ppermute(values, axes, [(i, i ^ one) for i in range(size)]) if one else values for one in partners
+        ]
         while len(parts) > 1:
             parts = [parts[k] + parts[k + 1] for k in range(0, len(parts), 2)]
         values = parts[0]
@@ -779,13 +805,15 @@
     operands = [
         density, momentum, tracer, cotangent, w_in.T, b_in[None], w_mid, b_mid[None], w_out, b_out[None]
     ]
-    rim, state, cots, *matrices = call(
+    rim, to_first, to_second, state, cots, *matrices = call(
         pack_kernel,
         [
             shape((8, rim_rows, ny), F32),
+            shape((8, FACES, ny), F32),
+            shape((8, FACES, ny), F32),
             shape((4, nx, ny), F32),
             shape((4, nx, ny), F32),
-            shape((wide, 6 * 64 + ONES), BF16),
+            shape((wide // 2, 6 * 32 + ONES), BF16),
             shape((wide, 6 * 128), BF16),
             shape((wide, ny), F32),
             shape((4 * hid, 8 * hid), BF16),
@@ -794,8 +822,8 @@
             shape((64, ny), F32),
             shape((wide, 192), BF16),
             shape((2 * hid, 6 * hid), BF16),
-            shape((128, 2 * wide), BF16),
-            shape((256, 2 * wide), BF16),
+            shape((64, wide), BF16),
+            shape((128, wide), BF16),
         ],
         [pltpu.with_memory_space_constraint(one, pltpu.HBM) for one in operands],
         in_spaces=whole(10, pltpu.HBM),
@@ -803,7 +831,9 @@
     )
     axes = ("tx", "ty")
     swaps = [[(i, (i + 1 if (i + first) % 2 == 0 else i - 1) % ring) for i in range(ring)] for first in range(2)]
-    from_first, from_second = (lax.ppermute(rim, axes, swap) for swap in swaps)
+    from_first, from_second = (
+        lax.ppermute(one, axes, swap) for one, swap in zip((to_first, to_second), swaps)
+    )
 
     middle, *kept = call(
         x_forward_kernel,
@@ -834,7 +864,7 @@
             pltpu.VMEM((2 * wide, 256), F32),
             pltpu.VMEM((2 * wide, 256), F32),
             pltpu.VMEM((wide, ny), F32),
-            pltpu.VMEM((2 * hid + ONES, 2 * hid), F32),
+            pltpu.VMEM((8 * hid + ONES, 8 * hid), F32),
             pltpu.VMEM((2 * wide, 128), F32),
             pltpu.VMEM((64, lanes), F32),
         ],

time: 58.8 us -> 55.7 us (0.947)
  waiting for transfers between devices: 8.62 us -> 6.19 us
  Pallas kernels: 36.2 us -> 34.1 us
  starting transfers between devices: 13.1 us -> 14.5 us
    ppermute x9, waiting for transfers between devices: 8.62 us -> 6.19 us  [the longest x7 6.18 us: sum_all(): lax.ppermute(values, axes, [(i, i ^ one) for i in range(size)])]
    pallas_call x4, Pallas kernels: 36.2 us -> 34.1 us  [call(): pl.pallas_call(kernel, out_shape=outs, in_specs=in_spaces or whole(len(op...]
    ppermute x9, starting transfers between devices: 13.1 us -> 14.5 us  [the longest x7 7.94 us: sum_all(): lax.ppermute(values, axes, [(i, i ^ one) for i in range(size)])]
  transfers between devices with their start and end apart: 9 -> 9, of which waited for: 7 -> 6; matrix products, arithmetic and copies ran while one was open for 0% -> 0% of each run, Pallas kernels for 9% -> 9%
where the time goes in v6:
time: 55.7 us; the launch traced here: 55.5 us
  Pallas kernels  34.1 us (61%)
  starting transfers between devices  14.5 us (26%)
  waiting for transfers between devices  6.19 us (11%)
  between operations  0.69 us (1%)
    pallas_call x4, Pallas kernels, call(): pl.pallas_call(kernel, out_shape=outs, in_specs=in_spaces or whole(len(op...  34.1 us
    ppermute x7, starting transfers between devices, sum_all(): lax.ppermute(values, axes, [(i, i ^ one) for i in range(size)])  7.94 us
    ppermute x2, starting transfers between devices, body(): lax.ppermute(one, axes, swap)  6.52 us
    ppermute x7, waiting for transfers between devices, sum_all(): lax.ppermute(values, axes, [(i, i ^ one) for i in range(size)])  6.18 us
  transfers between devices with their start and end apart: 9, of which 6 were waited for; matrix products, arithmetic and copies ran while one was open for 0% of the time, Pallas kernels for 9%

profile of v6, /device:TPU:0, one launch (start us, length us, event | category | flops | bytes accessed | tf_op | source)
XLA Modules:
  0.0 55.5 jit_solution(15099985641934902558)
XLA Ops:
  0.6 2.9 %shard_map.169 = (f32[8,32,128]{2,1,0:T(8,128)S(1)}, f32[8,8,128]{2,1,0:T(8,128)S(1)}, f32[8,8,128]{2,1,0:T(8,128)S(1)}, f32[4,256,128]{2,1,0:T(8,128)S(1)}, f32...) custom-call(f32[1,256,128]{2,1,0:T(8,128)} %den.1, ...), custom_call_target="tpu_custom_call" | custom-call | tf_op jit(solution)/shard_map/pallas_call | solution.py:759
  3.5 3.1 %collective-permute-start = (f32[8,8,128]{2,1,0:T(8,128)S(1)}, f32[8,8,128]{2,1,0:T(8,128)S(1)}, u32[]{:S(2)}, u32[]{:S(2)}) collective-permute-start(f32[8,8,128]{2,1,0:T(8,128)S(1)} %get-tuple-element.50), channel_id=1, source_target_pairs={{0,1},{1,0},{2,3},{3,2},{4,5},{5,4},{6,7},{7,6},{8,9},{9,8},{10,11... | collective-permute-start | bytes 98312 | tf_op jit(solution)/shard_map/ppermute | solution.py:835
  6.6 3.4 %collective-permute-start.1 = (f32[8,8,128]{2,1,0:T(8,128)S(1)}, f32[8,8,128]{2,1,0:T(8,128)S(1)}, u32[]{:S(2)}, u32[]{:S(2)}) collective-permute-start(f32[8,8,128]{2,1,0:T(8,128)S(1)} %get-tuple-element.51), channel_id=1, source_target_pairs={{0,7},{1,2},{2,1},{3,4},{4,3},{5,6},{6,5},{7,0},{8,15},{9,10},{10,... | collective-permute-start | bytes 98312 | tf_op jit(solution)/shard_map/ppermute | solution.py:835
  10.1 4.9 %shard_map.170 = (f32[4,256,128]{2,1,0:T(8,128)S(1)}, bf16[4,256,1024]{2,1,0:T(8,128)(2,1)S(1)}, bf16[4,256,1024]{2,1,0:T(8,128)(2,1)S(1)}, bf16[4,256,1024]{2,1...) custom-call(f32[4,256,128]{2,1,0:T(8,128)S(1)} %get-tuple-element.41.state, ...), custom_call_target="tpu_custom_call" | custom-call | flops 10000000000 | bytes 10000000 | tf_op jit(solution)/shard_map/pallas_call | solution.py:759
  15.0 0.0 collective-permute-done.from_first
  15.0 0.0 collective-permute-done.1.from_second
  15.0 25.6 %shard_map.171 = (f32[1,256,128]{2,1,0:T(8,128)}, f32[1,2,256,128]{3,2,1,0:T(8,128)}, f32[1,256,128]{2,1,0:T(8,128)}, f32[40,128]{1,0:T(8,128)S(1)}) custom-call(f32[4,256,128]{2,1,0:T(8,128)S(1)} %get-tuple-element.41.state, f32[4,256,128]{2,1,0:T(8,128)S(1)} %get-tuple-element.42.cot, f32[4,256,128]{2,1,0:T(8,128)S(1)} %get-tuple-element.48.middle, ...), custom_call_target="tpu_custom_call" | custom-call | flops 40000000000 | bytes 20000000 | tf_op jit(solution)/shard_map/pallas_call | solution.py:759
  40.7 0.0 collective-permute-start.2
  40.7 1.2 %collective-permute-done.2 = f32[40,128]{1,0:T(8,128)S(1)} collective-permute-done((f32[40,128]{1,0:T(8,128)S(1)}, f32[40,128]{1,0:T(8,128)S(1)}, u32[]{:S(2)}, u32[]{:S(2)}) %collective-permute-start.2) | collective-permute-done | bytes 20512 | tf_op jit(solution)/shard_map/ppermute | solution.py:785
  41.9 1.4 %collective-permute-start.5 = (f32[40,128]{1,0:T(8,128)S(1)}, f32[40,128]{1,0:T(8,128)S(1)}, u32[]{:S(2)}, u32[]{:S(2)}) collective-permute-start(f32[40,128]{1,0:T(8,128)S(1)} %add.21), channel_id=1, source_target_pairs={{0,20},{1,21},{2,22},{3,23},{4,16},{5,17},{6,18},{7,19},{8,28},{9,... | collective-permute-start | bytes 61448 | tf_op jit(solution)/shard_map/ppermute | solution.py:785
  43.3 1.5 %collective-permute-start.4 = (f32[40,128]{1,0:T(8,128)S(1)}, f32[40,128]{1,0:T(8,128)S(1)}, u32[]{:S(2)}, u32[]{:S(2)}) collective-permute-start(f32[40,128]{1,0:T(8,128)S(1)} %add.21), channel_id=1, source_target_pairs={{0,4},{1,5},{2,6},{3,7},{4,0},{5,1},{6,2},{7,3},{8,12},{9,13},{10,... | collective-permute-start | bytes 61448 | tf_op jit(solution)/shard_map/ppermute | solution.py:785
  44.8 0.5 collective-permute-start.3
  45.3 1.2 %collective-permute-done.5 = f32[40,128]{1,0:T(8,128)S(1)} collective-permute-done((f32[40,128]{1,0:T(8,128)S(1)}, f32[40,128]{1,0:T(8,128)S(1)}, u32[]{:S(2)}, u32[]{:S(2)}) %collective-permute-start.5) | collective-permute-done | bytes 20512 | tf_op jit(solution)/shard_map/ppermute | solution.py:785
  46.5 0.5 collective-permute-done.4
  47.1 1.5 %collective-permute-done.3 = f32[40,128]{1,0:T(8,128)S(1)} collective-permute-done((f32[40,128]{1,0:T(8,128)S(1)}, f32[40,128]{1,0:T(8,128)S(1)}, u32[]{:S(2)}, u32[]{:S(2)}) %collective-permute-start.3) | collective-permute-done | bytes 20512 | tf_op jit(solution)/shard_map/ppermute | solution.py:785
  48.6 1.4 %collective-permute-start.8 = (f32[40,128]{1,0:T(8,128)S(1)}, f32[40,128]{1,0:T(8,128)S(1)}, u32[]{:S(2)}, u32[]{:S(2)}) collective-permute-start(f32[40,128]{1,0:T(8,128)S(1)} %add_add_fusion.1), channel_id=1, source_target_pairs={{0,3},{1,2},{2,1},{3,0},{4,7},{5,6},{6,5},{7,4},{8,11},{9,10},{10,... | collective-permute-start | bytes 61448 | tf_op jit(solution)/shard_map/ppermute | solution.py:785
  50.0 0.0 collective-permute-start.7
  50.0 3.0 %collective-permute-start.6 = (f32[40,128]{1,0:T(8,128)S(1)}, f32[40,128]{1,0:T(8,128)S(1)}, u32[]{:S(2)}, u32[]{:S(2)}) collective-permute-start(f32[40,128]{1,0:T(8,128)S(1)} %add_add_fusion.1), channel_id=1, source_target_pairs={{0,2},{1,3},{2,0},{3,1},{4,6},{5,7},{6,4},{7,5},{8,10},{9,11},{10,... | collective-permute-start | bytes 61448 | tf_op jit(solution)/shard_map/ppermute | solution.py:785
  53.0 1.2 %collective-permute-done.8 = f32[40,128]{1,0:T(8,128)S(1)} collective-permute-done((f32[40,128]{1,0:T(8,128)S(1)}, f32[40,128]{1,0:T(8,128)S(1)}, u32[]{:S(2)}, u32[]{:S(2)}) %collective-permute-start.8) | collective-permute-done | bytes 20512 | tf_op jit(solution)/shard_map/ppermute | solution.py:785
  54.2 0.0 collective-permute-done.7
  54.2 0.6 %collective-permute-done.6 = f32[40,128]{1,0:T(8,128)S(1)} collective-permute-done((f32[40,128]{1,0:T(8,128)S(1)}, f32[40,128]{1,0:T(8,128)S(1)}, u32[]{:S(2)}, u32[]{:S(2)}) %collective-permute-start.6) | collective-permute-done | bytes 20512 | tf_op jit(solution)/shard_map/ppermute | solution.py:785
  54.8 0.7 %shard_map.172 = (f32[16,32]{1,0:T(8,128)}, f32[1,32]{1,0:T(1,128)}, f32[32,32]{1,0:T(8,128)}, f32[1,32]{1,0:T(1,128)}, f32[8,32]{1,0:T(8,128)}, /*index=5*/f32[1,8]{1,0:T(1,128)}) custom-call(f32[40,128]{1,0:T(8,128)S(1)} %add_add_fusion.total), custom_call_target="tpu_custom_call" | custom-call | tf_op jit(solution)/shard_map/pallas_call | solution.py:759
  (3 shorter events, 0.0 us)
Async XLA Ops:
  3.5 11.5 %collective-permute-start = (f32[8,8,128]{2,1,0:T(8,128)S(1)}, f32[8,8,128]{2,1,0:T(8,128)S(1)}, u32[]{:S(2)}, u32[]{:S(2)}) collective-permute-start(f32[8,8,128]{2,1,0:T(8,128)S(1)} %get-tuple-element.50), channel_id=1, source_target_pairs={{0,1},{1,0},{2,3},{3,2},{4,5},{5,4},{6,7},{7,6},{8,9},{9,8},{10,11... | collective-permute-start | bytes 98312 | tf_op jit(solution)/shard_map/ppermute | solution.py:835
  6.6 8.4 %collective-permute-start.1 = (f32[8,8,128]{2,1,0:T(8,128)S(1)}, f32[8,8,128]{2,1,0:T(8,128)S(1)}, u32[]{:S(2)}, u32[]{:S(2)}) collective-permute-start(f32[8,8,128]{2,1,0:T(8,128)S(1)} %get-tuple-element.51), channel_id=1, source_target_pairs={{0,7},{1,2},{2,1},{3,4},{4,3},{5,6},{6,5},{7,0},{8,15},{9,10},{10,... | collective-permute-start | bytes 98312 | tf_op jit(solution)/shard_map/ppermute | solution.py:835
  40.7 1.2 %collective-permute-start.2 = (f32[40,128]{1,0:T(8,128)S(1)}, f32[40,128]{1,0:T(8,128)S(1)}, u32[]{:S(2)}, u32[]{:S(2)}) collective-permute-start(f32[40,128]{1,0:T(8,128)S(1)} %get-tuple-element.66), channel_id=1, source_target_pairs={{0,8},{1,9},{2,10},{3,11},{4,12},{5,13},{6,14},{7,15},{8,0},{9,1},... | collective-permute-start | bytes 61448 | tf_op jit(solution)/shard_map/ppermute | solution.py:785
  41.9 4.7 %collective-permute-start.5 = (f32[40,128]{1,0:T(8,128)S(1)}, f32[40,128]{1,0:T(8,128)S(1)}, u32[]{:S(2)}, u32[]{:S(2)}) collective-permute-start(f32[40,128]{1,0:T(8,128)S(1)} %add.21), channel_id=1, source_target_pairs={{0,20},{1,21},{2,22},{3,23},{4,16},{5,17},{6,18},{7,19},{8,28},{9,... | collective-permute-start | bytes 61448 | tf_op jit(solution)/shard_map/ppermute | solution.py:785
  43.3 3.8 %collective-permute-start.4 = (f32[40,128]{1,0:T(8,128)S(1)}, f32[40,128]{1,0:T(8,128)S(1)}, u32[]{:S(2)}, u32[]{:S(2)}) collective-permute-start(f32[40,128]{1,0:T(8,128)S(1)} %add.21), channel_id=1, source_target_pairs={{0,4},{1,5},{2,6},{3,7},{4,0},{5,1},{6,2},{7,3},{8,12},{9,13},{10,... | collective-permute-start | bytes 61448 | tf_op jit(solution)/shard_map/ppermute | solution.py:785
  44.8 3.8 %collective-permute-start.3 = (f32[40,128]{1,0:T(8,128)S(1)}, f32[40,128]{1,0:T(8,128)S(1)}, u32[]{:S(2)}, u32[]{:S(2)}) collective-permute-start(f32[40,128]{1,0:T(8,128)S(1)} %add.21), channel_id=1, source_target_pairs={{0,16},{1,17},{2,18},{3,19},{4,20},{5,21},{6,22},{7,23},{8,24},{9,... | collective-permute-start | bytes 61448 | tf_op jit(solution)/shard_map/ppermute | solution.py:785
  48.6 5.6 %collective-permute-start.8 = (f32[40,128]{1,0:T(8,128)S(1)}, f32[40,128]{1,0:T(8,128)S(1)}, u32[]{:S(2)}, u32[]{:S(2)}) collective-permute-start(f32[40,128]{1,0:T(8,128)S(1)} %add_add_fusion.1), channel_id=1, source_target_pairs={{0,3},{1,2},{2,1},{3,0},{4,7},{5,6},{6,5},{7,4},{8,11},{9,10},{10,... | collective-permute-start | bytes 61448 | tf_op jit(solution)/shard_map/ppermute | solution.py:785
  50.0 4.2 %collective-permute-start.7 = (f32[40,128]{1,0:T(8,128)S(1)}, f32[40,128]{1,0:T(8,128)S(1)}, u32[]{:S(2)}, u32[]{:S(2)}) collective-permute-start(f32[40,128]{1,0:T(8,128)S(1)} %add_add_fusion.1), channel_id=1, source_target_pairs={{0,1},{1,0},{2,3},{3,2},{4,5},{5,4},{6,7},{7,6},{8,9},{9,8},{10,11... | collective-permute-start | bytes 61448 | tf_op jit(solution)/shard_map/ppermute | solution.py:785
  50.0 4.8 %collective-permute-start.6 = (f32[40,128]{1,0:T(8,128)S(1)}, f32[40,128]{1,0:T(8,128)S(1)}, u32[]{:S(2)}, u32[]{:S(2)}) collective-permute-start(f32[40,128]{1,0:T(8,128)S(1)} %add_add_fusion.1), channel_id=1, source_target_pairs={{0,2},{1,3},{2,0},{3,1},{4,6},{5,7},{6,4},{7,5},{8,10},{9,11},{10,... | collective-permute-start | bytes 61448 | tf_op jit(solution)/shard_map/ppermute | solution.py:785

commit v7 on v6

--- a/solution.py
+++ b/solution.py
@@ -14,10 +14,10 @@
 FACES = 8
 SEG = 16
 RIM = 4
-PAIR = 8
+PAIR = 16
 RIM_PAIR = 4
 ONES = 16
-VMEM_BYTES = 32 * 2**20
+VMEM_BYTES = 28 * 2**20
 
 
 def dot(a, b):
@@ -132,19 +132,24 @@
     wide = FACES * hid
 
     def source(q, n):
-        in_x = (q < 256) & (n == 4 * (q >> 6) + ((q & 63) >> 4))
-        in_y = (q >= 256) & (n == ((q - 256) >> 3))
+        in_x = (q < 512) & (n == 4 * (q >> 7) + ((q & 63) >> 4))
+        in_y = (q >= 512) & (n == (((q - 512) & 127) >> 3))
         return in_x | in_y
 
-    rows = exact(pick((256 + 128, 16), source, F32), w_t).astype(BF16)
-    value = dot(rows, pick((hid, wide), lambda q, n: rest(n, hid) == q))
-    r, c = rows_cols((64, wide))
-    shift = (r & 15) - quot(c, hid)
-    back_x = jnp.zeros((64, wide), F32)
+    rows = exact(pick((512 + 256, 16), source, F32), w_t)
+    right = pick((hid, 2 * wide), lambda q, n: rest(n, hid) == q)
+    high, low = (dot(part, right) for part in split(rows))
+    r, c = rows_cols(high.shape)
+    is_low = jnp.where(r < 512, r & 64, (r - 512) & 128) > 0
+    value = jnp.where(is_low, jnp.where(c < wide, low, 0.0), high)
+    face = quot(rest(c, wide), hid)
+    r, c = r[:128], c[:128]
+    shift = (r & 15) - face[:128]
+    back_x = jnp.zeros((128, 2 * wide), F32)
     for s in range(4):
-        back_x = jnp.where(shift == s, value[64 * s : 64 * (s + 1)], back_x)
-    r, c = rows_cols((128, wide))
-    back_y = jnp.where((r & 7) == quot(c, hid), value[256:], 0.0)
+        back_x = jnp.where(shift == s, value[128 * s : 128 * (s + 1)], back_x)
+    r, _ = rows_cols((256, 2 * wide))
+    back_y = jnp.where((r & 7) == face[512:], value[512:], 0.0)
     return back_x.astype(BF16), back_y.astype(BF16)
 
 
@@ -225,13 +230,13 @@
     return h1, h1_parts[:2], h2, h2_parts[:2], gates
 
 
-def limiter_backward(d3, h1, h2, h1_pair, h2_pair, out_back_ref, mid_back_ref, acc, hid):
+def limiter_backward(d3, slope1, slope2, h1_pair, h2_pair, out_back_ref, mid_back_ref, acc, hid):
     d3_hi, d3_lo = split(d3)
     dh2 = dot(out_back_ref[...], stack([d3_hi, d3_hi, d3_lo]))
     if acc is not None:
         acc[2][...] += dot_nt(stack(list(h2_pair)), stack([d3_hi, d3_lo]))
         acc[3][...] += d3
-    d2_hi, d2_lo = split(dh2 * (1.0 - h2 * h2))
+    d2_hi, d2_lo = split(dh2 * slope2)
     block = 2 * hid
     parts = []
     for at in range(0, FACES * hid, block):
@@ -244,7 +249,13 @@
             lefts.append(stack([part[at : at + 2 * block] for part in h1_pair] + [ones]))
             rights.append(stack([part[at : at + 2 * block] for part in (d2_hi, d2_lo)]))
         acc[1][...] += dot_nt(side(lefts), side(rights))
-    return stack(parts) * (1.0 - h1 * h1)
+    return stack(parts) * slope1
+
+
+def first_backward(d1, back_ref):
+    both = dot(back_ref[...], stack([d1[0], d1[1]]))
+    half = both.shape[0] // 2
+    return both[:half] + both[half:]
 
 
 def add_first_grads(first, d1, acc_in):
@@ -423,7 +434,7 @@
 def x_forward(tiles, weights, hid):
     h1, h1_pair, h2, h2_pair, gates = limiter_forward(x_windows(tiles), weights, hid)
     cells = x_cells(tiles)
-    return h1_pair, h2_pair, gates, face_flux(*edge_states(cells, gates))
+    return h1, h2, h1_pair, h2_pair, gates, face_flux(*edge_states(cells, gates))
 
 
 def update_cells(plane_rows, flux_rows):
@@ -433,7 +444,7 @@
 
 
 def x_forward_kernel(state, first_x, mid, mid_bias, out, out_bias,
-                     middle, h1_hi, h1_lo, h2_hi, h2_lo, gates_out, flux):
+                     middle, h1_hi, h1_lo, h2_hi, h2_lo, slope1, slope2, gates_out, flux):
     nx, ny = state.shape[1:]
     groups = nx // FACES
     half = groups // PAIR
@@ -443,9 +454,11 @@
 
     def step_of(step, _):
         tiles = pair_tiles(planes, step, half)
-        h1_pair, h2_pair, gates, fluxes = x_forward(tiles, x_weights, hid)
+        h1, h2, h1_pair, h2_pair, gates, fluxes = x_forward(tiles, x_weights, hid)
         for target, value in zip((h1_hi, h1_lo, h2_hi, h2_lo, gates_out), h1_pair + h2_pair + (gates,)):
             target[step] = value
+        slope1[step] = 1.0 - h1 * h1
+        slope2[step] = 1.0 - h2 * h2
         for c in range(4):
             for k in range(PAIR):
                 flux[c, row_block(step + k * half + 1), :] = fluxes[c][:, k * ny : (k + 1) * ny]
@@ -483,9 +496,11 @@
         d_left = [jnp.where(halo_mask, d, 0.0) for d in d_left]
         d_right = [jnp.where(halo_mask, d, 0.0) for d in d_right]
     d3_full, direct = edge_backward(cells, gates, d_left, d_right)
-    d1_full = limiter_backward(d3_full, h1, h2, h1_pair, h2_pair, out_back, mid_back, acc, hid)
+    d1_full = limiter_backward(
+        d3_full, 1.0 - h1 * h1, 1.0 - h2 * h2, h1_pair, h2_pair, out_back, mid_back, acc, hid
+    )
     d1 = split(d1_full)
-    d_window = dot(first_y_back[...], d1[0])
+    d_window = first_backward(d1, first_y_back)
     if acc is not None:
         add_first_grads(window, d1, acc[0])
         ny = acc[4].shape[1]
@@ -514,7 +529,7 @@
 def back_kernel(state, cot, middle, own, from_first, from_second,
                 first_x, first_y, first_bias, mid, mid_bias, out, out_bias,
                 out_back, mid_back, first_x_back, first_y_back,
-                h1_hi, h1_lo, h2_hi, h2_lo, gates_in,
+                h1_hi, h1_lo, h2_hi, h2_lo, slope1, slope2, gates_in,
                 g_den, g_mom, g_tra, g_weights,
                 rim_state, rim_cot, rim_flux, rim_middle, rim_grad, d_middle,
                 acc_x, acc_y, acc_y_bias, acc_mid, acc_out, acc_out_bias):
@@ -567,7 +582,7 @@
             for k in range(RIM_PAIR)
         ]
         tiles = [side([one[c] for one in sets]) for c in range(4)]
-        fluxes = x_forward(tiles, x_weights, hid)[3]
+        fluxes = x_forward(tiles, x_weights, hid)[-1]
         for c in range(4):
             for k in range(RIM_PAIR):
                 rim_flux[c, row_block(step + k * rim_half + 1), :] = fluxes[c][:, k * ny : (k + 1) * ny]
@@ -667,18 +682,16 @@
         gates = gates_in[step]
         h1_pair = (h1_hi[step], h1_lo[step])
         h2_pair = (h2_hi[step], h2_lo[step])
-        h1 = h1_pair[0].astype(F32) + h1_pair[1].astype(F32)
-        h2 = h2_pair[0].astype(F32) + h2_pair[1].astype(F32)
         cells = x_cells(tiles)
         left, right = edge_states(cells, gates)
         d_flux = [courant * (turn(d, -2, 0)[:FACES] - turn(d, -1, 0)[:FACES]) for d in d_tiles]
         d_left, d_right = face_flux_backward(left, right, d_flux)
         d3_full, direct = edge_backward(cells, gates, d_left, d_right)
         d1_full = limiter_backward(
-            d3_full, h1, h2, h1_pair, h2_pair, out_back, mid_back, (acc_x, acc_mid, acc_out, acc_out_bias), hid
+            d3_full, slope1[step], slope2[step], h1_pair, h2_pair, out_back, mid_back, (acc_x, acc_mid, acc_out, acc_out_bias), hid
         )
         d1 = split(d1_full)
-        d_window = dot(first_x_back[...], d1[0])
+        d_window = first_backward(d1, first_x_back)
         add_first_grads(split(stack(tiles)), d1, acc_x)
         later = []
         for c in range(4):
@@ -822,8 +835,8 @@
             shape((64, ny), F32),
             shape((wide, 192), BF16),
             shape((2 * hid, 6 * hid), BF16),
-            shape((64, wide), BF16),
-            shape((128, wide), BF16),
+            shape((128, 2 * wide), BF16),
+            shape((256, 2 * wide), BF16),
         ],
         [pltpu.with_memory_space_constraint(one, pltpu.HBM) for one in operands],
         in_spaces=whole(10, pltpu.HBM),
@@ -839,6 +852,7 @@
         x_forward_kernel,
         [shape((4, nx, ny), F32)]
         + [shape((half, wide, lanes), BF16)] * 4
+        + [shape((half, wide, lanes), F32)] * 2
         + [shape((half, 64, lanes), F32)],
         [state, matrices[0]] + matrices[3:7],
         scratch=[pltpu.VMEM((4, nx + FACES, ny), F32)],

time: 55.7 us -> 58.1 us (1.043)
  Pallas kernels: 34.1 us -> 36.5 us
    pallas_call x4, Pallas kernels: 34.1 us -> 36.5 us  [call(): pl.pallas_call(kernel, out_shape=outs, in_specs=in_spaces or whole(len(op...]
  transfers between devices with their start and end apart: 9 -> 9, of which waited for: 6 -> 6; matrix products, arithmetic and copies ran while one was open for 0% -> 0% of each run, Pallas kernels for 9% -> 10%
where the time goes in v7:
time: 58.1 us; the launch traced here: 57.9 us
  Pallas kernels  36.5 us (63%)
  starting transfers between devices  14.5 us (25%)
  waiting for transfers between devices  6.2 us (11%)
  between operations  0.69 us (1%)
    pallas_call x4, Pallas kernels, call(): pl.pallas_call(kernel, out_shape=outs, in_specs=in_spaces or whole(len(op...  36.5 us
    ppermute x7, starting transfers between devices, sum_all(): lax.ppermute(values, axes, [(i, i ^ one) for i in range(size)])  7.94 us
    ppermute x2, starting transfers between devices, body(): lax.ppermute(one, axes, swap)  6.51 us
    ppermute x7, waiting for transfers between devices, sum_all(): lax.ppermute(values, axes, [(i, i ^ one) for i in range(size)])  6.2 us
  transfers between devices with their start and end apart: 9, of which 6 were waited for; matrix products, arithmetic and copies ran while one was open for 0% of the time, Pallas kernels for 10%

profile of v7, /device:TPU:0, one launch (start us, length us, event | category | flops | bytes accessed | tf_op | source)
XLA Modules:
  0.0 57.9 jit_solution(2909551851902066116)
XLA Ops:
  0.6 3.7 %shard_map.169 = (f32[8,32,128]{2,1,0:T(8,128)S(1)}, f32[8,8,128]{2,1,0:T(8,128)S(1)}, f32[8,8,128]{2,1,0:T(8,128)S(1)}, f32[4,256,128]{2,1,0:T(8,128)S(1)}, f32...) custom-call(f32[1,256,128]{2,1,0:T(8,128)} %den.1, ...), custom_call_target="tpu_custom_call" | custom-call | tf_op jit(solution)/shard_map/pallas_call | solution.py:772
  4.3 3.1 %collective-permute-start = (f32[8,8,128]{2,1,0:T(8,128)S(1)}, f32[8,8,128]{2,1,0:T(8,128)S(1)}, u32[]{:S(2)}, u32[]{:S(2)}) collective-permute-start(f32[8,8,128]{2,1,0:T(8,128)S(1)} %get-tuple-element.52), channel_id=1, source_target_pairs={{0,1},{1,0},{2,3},{3,2},{4,5},{5,4},{6,7},{7,6},{8,9},{9,8},{10,11... | collective-permute-start | bytes 98312 | tf_op jit(solution)/shard_map/ppermute | solution.py:848
  7.4 3.4 %collective-permute-start.1 = (f32[8,8,128]{2,1,0:T(8,128)S(1)}, f32[8,8,128]{2,1,0:T(8,128)S(1)}, u32[]{:S(2)}, u32[]{:S(2)}) collective-permute-start(f32[8,8,128]{2,1,0:T(8,128)S(1)} %get-tuple-element.53), channel_id=1, source_target_pairs={{0,7},{1,2},{2,1},{3,4},{4,3},{5,6},{6,5},{7,0},{8,15},{9,10},{10,... | collective-permute-start | bytes 98312 | tf_op jit(solution)/shard_map/ppermute | solution.py:848
  10.8 5.6 %shard_map.170 = (f32[4,256,128]{2,1,0:T(8,128)S(1)}, bf16[2,256,2048]{2,1,0:T(8,128)(2,1)S(1)}, bf16[2,256,2048]{2,1,0:T(8,128)(2,1)S(1)}, bf16[2,256,2048]{2,1...) custom-call(f32[4,256,128]{2,1,0:T(8,128)S(1)} %get-tuple-element.43, ...), custom_call_target="tpu_custom_call" | custom-call | flops 10000000000 | bytes 10000000 | tf_op jit(solution)/shard_map/pallas_call | solution.py:772
  16.4 0.0 collective-permute-done.from_first
  16.4 0.0 collective-permute-done.1.from_second
  16.4 26.6 %shard_map.171 = (f32[1,256,128]{2,1,0:T(8,128)}, f32[1,2,256,128]{3,2,1,0:T(8,128)}, f32[1,256,128]{2,1,0:T(8,128)}, f32[40,128]{1,0:T(8,128)S(1)}) custom-call(f32[4,256,128]{2,1,0:T(8,128)S(1)} %get-tuple-element.43.state, f32[4,256,128]{2,1,0:T(8,128)S(1)} %get-tuple-element.44.cot, f32[4,256,128]{2,1,0:T(8,128)S(1)} %get-tuple-element.50.middle, ...), custom_call_target="tpu_custom_call" | custom-call | flops 40000000000 | bytes 20000000 | tf_op jit(solution)/shard_map/pallas_call | solution.py:772
  43.0 0.0 collective-permute-start.2
  43.0 1.2 %collective-permute-done.2 = f32[40,128]{1,0:T(8,128)S(1)} collective-permute-done((f32[40,128]{1,0:T(8,128)S(1)}, f32[40,128]{1,0:T(8,128)S(1)}, u32[]{:S(2)}, u32[]{:S(2)}) %collective-permute-start.2) | collective-permute-done | bytes 20512 | tf_op jit(solution)/shard_map/ppermute | solution.py:798
  44.2 1.5 %collective-permute-start.5 = (f32[40,128]{1,0:T(8,128)S(1)}, f32[40,128]{1,0:T(8,128)S(1)}, u32[]{:S(2)}, u32[]{:S(2)}) collective-permute-start(f32[40,128]{1,0:T(8,128)S(1)} %add.21), channel_id=1, source_target_pairs={{0,20},{1,21},{2,22},{3,23},{4,16},{5,17},{6,18},{7,19},{8,28},{9,... | collective-permute-start | bytes 61448 | tf_op jit(solution)/shard_map/ppermute | solution.py:798
  45.7 1.5 %collective-permute-start.4 = (f32[40,128]{1,0:T(8,128)S(1)}, f32[40,128]{1,0:T(8,128)S(1)}, u32[]{:S(2)}, u32[]{:S(2)}) collective-permute-start(f32[40,128]{1,0:T(8,128)S(1)} %add.21), channel_id=1, source_target_pairs={{0,4},{1,5},{2,6},{3,7},{4,0},{5,1},{6,2},{7,3},{8,12},{9,13},{10,... | collective-permute-start | bytes 61448 | tf_op jit(solution)/shard_map/ppermute | solution.py:798
  47.2 0.5 collective-permute-start.3
  47.7 1.2 %collective-permute-done.5 = f32[40,128]{1,0:T(8,128)S(1)} collective-permute-done((f32[40,128]{1,0:T(8,128)S(1)}, f32[40,128]{1,0:T(8,128)S(1)}, u32[]{:S(2)}, u32[]{:S(2)}) %collective-permute-start.5) | collective-permute-done | bytes 20512 | tf_op jit(solution)/shard_map/ppermute | solution.py:798
  48.9 0.6 collective-permute-done.4
  49.5 1.5 %collective-permute-done.3 = f32[40,128]{1,0:T(8,128)S(1)} collective-permute-done((f32[40,128]{1,0:T(8,128)S(1)}, f32[40,128]{1,0:T(8,128)S(1)}, u32[]{:S(2)}, u32[]{:S(2)}) %collective-permute-start.3) | collective-permute-done | bytes 20512 | tf_op jit(solution)/shard_map/ppermute | solution.py:798
  51.0 1.4 %collective-permute-start.8 = (f32[40,128]{1,0:T(8,128)S(1)}, f32[40,128]{1,0:T(8,128)S(1)}, u32[]{:S(2)}, u32[]{:S(2)}) collective-permute-start(f32[40,128]{1,0:T(8,128)S(1)} %add_add_fusion.1), channel_id=1, source_target_pairs={{0,3},{1,2},{2,1},{3,0},{4,7},{5,6},{6,5},{7,4},{8,11},{9,10},{10,... | collective-permute-start | bytes 61448 | tf_op jit(solution)/shard_map/ppermute | solution.py:798
  52.4 0.0 collective-permute-start.7
  52.4 3.0 %collective-permute-start.6 = (f32[40,128]{1,0:T(8,128)S(1)}, f32[40,128]{1,0:T(8,128)S(1)}, u32[]{:S(2)}, u32[]{:S(2)}) collective-permute-start(f32[40,128]{1,0:T(8,128)S(1)} %add_add_fusion.1), channel_id=1, source_target_pairs={{0,2},{1,3},{2,0},{3,1},{4,6},{5,7},{6,4},{7,5},{8,10},{9,11},{10,... | collective-permute-start | bytes 61448 | tf_op jit(solution)/shard_map/ppermute | solution.py:798
  55.4 1.2 %collective-permute-done.8 = f32[40,128]{1,0:T(8,128)S(1)} collective-permute-done((f32[40,128]{1,0:T(8,128)S(1)}, f32[40,128]{1,0:T(8,128)S(1)}, u32[]{:S(2)}, u32[]{:S(2)}) %collective-permute-start.8) | collective-permute-done | bytes 20512 | tf_op jit(solution)/shard_map/ppermute | solution.py:798
  56.6 0.0 collective-permute-done.7
  56.6 0.6 collective-permute-done.6
  57.2 0.7 %shard_map.172 = (f32[16,32]{1,0:T(8,128)}, f32[1,32]{1,0:T(1,128)}, f32[32,32]{1,0:T(8,128)}, f32[1,32]{1,0:T(1,128)}, f32[8,32]{1,0:T(8,128)}, /*index=5*/f32[1,8]{1,0:T(1,128)}) custom-call(f32[40,128]{1,0:T(8,128)S(1)} %add_add_fusion.total), custom_call_target="tpu_custom_call" | custom-call | tf_op jit(solution)/shard_map/pallas_call | solution.py:772
  (3 shorter events, 0.0 us)
Async XLA Ops:
  4.3 12.1 %collective-permute-start = (f32[8,8,128]{2,1,0:T(8,128)S(1)}, f32[8,8,128]{2,1,0:T(8,128)S(1)}, u32[]{:S(2)}, u32[]{:S(2)}) collective-permute-start(f32[8,8,128]{2,1,0:T(8,128)S(1)} %get-tuple-element.52), channel_id=1, source_target_pairs={{0,1},{1,0},{2,3},{3,2},{4,5},{5,4},{6,7},{7,6},{8,9},{9,8},{10,11... | collective-permute-start | bytes 98312 | tf_op jit(solution)/shard_map/ppermute | solution.py:848
  7.4 9.0 %collective-permute-start.1 = (f32[8,8,128]{2,1,0:T(8,128)S(1)}, f32[8,8,128]{2,1,0:T(8,128)S(1)}, u32[]{:S(2)}, u32[]{:S(2)}) collective-permute-start(f32[8,8,128]{2,1,0:T(8,128)S(1)} %get-tuple-element.53), channel_id=1, source_target_pairs={{0,7},{1,2},{2,1},{3,4},{4,3},{5,6},{6,5},{7,0},{8,15},{9,10},{10,... | collective-permute-start | bytes 98312 | tf_op jit(solution)/shard_map/ppermute | solution.py:848
  43.0 1.2 %collective-permute-start.2 = (f32[40,128]{1,0:T(8,128)S(1)}, f32[40,128]{1,0:T(8,128)S(1)}, u32[]{:S(2)}, u32[]{:S(2)}) collective-permute-start(f32[40,128]{1,0:T(8,128)S(1)} %get-tuple-element.70), channel_id=1, source_target_pairs={{0,8},{1,9},{2,10},{3,11},{4,12},{5,13},{6,14},{7,15},{8,0},{9,1},... | collective-permute-start | bytes 61448 | tf_op jit(solution)/shard_map/ppermute | solution.py:798
  44.2 4.7 %collective-permute-start.5 = (f32[40,128]{1,0:T(8,128)S(1)}, f32[40,128]{1,0:T(8,128)S(1)}, u32[]{:S(2)}, u32[]{:S(2)}) collective-permute-start(f32[40,128]{1,0:T(8,128)S(1)} %add.21), channel_id=1, source_target_pairs={{0,20},{1,21},{2,22},{3,23},{4,16},{5,17},{6,18},{7,19},{8,28},{9,... | collective-permute-start | bytes 61448 | tf_op jit(solution)/shard_map/ppermute | solution.py:798
  45.7 3.8 %collective-permute-start.4 = (f32[40,128]{1,0:T(8,128)S(1)}, f32[40,128]{1,0:T(8,128)S(1)}, u32[]{:S(2)}, u32[]{:S(2)}) collective-permute-start(f32[40,128]{1,0:T(8,128)S(1)} %add.21), channel_id=1, source_target_pairs={{0,4},{1,5},{2,6},{3,7},{4,0},{5,1},{6,2},{7,3},{8,12},{9,13},{10,... | collective-permute-start | bytes 61448 | tf_op jit(solution)/shard_map/ppermute | solution.py:798
  47.2 3.8 %collective-permute-start.3 = (f32[40,128]{1,0:T(8,128)S(1)}, f32[40,128]{1,0:T(8,128)S(1)}, u32[]{:S(2)}, u32[]{:S(2)}) collective-permute-start(f32[40,128]{1,0:T(8,128)S(1)} %add.21), channel_id=1, source_target_pairs={{0,16},{1,17},{2,18},{3,19},{4,20},{5,21},{6,22},{7,23},{8,24},{9,... | collective-permute-start | bytes 61448 | tf_op jit(solution)/shard_map/ppermute | solution.py:798
  51.0 5.6 %collective-permute-start.8 = (f32[40,128]{1,0:T(8,128)S(1)}, f32[40,128]{1,0:T(8,128)S(1)}, u32[]{:S(2)}, u32[]{:S(2)}) collective-permute-start(f32[40,128]{1,0:T(8,128)S(1)} %add_add_fusion.1), channel_id=1, source_target_pairs={{0,3},{1,2},{2,1},{3,0},{4,7},{5,6},{6,5},{7,4},{8,11},{9,10},{10,... | collective-permute-start | bytes 61448 | tf_op jit(solution)/shard_map/ppermute | solution.py:798
  52.4 4.2 %collective-permute-start.7 = (f32[40,128]{1,0:T(8,128)S(1)}, f32[40,128]{1,0:T(8,128)S(1)}, u32[]{:S(2)}, u32[]{:S(2)}) collective-permute-start(f32[40,128]{1,0:T(8,128)S(1)} %add_add_fusion.1), channel_id=1, source_target_pairs={{0,1},{1,0},{2,3},{3,2},{4,5},{5,4},{6,7},{7,6},{8,9},{9,8},{10,11... | collective-permute-start | bytes 61448 | tf_op jit(solution)/shard_map/ppermute | solution.py:798
  52.4 4.8 %collective-permute-start.6 = (f32[40,128]{1,0:T(8,128)S(1)}, f32[40,128]{1,0:T(8,128)S(1)}, u32[]{:S(2)}, u32[]{:S(2)}) collective-permute-start(f32[40,128]{1,0:T(8,128)S(1)} %add_add_fusion.1), channel_id=1, source_target_pairs={{0,2},{1,3},{2,0},{3,1},{4,6},{5,7},{6,4},{7,5},{8,10},{9,11},{10,... | collective-permute-start | bytes 61448 | tf_op jit(solution)/shard_map/ppermute | solution.py:798

commit v8 on v6

--- a/solution.py
+++ b/solution.py
@@ -96,20 +96,27 @@
     return total
 
 
+def y_column(m):
+    return 4 * (2 * (m >> 5) + ((m & 7) >> 2)) + ((m & 31) >> 3)
+
+
 def build_first(w, b, hid):
-    x_cols, y_cols, step = 6 * 32 + ONES, 6 * 128, 256
+    x_cols, y_cols, step = 6 * 32 + ONES, 4 * 64, 256
 
     def source(q, n):
         s = n >> 8
         m = n & (step - 1)
         in_x = (s < 4) & (m < 192) & (q == 4 * s + ((m & 31) >> 3))
-        in_y = (n >= 4 * step) & (q == (((n - 4 * step) & 127) >> 3))
+        in_y = (s == 4) & (q == y_column(m & 63))
         return in_x | in_y
 
-    spread_out = exact(w, pick((16, 4 * step + y_cols), source, F32))
-    _, n = rows_cols(spread_out.shape)
-    block = jnp.where(n < 4 * step, (n & (step - 1)) >> 5, (n - 4 * step) >> 7)
-    spread_out = choose(spread_out, level_of(block))
+    values = exact(w, pick((16, 4 * step + y_cols), source, F32))
+    _, n = rows_cols(values.shape)
+    for_x = choose(values, level_of((n & (step - 1)) >> 5))
+    for_y = values[:, 4 * step :]
+    block = n[:, :y_cols] >> 6
+    upper = choose(for_y, jnp.where(block < 3, 0, 2))
+    lower = choose(for_y, jnp.where(block < 2, 1, -1))
 
     at, _ = rows_cols((x_cols, hid))
     rows = jnp.zeros((x_cols, hid), F32)
@@ -117,35 +124,42 @@
         rows = jnp.where(at == 192 + k, jnp.broadcast_to(level.astype(F32), (x_cols, hid)), rows)
     bias = dot_nt(pick((hid, hid), lambda q, n: q == n), rows.astype(BF16))
 
-    r, c = rows_cols((FACES // 2 * hid, x_cols))
+    half = FACES // 2
+    r, c = rows_cols((half * hid, x_cols))
     shift = jnp.where(c < 192, (c & 7) - quot(r, hid), -1)
-    first_x = stack([bias] * (FACES // 2))
+    first_x = stack([bias] * half)
     for s in range(4):
-        part = spread_out[:, s * step : s * step + x_cols]
-        first_x = jnp.where(shift == s, stack([part] * (FACES // 2)), first_x)
-    r, c = rows_cols((FACES * hid, y_cols))
-    first_y = jnp.where((c & 7) == quot(r, hid), stack([spread_out[:, 4 * step :]] * FACES), 0.0)
+        part = for_x[:, s * step : s * step + x_cols]
+        first_x = jnp.where(shift == s, stack([part] * half), first_x)
+    r, c = rows_cols((2 * half * hid, y_cols))
+    keep = (c & 3) == rest(quot(r, hid), half)
+    first_y = jnp.where(keep, stack([upper] * half + [lower] * half), 0.0)
     return first_x.astype(BF16), first_y.astype(BF16)
 
 
 def build_first_back(w_t, hid):
-    wide = FACES * hid
+    wide = FACES // 2 * hid
 
     def source(q, n):
-        in_x = (q < 256) & (n == 4 * (q >> 6) + ((q & 63) >> 4))
-        in_y = (q >= 256) & (n == ((q - 256) >> 3))
+        in_x = (q < 128) & (n == 4 * (q >> 5) + ((q & 31) >> 3))
+        in_y = (q >= 128) & (n == y_column(q - 128))
         return in_x | in_y
 
-    rows = exact(pick((256 + 128, 16), source, F32), w_t).astype(BF16)
-    value = dot(rows, pick((hid, wide), lambda q, n: rest(n, hid) == q))
-    r, c = rows_cols((64, wide))
-    shift = (r & 15) - quot(c, hid)
-    back_x = jnp.zeros((64, wide), F32)
+    rows = exact(pick((128 + 64, 16), source, F32), w_t)
+    right = pick((hid, 2 * wide), lambda q, n: rest(n, hid) == q)
+    high, low = (dot(part, right) for part in split(rows))
+    r, c = rows_cols(high.shape)
+    low = jnp.where(c < wide, low, 0.0)
+    face = quot(rest(c, wide), hid)
+    shift = (r & 7) - face
+    upper = lower = jnp.zeros((32, 2 * wide), F32)
     for s in range(4):
-        back_x = jnp.where(shift == s, value[64 * s : 64 * (s + 1)], back_x)
-    r, c = rows_cols((128, wide))
-    back_y = jnp.where((r & 7) == quot(c, hid), value[256:], 0.0)
-    return back_x.astype(BF16), back_y.astype(BF16)
+        keep = shift[:32] == s
+        upper = jnp.where(keep, high[32 * s : 32 * (s + 1)], upper)
+        lower = jnp.where(keep, low[32 * s : 32 * (s + 1)], lower)
+    keep = ((r & 3) == face)[128:]
+    back_y = stack([jnp.where(keep, high[128:], 0.0), jnp.where(keep, low[128:], 0.0)])
+    return stack([upper, lower]).astype(BF16), back_y.astype(BF16)
 
 
 def build_mid(w, hid):
@@ -205,7 +219,12 @@
         ones = [jnp.ones((ONES, width), BF16)]
         h1 = stack([jnp.tanh(dot(first_ref[...], stack(stacked(one) + ones))) for one in first])
     else:
-        h1 = jnp.tanh(dot(first_ref[...], stack(stacked(first[0]))) + spread(first_bias_ref, width))
+        parts = []
+        for high, middle, low in first:
+            both = dot(first_ref[...], stack([high, middle, low, high]))
+            half = both.shape[0] // 2
+            parts.append(jnp.tanh(both[:half] + both[half:] + spread(first_bias_ref, width)))
+        h1 = stack(parts)
     h1_parts = split3(h1)
     block = 2 * hid
     parts = []
@@ -247,14 +266,22 @@
     return stack(parts) * (1.0 - h1 * h1)
 
 
+def first_backward(d1, back_ref):
+    wide = d1[0].shape[0] // 2
+    found = []
+    for at in (0, wide):
+        both = dot(back_ref[...], stack([part[at : at + wide] for part in d1]))
+        half = both.shape[0] // 2
+        found.append(both[:half] + both[half:])
+    return found
+
+
 def add_first_grads(first, d1, acc_in):
-    high, low = first[:2]
-    both = stack(list(d1))
-    if 2 * high.shape[0] + ONES <= acc_in.shape[1]:
-        ones = jnp.ones((ONES, high.shape[1]), BF16)
-        acc_in[:, : 2 * high.shape[0] + ONES] += dot_nt(both, stack([high, low, ones]))
-    else:
-        acc_in[...] += dot_nt(both, stack([high, low]))
+    ones = jnp.ones((ONES, d1[0].shape[1]), BF16)
+    wide = d1[0].shape[0] // 2
+    lefts = [stack([one[0], one[1], ones]) for one in first]
+    rights = [stack([part[at : at + wide] for part in d1]) for at in (0, wide)]
+    acc_in[...] += dot_nt(side(lefts), side(rights))
 
 
 def edge_states(cells, gates):
@@ -360,7 +387,7 @@
     lanes = out_bias.shape[1]
     w_in_rows = exact_nt(pick((hid, hid), lambda q, n: q == n, F32), w_in[...])
     first_x[...], first_y[...] = build_first(w_in_rows, b_in[...], hid)
-    first_bias[...] = spread_bias(b_in[...], lanes, FACES)
+    first_bias[...] = spread_bias(b_in[...], lanes, FACES // 2)
     mid[...] = build_mid(w_mid[...], hid)
     mid_bias[...] = spread_bias(b_mid[...], lanes, 2)
     out[...] = build_out(w_out[...], hid)
@@ -417,11 +444,31 @@
 
 def x_windows(tiles):
     half = FACES // 2
-    return [split3(stack([turn(tile, -at, 0)[:FACES] for tile in tiles])) for at in (0, half)]
+    return [stack([turn(tile, -at, 0)[:FACES] for tile in tiles]) for at in (0, half)]
+
+
+def swap_halves(first, second):
+    half = FACES // 2
+    upper = rows_cols(first.shape)[0] < half
+    return jnp.where(upper, first, turn(second, half, 0)), jnp.where(upper, turn(first, half, 0), second)
+
+
+def y_windows(cells):
+    pairs = [swap_halves(cells[s][c], cells[s + 1][c]) for s in (0, 2) for c in range(4)]
+    return [stack([one[k] for one in pairs]) for k in range(2)]
+
+
+def y_unwindow(parts):
+    found = [[None] * 4 for _ in range(4)]
+    for s in (0, 2):
+        for c in range(4):
+            at = FACES * (2 * s + c)
+            found[s][c], found[s + 1][c] = swap_halves(parts[0][at : at + FACES], parts[1][at : at + FACES])
+    return found
 
 
 def x_forward(tiles, weights, hid):
-    h1, h1_pair, h2, h2_pair, gates = limiter_forward(x_windows(tiles), weights, hid)
+    h1, h1_pair, h2, h2_pair, gates = limiter_forward([split3(one) for one in x_windows(tiles)], weights, hid)
     cells = x_cells(tiles)
     return h1_pair, h2_pair, gates, face_flux(*edge_states(cells, gates))
 
@@ -474,8 +521,8 @@
 
 def y_step(cells, cots, halo_mask, refs, acc, hid):
     weights, out_back, mid_back, first_y_back = refs
-    window = split3(stack([cells[s][c] for s in range(4) for c in range(4)]))
-    h1, h1_pair, h2, h2_pair, gates = limiter_forward([window], weights, hid)
+    window = [split3(one) for one in y_windows(cells)]
+    h1, h1_pair, h2, h2_pair, gates = limiter_forward(window, weights, hid)
     left, right = edge_states(cells, gates)
     d_flux = [courant * (cots[1][c] - cots[0][c]) for c in range(4)]
     d_left, d_right = face_flux_backward(left, right, d_flux)
@@ -485,13 +532,11 @@
     d3_full, direct = edge_backward(cells, gates, d_left, d_right)
     d1_full = limiter_backward(d3_full, h1, h2, h1_pair, h2_pair, out_back, mid_back, acc, hid)
     d1 = split(d1_full)
-    d_window = dot(first_y_back[...], d1[0])
+    d_window = y_unwindow(first_backward(d1, first_y_back))
     if acc is not None:
         add_first_grads(window, d1, acc[0])
-        ny = acc[4].shape[1]
-        acc[4][...] += sum(d1_full[:, at : at + ny] for at in range(0, d1_full.shape[1], ny))
     return [
-        [d_window[FACES * (4 * s + c) : FACES * (4 * s + c + 1)] + direct[s][c] for c in range(4)]
+        [d_window[s][c] + direct[s][c] for c in range(4)]
         for s in range(4)
     ]
 
@@ -517,7 +562,7 @@
                 h1_hi, h1_lo, h2_hi, h2_lo, gates_in,
                 g_den, g_mom, g_tra, g_weights,
                 rim_state, rim_cot, rim_flux, rim_middle, rim_grad, d_middle,
-                acc_x, acc_y, acc_y_bias, acc_mid, acc_out, acc_out_bias):
+                acc_x, acc_y, acc_mid, acc_out, acc_out_bias):
     nx, ny = state.shape[1:]
     groups = nx // FACES
     half = groups // PAIR
@@ -528,7 +573,7 @@
     rim_groups = rim_rows // FACES
     rim_half = rim_groups // RIM_PAIR
 
-    for acc in (acc_x, acc_y, acc_y_bias, acc_mid, acc_out, acc_out_bias):
+    for acc in (acc_x, acc_y, acc_mid, acc_out, acc_out_bias):
         acc[...] = jnp.zeros(acc.shape, F32)
 
     lane = lane_index(ny)
@@ -635,7 +680,7 @@
                 cots[1][c].append(turn(low, -1, 1))
         cells = [y_order([side(one) for one in row]) for row in cells]
         cots = [y_order([side(one) for one in row]) for row in cots]
-        parts = y_step(cells, cots, None, refs, (acc_y, acc_mid, acc_out, acc_out_bias, acc_y_bias), hid)
+        parts = y_step(cells, cots, None, refs, (acc_y, acc_mid, acc_out, acc_out_bias), hid)
         for k in range(PAIR):
             group = step + k * half
             rows = row_block(group)
@@ -678,13 +723,16 @@
             d3_full, h1, h2, h1_pair, h2_pair, out_back, mid_back, (acc_x, acc_mid, acc_out, acc_out_bias), hid
         )
         d1 = split(d1_full)
-        d_window = dot(first_x_back[...], d1[0])
-        add_first_grads(split(stack(tiles)), d1, acc_x)
+        d_window = first_backward(d1, first_x_back)
+        add_first_grads([split(one) for one in x_windows(tiles)], d1, acc_x)
         later = []
         for c in range(4):
-            total = d_window[2 * FACES * c : 2 * FACES * (c + 1)]
-            for s in range(4):
-                total = total + turn(stack([direct[s][c], jnp.zeros_like(direct[s][c])]), s, 0)
+            rows = slice(FACES * c, FACES * (c + 1))
+            nothing = jnp.zeros_like(direct[0][c])
+            total = stack([direct[0][c] + d_window[0][rows], nothing])
+            total = total + turn(stack([d_window[1][rows], nothing]), FACES // 2, 0)
+            for s in range(1, 4):
+                total = total + turn(stack([direct[s][c], nothing]), s, 0)
             now = total[:FACES] + d_tiles[c][:FACES] + carry[c]
             for k in range(PAIR):
                 grads[c][row_block(step + k * half), :] = now[:, k * ny : (k + 1) * ny]
@@ -711,25 +759,28 @@
         acc_mid[8 * hid : 8 * hid + 8, :], pick((8 * hid, lanes), lambda q, n: rest(q, hid) == n, F32)
     )
     r, c = rows_cols(acc_x.shape)
-    face = rest(quot(r, hid), FACES)
-    values = acc_x[...]
-    found = [fold_rows(jnp.where((c & 15) - face == s, values, 0.0)[:, :128], hid) for s in range(4)]
-    found.append(fold_rows(values[:, 128:], hid))
-    found.append(fold_rows(jnp.where((c & 7) == face, acc_y[...], 0.0), hid))
-    found.append(fold_rows(acc_y_bias[...], hid))
-    found.append(fold_rows(jnp.where((c[:, :128] & 7) == face[:, :128], acc_out[...], 0.0), hid))
-    found = side(found)
+    values, shift = acc_x[...], (r & 7) - rest(quot(c, hid), 4)
+    found = [jnp.where((shift == s) & (r < 64), values, 0.0)[:64] for s in range(4)]
+    found.append(values[64:])
+    r, c = rows_cols(acc_y.shape)
+    found.append(jnp.where(((r & 3) == rest(quot(c, hid), 4)) | (r >= 128), acc_y[...], 0.0))
+    found = exact(
+        stack(found),
+        pick((8 * hid, lanes), lambda q, n: (rest(n - q, hid) == 0) & (n >= hid) & (n < 2 * hid), F32),
+    )
+    y_at = 4 * 64 + ONES
 
     def source(q, n):
-        block = n >> 7
-        in_x = (block < 4) & (q == 4 * block + ((n & 63) >> 4))
-        in_y = (block >= 5) & (block < 7) & (q == ((n & 127) >> 3))
-        in_bias = ((n == 512) | (block == 7)) & (q == 24)
-        in_out = (block == 8) & (q == 16 + ((n & 63) >> 3))
-        return in_x | in_y | in_bias | in_out
-
-    beside = exact_nt(
-        pick((32, found.shape[1]), source, F32),
+        in_x = (n < 256) & (q == 4 * (n >> 6) + ((n & 31) >> 3))
+        m = n - y_at
+        in_y = (m >= 0) & (m < 128) & (q == y_column(m & 63))
+        return in_x | in_y | ((n == 256) | (m == 128)) & (q == 24)
+
+    beside = exact(pick((32, found.shape[0]), source, F32), found)
+    r, c = rows_cols(acc_out.shape)
+    found = fold_rows(jnp.where((c & 7) == rest(quot(r, hid), FACES), acc_out[...], 0.0), hid)
+    beside = beside + exact_nt(
+        pick((32, found.shape[1]), lambda q, n: q == 16 + ((n & 63) >> 3), F32),
         stack([jnp.zeros((hid, found.shape[1]), F32), found, jnp.zeros((lanes - 2 * hid, found.shape[1]), F32)]),
     )
     out_bias_rows = exact_nt(jnp.ones((8, acc_out_bias.shape[1]), F32), acc_out_bias[...])
@@ -814,8 +865,8 @@
             shape((4, nx, ny), F32),
             shape((4, nx, ny), F32),
             shape((wide // 2, 6 * 32 + ONES), BF16),
-            shape((wide, 6 * 128), BF16),
-            shape((wide, ny), F32),
+            shape((wide, 4 * 64), BF16),
+            shape((wide // 2, ny), F32),
             shape((4 * hid, 8 * hid), BF16),
             shape((2 * hid, ny), F32),
             shape((192, wide), BF16),
@@ -861,9 +912,8 @@
             pltpu.VMEM((4, rim_rows, ny), F32),
             pltpu.VMEM((4, rim_rows, ny), F32),
             pltpu.VMEM((4, nx, ny), F32),
-            pltpu.VMEM((2 * wide, 256), F32),
-            pltpu.VMEM((2 * wide, 256), F32),
-            pltpu.VMEM((wide, ny), F32),
+            pltpu.VMEM((2 * 32 + ONES, wide), F32),
+            pltpu.VMEM((2 * 64 + ONES, wide), F32),
             pltpu.VMEM((8 * hid + ONES, 8 * hid), F32),
             pltpu.VMEM((2 * wide, 128), F32),
             pltpu.VMEM((64, lanes), F32),

time: 55.7 us -> 56.3 us (1.011)
  Pallas kernels: 34.1 us -> 34.7 us
where the time goes in v8:
time: 56.3 us; the launch traced here: 56 us
  Pallas kernels  34.7 us (62%)
  starting transfers between devices  14.5 us (26%)
  waiting for transfers between devices  6.19 us (11%)
  between operations  0.69 us (1%)
    pallas_call x4, Pallas kernels, call(): pl.pallas_call(kernel, out_shape=outs, in_specs=in_spaces or whole(len(op...  34.7 us
    ppermute x7, starting transfers between devices, sum_all(): lax.ppermute(values, axes, [(i, i ^ one) for i in range(size)])  7.94 us
    ppermute x2, starting transfers between devices, body(): lax.ppermute(one, axes, swap)  6.53 us
    ppermute x7, waiting for transfers between devices, sum_all(): lax.ppermute(values, axes, [(i, i ^ one) for i in range(size)])  6.18 us
  transfers between devices with their start and end apart: 9, of which 6 were waited for; matrix products, arithmetic and copies ran while one was open for 0% of the time, Pallas kernels for 9%

profile of v8, /device:TPU:0, one launch (start us, length us, event | category | flops | bytes accessed | tf_op | source)
XLA Modules:
  0.0 56.0 jit_solution(15106950637987236195)
XLA Ops:
  0.6 2.8 %shard_map.169 = (f32[8,32,128]{2,1,0:T(8,128)S(1)}, f32[8,8,128]{2,1,0:T(8,128)S(1)}, f32[8,8,128]{2,1,0:T(8,128)S(1)}, f32[4,256,128]{2,1,0:T(8,128)S(1)}, f32...) custom-call(f32[1,256,128]{2,1,0:T(8,128)} %den.1, ...), custom_call_target="tpu_custom_call" | custom-call | tf_op jit(solution)/shard_map/pallas_call | solution.py:810
  3.4 3.1 %collective-permute-start = (f32[8,8,128]{2,1,0:T(8,128)S(1)}, f32[8,8,128]{2,1,0:T(8,128)S(1)}, u32[]{:S(2)}, u32[]{:S(2)}) collective-permute-start(f32[8,8,128]{2,1,0:T(8,128)S(1)} %get-tuple-element.50), channel_id=1, source_target_pairs={{0,1},{1,0},{2,3},{3,2},{4,5},{5,4},{6,7},{7,6},{8,9},{9,8},{10,11... | collective-permute-start | bytes 98312 | tf_op jit(solution)/shard_map/ppermute | solution.py:886
  6.5 3.4 %collective-permute-start.1 = (f32[8,8,128]{2,1,0:T(8,128)S(1)}, f32[8,8,128]{2,1,0:T(8,128)S(1)}, u32[]{:S(2)}, u32[]{:S(2)}) collective-permute-start(f32[8,8,128]{2,1,0:T(8,128)S(1)} %get-tuple-element.51), channel_id=1, source_target_pairs={{0,7},{1,2},{2,1},{3,4},{4,3},{5,6},{6,5},{7,0},{8,15},{9,10},{10,... | collective-permute-start | bytes 98312 | tf_op jit(solution)/shard_map/ppermute | solution.py:886
  10.0 4.9 %shard_map.170 = (f32[4,256,128]{2,1,0:T(8,128)S(1)}, bf16[4,256,1024]{2,1,0:T(8,128)(2,1)S(1)}, bf16[4,256,1024]{2,1,0:T(8,128)(2,1)S(1)}, bf16[4,256,1024]{2,1...) custom-call(f32[4,256,128]{2,1,0:T(8,128)S(1)} %get-tuple-element.41.state, ...), custom_call_target="tpu_custom_call" | custom-call | flops 10000000000 | bytes 10000000 | tf_op jit(solution)/shard_map/pallas_call | solution.py:810
  14.9 0.0 collective-permute-done.from_first
  14.9 0.0 collective-permute-done.1.from_second
  14.9 26.3 %shard_map.171 = (f32[1,256,128]{2,1,0:T(8,128)}, f32[1,2,256,128]{3,2,1,0:T(8,128)}, f32[1,256,128]{2,1,0:T(8,128)}, f32[40,128]{1,0:T(8,128)S(1)}) custom-call(f32[4,256,128]{2,1,0:T(8,128)S(1)} %get-tuple-element.41.state, f32[4,256,128]{2,1,0:T(8,128)S(1)} %get-tuple-element.42.cot, f32[4,256,128]{2,1,0:T(8,128)S(1)} %get-tuple-element.48.middle, ...), custom_call_target="tpu_custom_call" | custom-call | flops 40000000000 | bytes 20000000 | tf_op jit(solution)/shard_map/pallas_call | solution.py:810
  41.2 0.0 collective-permute-start.2
  41.2 1.2 %collective-permute-done.2 = f32[40,128]{1,0:T(8,128)S(1)} collective-permute-done((f32[40,128]{1,0:T(8,128)S(1)}, f32[40,128]{1,0:T(8,128)S(1)}, u32[]{:S(2)}, u32[]{:S(2)}) %collective-permute-start.2) | collective-permute-done | bytes 20512 | tf_op jit(solution)/shard_map/ppermute | solution.py:836
  42.4 1.5 %collective-permute-start.5 = (f32[40,128]{1,0:T(8,128)S(1)}, f32[40,128]{1,0:T(8,128)S(1)}, u32[]{:S(2)}, u32[]{:S(2)}) collective-permute-start(f32[40,128]{1,0:T(8,128)S(1)} %add.21), channel_id=1, source_target_pairs={{0,20},{1,21},{2,22},{3,23},{4,16},{5,17},{6,18},{7,19},{8,28},{9,... | collective-permute-start | bytes 61448 | tf_op jit(solution)/shard_map/ppermute | solution.py:836
  43.9 1.5 %collective-permute-start.4 = (f32[40,128]{1,0:T(8,128)S(1)}, f32[40,128]{1,0:T(8,128)S(1)}, u32[]{:S(2)}, u32[]{:S(2)}) collective-permute-start(f32[40,128]{1,0:T(8,128)S(1)} %add.21), channel_id=1, source_target_pairs={{0,4},{1,5},{2,6},{3,7},{4,0},{5,1},{6,2},{7,3},{8,12},{9,13},{10,... | collective-permute-start | bytes 61448 | tf_op jit(solution)/shard_map/ppermute | solution.py:836
  45.4 0.5 collective-permute-start.3
  45.9 1.2 %collective-permute-done.5 = f32[40,128]{1,0:T(8,128)S(1)} collective-permute-done((f32[40,128]{1,0:T(8,128)S(1)}, f32[40,128]{1,0:T(8,128)S(1)}, u32[]{:S(2)}, u32[]{:S(2)}) %collective-permute-start.5) | collective-permute-done | bytes 20512 | tf_op jit(solution)/shard_map/ppermute | solution.py:836
  47.1 0.6 collective-permute-done.4
  47.7 1.5 %collective-permute-done.3 = f32[40,128]{1,0:T(8,128)S(1)} collective-permute-done((f32[40,128]{1,0:T(8,128)S(1)}, f32[40,128]{1,0:T(8,128)S(1)}, u32[]{:S(2)}, u32[]{:S(2)}) %collective-permute-start.3) | collective-permute-done | bytes 20512 | tf_op jit(solution)/shard_map/ppermute | solution.py:836
  49.1 1.4 %collective-permute-start.8 = (f32[40,128]{1,0:T(8,128)S(1)}, f32[40,128]{1,0:T(8,128)S(1)}, u32[]{:S(2)}, u32[]{:S(2)}) collective-permute-start(f32[40,128]{1,0:T(8,128)S(1)} %add_add_fusion.1), channel_id=1, source_target_pairs={{0,3},{1,2},{2,1},{3,0},{4,7},{5,6},{6,5},{7,4},{8,11},{9,10},{10,... | collective-permute-start | bytes 61448 | tf_op jit(solution)/shard_map/ppermute | solution.py:836
  50.6 0.0 collective-permute-start.7
  50.6 3.0 %collective-permute-start.6 = (f32[40,128]{1,0:T(8,128)S(1)}, f32[40,128]{1,0:T(8,128)S(1)}, u32[]{:S(2)}, u32[]{:S(2)}) collective-permute-start(f32[40,128]{1,0:T(8,128)S(1)} %add_add_fusion.1), channel_id=1, source_target_pairs={{0,2},{1,3},{2,0},{3,1},{4,6},{5,7},{6,4},{7,5},{8,10},{9,11},{10,... | collective-permute-start | bytes 61448 | tf_op jit(solution)/shard_map/ppermute | solution.py:836
  53.6 1.2 %collective-permute-done.8 = f32[40,128]{1,0:T(8,128)S(1)} collective-permute-done((f32[40,128]{1,0:T(8,128)S(1)}, f32[40,128]{1,0:T(8,128)S(1)}, u32[]{:S(2)}, u32[]{:S(2)}) %collective-permute-start.8) | collective-permute-done | bytes 20512 | tf_op jit(solution)/shard_map/ppermute | solution.py:836
  54.8 0.0 collective-permute-done.7
  54.8 0.6 %collective-permute-done.6 = f32[40,128]{1,0:T(8,128)S(1)} collective-permute-done((f32[40,128]{1,0:T(8,128)S(1)}, f32[40,128]{1,0:T(8,128)S(1)}, u32[]{:S(2)}, u32[]{:S(2)}) %collective-permute-start.6) | collective-permute-done | bytes 20512 | tf_op jit(solution)/shard_map/ppermute | solution.py:836
  55.4 0.7 %shard_map.172 = (f32[16,32]{1,0:T(8,128)}, f32[1,32]{1,0:T(1,128)}, f32[32,32]{1,0:T(8,128)}, f32[1,32]{1,0:T(1,128)}, f32[8,32]{1,0:T(8,128)}, /*index=5*/f32[1,8]{1,0:T(1,128)}) custom-call(f32[40,128]{1,0:T(8,128)S(1)} %add_add_fusion.total), custom_call_target="tpu_custom_call" | custom-call | tf_op jit(solution)/shard_map/pallas_call | solution.py:810
  (3 shorter events, 0.0 us)
Async XLA Ops:
  3.4 11.5 %collective-permute-start = (f32[8,8,128]{2,1,0:T(8,128)S(1)}, f32[8,8,128]{2,1,0:T(8,128)S(1)}, u32[]{:S(2)}, u32[]{:S(2)}) collective-permute-start(f32[8,8,128]{2,1,0:T(8,128)S(1)} %get-tuple-element.50), channel_id=1, source_target_pairs={{0,1},{1,0},{2,3},{3,2},{4,5},{5,4},{6,7},{7,6},{8,9},{9,8},{10,11... | collective-permute-start | bytes 98312 | tf_op jit(solution)/shard_map/ppermute | solution.py:886
  6.5 8.4 %collective-permute-start.1 = (f32[8,8,128]{2,1,0:T(8,128)S(1)}, f32[8,8,128]{2,1,0:T(8,128)S(1)}, u32[]{:S(2)}, u32[]{:S(2)}) collective-permute-start(f32[8,8,128]{2,1,0:T(8,128)S(1)} %get-tuple-element.51), channel_id=1, source_target_pairs={{0,7},{1,2},{2,1},{3,4},{4,3},{5,6},{6,5},{7,0},{8,15},{9,10},{10,... | collective-permute-start | bytes 98312 | tf_op jit(solution)/shard_map/ppermute | solution.py:886
  41.2 1.2 %collective-permute-start.2 = (f32[40,128]{1,0:T(8,128)S(1)}, f32[40,128]{1,0:T(8,128)S(1)}, u32[]{:S(2)}, u32[]{:S(2)}) collective-permute-start(f32[40,128]{1,0:T(8,128)S(1)} %get-tuple-element.66), channel_id=1, source_target_pairs={{0,8},{1,9},{2,10},{3,11},{4,12},{5,13},{6,14},{7,15},{8,0},{9,1},... | collective-permute-start | bytes 61448 | tf_op jit(solution)/shard_map/ppermute | solution.py:836
  42.4 4.7 %collective-permute-start.5 = (f32[40,128]{1,0:T(8,128)S(1)}, f32[40,128]{1,0:T(8,128)S(1)}, u32[]{:S(2)}, u32[]{:S(2)}) collective-permute-start(f32[40,128]{1,0:T(8,128)S(1)} %add.21), channel_id=1, source_target_pairs={{0,20},{1,21},{2,22},{3,23},{4,16},{5,17},{6,18},{7,19},{8,28},{9,... | collective-permute-start | bytes 61448 | tf_op jit(solution)/shard_map/ppermute | solution.py:836
  43.9 3.8 %collective-permute-start.4 = (f32[40,128]{1,0:T(8,128)S(1)}, f32[40,128]{1,0:T(8,128)S(1)}, u32[]{:S(2)}, u32[]{:S(2)}) collective-permute-start(f32[40,128]{1,0:T(8,128)S(1)} %add.21), channel_id=1, source_target_pairs={{0,4},{1,5},{2,6},{3,7},{4,0},{5,1},{6,2},{7,3},{8,12},{9,13},{10,... | collective-permute-start | bytes 61448 | tf_op jit(solution)/shard_map/ppermute | solution.py:836
  45.4 3.8 %collective-permute-start.3 = (f32[40,128]{1,0:T(8,128)S(1)}, f32[40,128]{1,0:T(8,128)S(1)}, u32[]{:S(2)}, u32[]{:S(2)}) collective-permute-start(f32[40,128]{1,0:T(8,128)S(1)} %add.21), channel_id=1, source_target_pairs={{0,16},{1,17},{2,18},{3,19},{4,20},{5,21},{6,22},{7,23},{8,24},{9,... | collective-permute-start | bytes 61448 | tf_op jit(solution)/shard_map/ppermute | solution.py:836
  49.1 5.6 %collective-permute-start.8 = (f32[40,128]{1,0:T(8,128)S(1)}, f32[40,128]{1,0:T(8,128)S(1)}, u32[]{:S(2)}, u32[]{:S(2)}) collective-permute-start(f32[40,128]{1,0:T(8,128)S(1)} %add_add_fusion.1), channel_id=1, source_target_pairs={{0,3},{1,2},{2,1},{3,0},{4,7},{5,6},{6,5},{7,4},{8,11},{9,10},{10,... | collective-permute-start | bytes 61448 | tf_op jit(solution)/shard_map/ppermute | solution.py:836
  50.6 4.2 %collective-permute-start.7 = (f32[40,128]{1,0:T(8,128)S(1)}, f32[40,128]{1,0:T(8,128)S(1)}, u32[]{:S(2)}, u32[]{:S(2)}) collective-permute-start(f32[40,128]{1,0:T(8,128)S(1)} %add_add_fusion.1), channel_id=1, source_target_pairs={{0,1},{1,0},{2,3},{3,2},{4,5},{5,4},{6,7},{7,6},{8,9},{9,8},{10,11... | collective-permute-start | bytes 61448 | tf_op jit(solution)/shard_map/ppermute | solution.py:836
  50.6 4.8 %collective-permute-start.6 = (f32[40,128]{1,0:T(8,128)S(1)}, f32[40,128]{1,0:T(8,128)S(1)}, u32[]{:S(2)}, u32[]{:S(2)}) collective-permute-start(f32[40,128]{1,0:T(8,128)S(1)} %add_add_fusion.1), channel_id=1, source_target_pairs={{0,2},{1,3},{2,0},{3,1},{4,6},{5,7},{6,4},{7,5},{8,10},{9,11},{10,... | collective-permute-start | bytes 61448 | tf_op jit(solution)/shard_map/ppermute | solution.py:836

commit v9 on v8

--- a/solution.py
+++ b/solution.py
@@ -558,9 +558,9 @@
 
 def back_kernel(state, cot, middle, own, from_first, from_second,
                 first_x, first_y, first_bias, mid, mid_bias, out, out_bias,
-                out_back, mid_back, first_x_back, first_y_back,
+                out_back, mid_back, first_y_back,
                 h1_hi, h1_lo, h2_hi, h2_lo, gates_in,
-                g_den, g_mom, g_tra, g_weights,
+                base, d1_hi, d1_lo, g_weights,
                 rim_state, rim_cot, rim_flux, rim_middle, rim_grad, d_middle,
                 acc_x, acc_y, acc_mid, acc_out, acc_out_bias):
     nx, ny = state.shape[1:]
@@ -703,7 +703,6 @@
     lax.fori_loop(0, half, main_y, 0)
 
     planes = [state.at[c] for c in range(4)]
-    grads = [g_den.at[0], g_mom.at[0, 0], g_mom.at[0, 1], g_tra.at[0]]
     d_planes = [d_middle.at[c] for c in range(4)]
 
     def main_x(step, carry):
@@ -723,19 +722,17 @@
             d3_full, h1, h2, h1_pair, h2_pair, out_back, mid_back, (acc_x, acc_mid, acc_out, acc_out_bias), hid
         )
         d1 = split(d1_full)
-        d_window = first_backward(d1, first_x_back)
+        d1_hi[step], d1_lo[step] = d1
         add_first_grads([split(one) for one in x_windows(tiles)], d1, acc_x)
         later = []
         for c in range(4):
-            rows = slice(FACES * c, FACES * (c + 1))
             nothing = jnp.zeros_like(direct[0][c])
-            total = stack([direct[0][c] + d_window[0][rows], nothing])
-            total = total + turn(stack([d_window[1][rows], nothing]), FACES // 2, 0)
+            total = stack([direct[0][c], nothing])
             for s in range(1, 4):
                 total = total + turn(stack([direct[s][c], nothing]), s, 0)
             now = total[:FACES] + d_tiles[c][:FACES] + carry[c]
             for k in range(PAIR):
-                grads[c][row_block(step + k * half), :] = now[:, k * ny : (k + 1) * ny]
+                base[c, row_block(step + k * half), :] = now[:, k * ny : (k + 1) * ny]
             later.append(total[FACES:])
         return tuple(later)
 
@@ -744,7 +741,7 @@
     for c in range(4):
         for k in range(PAIR):
             at = (k + 1) % PAIR * half * FACES
-            grads[c][pl.ds(at, FACES), :] += last[c][:, k * ny : (k + 1) * ny]
+            base[c, pl.ds(at, FACES), :] += last[c][:, k * ny : (k + 1) * ny]
 
     lanes = g_weights.shape[1]
     values = acc_mid[: 8 * hid, :]
@@ -789,6 +786,33 @@
     g_weights[:hid, :] = grad_mid + beside
     g_weights[25:26, :] += grad_out_bias[:1]
     g_weights[hid:, :] = grad_mid_bias
+
+
+def state_kernel(base, d1_hi, d1_lo, first_x_back, _, g_den, g_mom, g_tra):
+    nx, ny = base.shape[1:]
+    half = nx // FACES // PAIR
+    grads = [g_den.at[0], g_mom.at[0, 0], g_mom.at[0, 1], g_tra.at[0]]
+    upper = rows_cols((FACES, PAIR * ny))[0] < FACES // 2
+
+    def step_of(step, carry):
+        first, second = first_backward((d1_hi[step], d1_lo[step]), first_x_back)
+        later = []
+        for c in range(4):
+            rows = slice(FACES * c, FACES * (c + 1))
+            moved = turn(second[rows], FACES // 2, 0)
+            now = first[rows] + jnp.where(upper, 0.0, moved) + carry[c]
+            for k in range(PAIR):
+                at = row_block(step + k * half)
+                grads[c][at, :] = base[c, at, :] + now[:, k * ny : (k + 1) * ny]
+            later.append(jnp.where(upper, moved, 0.0))
+        return tuple(later)
+
+    start = tuple(jnp.zeros((FACES, PAIR * ny), F32) for _ in range(4))
+    last = lax.fori_loop(0, half, step_of, start)
+    for c in range(4):
+        for k in range(PAIR):
+            at = (k + 1) % PAIR * half * FACES
+            grads[c][pl.ds(at, FACES), :] += last[c][:, k * ny : (k + 1) * ny]
 
 
 def finish_kernel(total, g_w_in, g_b_in, g_w_mid, g_b_mid, g_w_out, g_b_out):
@@ -818,17 +842,17 @@
     )(*operands)
 
 
-def sum_all(values, sizes):
+def sum_rounds(values, sizes):
     axes, size = tuple(sizes), 1
     for one in sizes.values():
         size *= one
     if size & (size - 1):
-        return lax.psum(values, axes)
+        return [values, lax.psum(values, axes)]
     bits = [1 << k for k in range(size.bit_length() - 1)]
     core = size // sizes["traj"]
     others = [bit for bit in reversed(bits) if bit != core]
-    rounds = [[core]] * (core in bits) + [others[k : k + 2] for k in range(0, len(others), 2)]
-    for masks in rounds:
+    found = [values]
+    for masks in [[core]] * (core in bits) + [others[k : k + 2] for k in range(0, len(others), 2)]:
         partners = [0]
         for mask in masks:
             partners = partners + [one ^ mask for one in partners]
@@ -838,7 +862,8 @@
         while len(parts) > 1:
             parts = [parts[k] + parts[k + 1] for k in range(0, len(parts), 2)]
         values = parts[0]
-    return values
+        found.append(values)
+    return found
 
 
 def body(sizes, density, momentum, tracer, cotangent, w_in, b_in, w_mid, b_mid, w_out, b_out):
@@ -896,12 +921,13 @@
         flops=10**10,
         moved=10**7,
     )
-    g_den, g_mom, g_tra, g_weights = call(
+    first_x_back = matrices.pop(-2)
+    *found, g_weights = call(
         back_kernel,
         [
-            shape(density.shape, F32),
-            shape(momentum.shape, F32),
-            shape(tracer.shape, F32),
+            shape((4, nx, ny), F32),
+            shape((half, wide, lanes), BF16),
+            shape((half, wide, lanes), BF16),
             shape((hid + 8, 128), F32),
         ],
         [state, cots, middle, rim, from_first, from_second] + matrices + kept,
@@ -921,7 +947,15 @@
         flops=4 * 10**10,
         moved=2 * 10**7,
     )
-    total = sum_all(g_weights, sizes)
+    rounds = sum_rounds(g_weights, sizes)
+    g_den, g_mom, g_tra = call(
+        state_kernel,
+        [shape(density.shape, F32), shape(momentum.shape, F32), shape(tracer.shape, F32)],
+        found + [first_x_back, rounds[min(1, len(rounds) - 1)]],
+        flops=2 * 10**9,
+        moved=10**6,
+    )
+    total = rounds[-1]
     g_w_in, g_b_in, g_w_mid, g_b_mid, g_w_out, g_b_out = call(
         finish_kernel,
         [

time: 56.3 us -> 54.8 us (0.973)
  waiting for transfers between devices: 6.19 us -> 4.44 us
    ppermute x7, waiting for transfers between devices: 6.18 us -> 4.43 us  [sum_rounds(): lax.ppermute(values, axes, [(i, i ^ one) for i in range(size)])]
    pallas_call x4 -> x5, Pallas kernels: 34.7 us -> 35 us  [call(): pl.pallas_call(kernel, out_shape=outs, in_specs=in_spaces or whole(len(op...]
  transfers between devices with their start and end apart: 9 -> 9, of which waited for: 6 -> 4; matrix products, arithmetic and copies ran while one was open for 0% -> 0% of each run, Pallas kernels for 9% -> 13%
where the time goes in v9:
time: 54.8 us; the launch traced here: 54.6 us
  Pallas kernels  35 us (64%)
  starting transfers between devices  14.5 us (26%)
  waiting for transfers between devices  4.44 us (8%)
  between operations  0.71 us (1%)
    pallas_call x5, Pallas kernels, call(): pl.pallas_call(kernel, out_shape=outs, in_specs=in_spaces or whole(len(op...  35 us
    ppermute x7, starting transfers between devices, sum_rounds(): lax.ppermute(values, axes, [(i, i ^ one) for i in range(size)])  7.95 us
    ppermute x2, starting transfers between devices, body(): lax.ppermute(one, axes, swap)  6.53 us
    ppermute x7, waiting for transfers between devices, sum_rounds(): lax.ppermute(values, axes, [(i, i ^ one) for i in range(size)])  4.43 us
  transfers between devices with their start and end apart: 9, of which 4 were waited for; matrix products, arithmetic and copies ran while one was open for 0% of the time, Pallas kernels for 13%

profile of v9, /device:TPU:0, one launch (start us, length us, event | category | flops | bytes accessed | tf_op | source)
XLA Modules:
  0.0 54.6 jit_solution(9123346007659650482)
XLA Ops:
  0.6 2.8 %shard_map.169 = (f32[8,32,128]{2,1,0:T(8,128)S(1)}, f32[8,8,128]{2,1,0:T(8,128)S(1)}, f32[8,8,128]{2,1,0:T(8,128)S(1)}, f32[4,256,128]{2,1,0:T(8,128)S(1)}, f32...) custom-call(f32[1,256,128]{2,1,0:T(8,128)} %den.1, ...), custom_call_target="tpu_custom_call" | custom-call | tf_op jit(solution)/shard_map/pallas_call | solution.py:834
  3.4 3.1 %collective-permute-start = (f32[8,8,128]{2,1,0:T(8,128)S(1)}, f32[8,8,128]{2,1,0:T(8,128)S(1)}, u32[]{:S(2)}, u32[]{:S(2)}) collective-permute-start(f32[8,8,128]{2,1,0:T(8,128)S(1)} %get-tuple-element.53), channel_id=1, source_target_pairs={{0,1},{1,0},{2,3},{3,2},{4,5},{5,4},{6,7},{7,6},{8,9},{9,8},{10,11... | collective-permute-start | bytes 98312 | tf_op jit(solution)/shard_map/ppermute | solution.py:911
  6.5 3.4 %collective-permute-start.1 = (f32[8,8,128]{2,1,0:T(8,128)S(1)}, f32[8,8,128]{2,1,0:T(8,128)S(1)}, u32[]{:S(2)}, u32[]{:S(2)}) collective-permute-start(f32[8,8,128]{2,1,0:T(8,128)S(1)} %get-tuple-element.54), channel_id=1, source_target_pairs={{0,7},{1,2},{2,1},{3,4},{4,3},{5,6},{6,5},{7,0},{8,15},{9,10},{10,... | collective-permute-start | bytes 98312 | tf_op jit(solution)/shard_map/ppermute | solution.py:911
  10.0 4.9 %shard_map.170 = (f32[4,256,128]{2,1,0:T(8,128)S(1)}, bf16[4,256,1024]{2,1,0:T(8,128)(2,1)S(1)}, bf16[4,256,1024]{2,1,0:T(8,128)(2,1)S(1)}, bf16[4,256,1024]{2,1...) custom-call(f32[4,256,128]{2,1,0:T(8,128)S(1)} %get-tuple-element.44.state, ...), custom_call_target="tpu_custom_call" | custom-call | flops 10000000000 | bytes 10000000 | tf_op jit(solution)/shard_map/pallas_call | solution.py:834
  14.9 0.0 collective-permute-done.from_first
  14.9 0.0 collective-permute-done.1.from_second
  14.9 24.5 %shard_map.171 = (f32[4,256,128]{2,1,0:T(8,128)S(1)}, bf16[4,256,1024]{2,1,0:T(8,128)(2,1)S(1)}, bf16[4,256,1024]{2,1,0:T(8,128)(2,1)S(1)}, f32[40,128]{1,0:T(8,128)S(1)}) custom-call(f32[4,256,128]{2,1,0:T(8,128)S(1)} %get-tuple-element.44.state, f32[4,256,128]{2,1,0:T(8,128)S(1)} %get-tuple-element.45.cot, f32[4,256,128]{2,1,0:T(8,128)S(1)} %get-tuple-element.51.middle, ...), custom_call_target="tpu_custom_call" | custom-call | flops 40000000000 | bytes 20000000 | tf_op jit(solution)/shard_map/pallas_call | solution.py:834
  39.4 0.0 collective-permute-start.2
  39.4 1.2 %collective-permute-done.2 = f32[40,128]{1,0:T(8,128)S(1)} collective-permute-done((f32[40,128]{1,0:T(8,128)S(1)}, f32[40,128]{1,0:T(8,128)S(1)}, u32[]{:S(2)}, u32[]{:S(2)}) %collective-permute-start.2) | collective-permute-done | bytes 20512 | tf_op jit(solution)/shard_map/ppermute | solution.py:860
  40.6 1.5 %collective-permute-start.5 = (f32[40,128]{1,0:T(8,128)S(1)}, f32[40,128]{1,0:T(8,128)S(1)}, u32[]{:S(2)}, u32[]{:S(2)}) collective-permute-start(f32[40,128]{1,0:T(8,128)S(1)} %add.21._), channel_id=1, source_target_pairs={{0,20},{1,21},{2,22},{3,23},{4,16},{5,17},{6,18},{7,19},{8,28},{9,... | collective-permute-start | bytes 61448 | tf_op jit(solution)/shard_map/ppermute | solution.py:860
  42.1 1.5 %collective-permute-start.4 = (f32[40,128]{1,0:T(8,128)S(1)}, f32[40,128]{1,0:T(8,128)S(1)}, u32[]{:S(2)}, u32[]{:S(2)}) collective-permute-start(f32[40,128]{1,0:T(8,128)S(1)} %add.21._), channel_id=1, source_target_pairs={{0,4},{1,5},{2,6},{3,7},{4,0},{5,1},{6,2},{7,3},{8,12},{9,13},{10,... | collective-permute-start | bytes 61448 | tf_op jit(solution)/shard_map/ppermute | solution.py:860
  43.6 0.5 collective-permute-start.3
  44.1 1.2 %collective-permute-done.5 = f32[40,128]{1,0:T(8,128)S(1)} collective-permute-done((f32[40,128]{1,0:T(8,128)S(1)}, f32[40,128]{1,0:T(8,128)S(1)}, u32[]{:S(2)}, u32[]{:S(2)}) %collective-permute-start.5) | collective-permute-done | bytes 20512 | tf_op jit(solution)/shard_map/ppermute | solution.py:860
  45.3 0.6 %collective-permute-done.4 = f32[40,128]{1,0:T(8,128)S(1)} collective-permute-done((f32[40,128]{1,0:T(8,128)S(1)}, f32[40,128]{1,0:T(8,128)S(1)}, u32[]{:S(2)}, u32[]{:S(2)}) %collective-permute-start.4) | collective-permute-done | bytes 20512 | tf_op jit(solution)/shard_map/ppermute | solution.py:860
  45.9 1.5 %collective-permute-done.3 = f32[40,128]{1,0:T(8,128)S(1)} collective-permute-done((f32[40,128]{1,0:T(8,128)S(1)}, f32[40,128]{1,0:T(8,128)S(1)}, u32[]{:S(2)}, u32[]{:S(2)}) %collective-permute-start.3) | collective-permute-done | bytes 20512 | tf_op jit(solution)/shard_map/ppermute | solution.py:860
  47.4 1.4 %collective-permute-start.8 = (f32[40,128]{1,0:T(8,128)S(1)}, f32[40,128]{1,0:T(8,128)S(1)}, u32[]{:S(2)}, u32[]{:S(2)}) collective-permute-start(f32[40,128]{1,0:T(8,128)S(1)} %add_add_fusion.1), channel_id=1, source_target_pairs={{0,3},{1,2},{2,1},{3,0},{4,7},{5,6},{6,5},{7,4},{8,11},{9,10},{10,... | collective-permute-start | bytes 61448 | tf_op jit(solution)/shard_map/ppermute | solution.py:860
  48.8 0.0 collective-permute-start.7
  48.8 3.0 %collective-permute-start.6 = (f32[40,128]{1,0:T(8,128)S(1)}, f32[40,128]{1,0:T(8,128)S(1)}, u32[]{:S(2)}, u32[]{:S(2)}) collective-permute-start(f32[40,128]{1,0:T(8,128)S(1)} %add_add_fusion.1), channel_id=1, source_target_pairs={{0,2},{1,3},{2,0},{3,1},{4,6},{5,7},{6,4},{7,5},{8,10},{9,11},{10,... | collective-permute-start | bytes 61448 | tf_op jit(solution)/shard_map/ppermute | solution.py:860
  51.8 2.1 %shard_map.172 = (f32[1,256,128]{2,1,0:T(8,128)}, f32[1,2,256,128]{3,2,1,0:T(8,128)}, f32[1,256,128]{2,1,0:T(8,128)}) custom-call(f32[4,256,128]{2,1,0:T(8,128)S(1)} %get-tuple-element.65.base, bf16[4,256,1024]{2,1,0:T(8,128)(2,1)S(1)} %get-tuple-element.66.d1_hi, bf16[4,256,1024]{2,1,0:T(8,128)(2,1)S(1)} %get-tuple-element.67.d1_lo, ...), custom_call_target="tpu_custom_call" | custom-call | flops 2000000000 | bytes 1000000 | tf_op jit(solution)/shard_map/pallas_call | solution.py:834
  53.9 0.0 collective-permute-done.8
  53.9 0.0 collective-permute-done.7
  53.9 0.0 collective-permute-done.6
  53.9 0.7 %shard_map.173 = (f32[16,32]{1,0:T(8,128)}, f32[1,32]{1,0:T(1,128)}, f32[32,32]{1,0:T(8,128)}, f32[1,32]{1,0:T(1,128)}, f32[8,32]{1,0:T(8,128)}, /*index=5*/f32[1,8]{1,0:T(1,128)}) custom-call(f32[40,128]{1,0:T(8,128)S(1)} %add_add_fusion.total), custom_call_target="tpu_custom_call" | custom-call | tf_op jit(solution)/shard_map/pallas_call | solution.py:834
  (3 shorter events, 0.0 us)
Async XLA Ops:
  3.4 11.5 %collective-permute-start = (f32[8,8,128]{2,1,0:T(8,128)S(1)}, f32[8,8,128]{2,1,0:T(8,128)S(1)}, u32[]{:S(2)}, u32[]{:S(2)}) collective-permute-start(f32[8,8,128]{2,1,0:T(8,128)S(1)} %get-tuple-element.53), channel_id=1, source_target_pairs={{0,1},{1,0},{2,3},{3,2},{4,5},{5,4},{6,7},{7,6},{8,9},{9,8},{10,11... | collective-permute-start | bytes 98312 | tf_op jit(solution)/shard_map/ppermute | solution.py:911
  6.5 8.4 %collective-permute-start.1 = (f32[8,8,128]{2,1,0:T(8,128)S(1)}, f32[8,8,128]{2,1,0:T(8,128)S(1)}, u32[]{:S(2)}, u32[]{:S(2)}) collective-permute-start(f32[8,8,128]{2,1,0:T(8,128)S(1)} %get-tuple-element.54), channel_id=1, source_target_pairs={{0,7},{1,2},{2,1},{3,4},{4,3},{5,6},{6,5},{7,0},{8,15},{9,10},{10,... | collective-permute-start | bytes 98312 | tf_op jit(solution)/shard_map/ppermute | solution.py:911
  39.4 1.2 %collective-permute-start.2 = (f32[40,128]{1,0:T(8,128)S(1)}, f32[40,128]{1,0:T(8,128)S(1)}, u32[]{:S(2)}, u32[]{:S(2)}) collective-permute-start(f32[40,128]{1,0:T(8,128)S(1)} %get-tuple-element.69), channel_id=1, source_target_pairs={{0,8},{1,9},{2,10},{3,11},{4,12},{5,13},{6,14},{7,15},{8,0},{9,1},... | collective-permute-start | bytes 61448 | tf_op jit(solution)/shard_map/ppermute | solution.py:860
  40.6 4.7 %collective-permute-start.5 = (f32[40,128]{1,0:T(8,128)S(1)}, f32[40,128]{1,0:T(8,128)S(1)}, u32[]{:S(2)}, u32[]{:S(2)}) collective-permute-start(f32[40,128]{1,0:T(8,128)S(1)} %add.21._), channel_id=1, source_target_pairs={{0,20},{1,21},{2,22},{3,23},{4,16},{5,17},{6,18},{7,19},{8,28},{9,... | collective-permute-start | bytes 61448 | tf_op jit(solution)/shard_map/ppermute | solution.py:860
  42.1 3.8 %collective-permute-start.4 = (f32[40,128]{1,0:T(8,128)S(1)}, f32[40,128]{1,0:T(8,128)S(1)}, u32[]{:S(2)}, u32[]{:S(2)}) collective-permute-start(f32[40,128]{1,0:T(8,128)S(1)} %add.21._), channel_id=1, source_target_pairs={{0,4},{1,5},{2,6},{3,7},{4,0},{5,1},{6,2},{7,3},{8,12},{9,13},{10,... | collective-permute-start | bytes 61448 | tf_op jit(solution)/shard_map/ppermute | solution.py:860
  43.6 3.8 %collective-permute-start.3 = (f32[40,128]{1,0:T(8,128)S(1)}, f32[40,128]{1,0:T(8,128)S(1)}, u32[]{:S(2)}, u32[]{:S(2)}) collective-permute-start(f32[40,128]{1,0:T(8,128)S(1)} %add.21._), channel_id=1, source_target_pairs={{0,16},{1,17},{2,18},{3,19},{4,20},{5,21},{6,22},{7,23},{8,24},{9,... | collective-permute-start | bytes 61448 | tf_op jit(solution)/shard_map/ppermute | solution.py:860
  47.4 6.5 %collective-permute-start.8 = (f32[40,128]{1,0:T(8,128)S(1)}, f32[40,128]{1,0:T(8,128)S(1)}, u32[]{:S(2)}, u32[]{:S(2)}) collective-permute-start(f32[40,128]{1,0:T(8,128)S(1)} %add_add_fusion.1), channel_id=1, source_target_pairs={{0,3},{1,2},{2,1},{3,0},{4,7},{5,6},{6,5},{7,4},{8,11},{9,10},{10,... | collective-permute-start | bytes 61448 | tf_op jit(solution)/shard_map/ppermute | solution.py:860
  48.8 5.1 %collective-permute-start.7 = (f32[40,128]{1,0:T(8,128)S(1)}, f32[40,128]{1,0:T(8,128)S(1)}, u32[]{:S(2)}, u32[]{:S(2)}) collective-permute-start(f32[40,128]{1,0:T(8,128)S(1)} %add_add_fusion.1), channel_id=1, source_target_pairs={{0,1},{1,0},{2,3},{3,2},{4,5},{5,4},{6,7},{7,6},{8,9},{9,8},{10,11... | collective-permute-start | bytes 61448 | tf_op jit(solution)/shard_map/ppermute | solution.py:860
  48.8 5.1 %collective-permute-start.6 = (f32[40,128]{1,0:T(8,128)S(1)}, f32[40,128]{1,0:T(8,128)S(1)}, u32[]{:S(2)}, u32[]{:S(2)}) collective-permute-start(f32[40,128]{1,0:T(8,128)S(1)} %add_add_fusion.1), channel_id=1, source_target_pairs={{0,2},{1,3},{2,0},{3,1},{4,6},{5,7},{6,4},{7,5},{8,10},{9,11},{10,... | collective-permute-start | bytes 61448 | tf_op jit(solution)/shard_map/ppermute | solution.py:860

commit v10 on v9

--- a/solution.py
+++ b/solution.py
@@ -244,13 +244,13 @@
     return h1, h1_parts[:2], h2, h2_parts[:2], gates
 
 
-def limiter_backward(d3, h1, h2, h1_pair, h2_pair, out_back_ref, mid_back_ref, acc, hid):
+def limiter_backward(d3, slope1, slope2, h1_pair, h2_pair, out_back_ref, mid_back_ref, acc, hid):
     d3_hi, d3_lo = split(d3)
     dh2 = dot(out_back_ref[...], stack([d3_hi, d3_hi, d3_lo]))
     if acc is not None:
         acc[2][...] += dot_nt(stack(list(h2_pair)), stack([d3_hi, d3_lo]))
         acc[3][...] += d3
-    d2_hi, d2_lo = split(dh2 * (1.0 - h2 * h2))
+    d2_hi, d2_lo = split(dh2 * slope2)
     block = 2 * hid
     parts = []
     for at in range(0, FACES * hid, block):
@@ -263,7 +263,7 @@
             lefts.append(stack([part[at : at + 2 * block] for part in h1_pair] + [ones]))
             rights.append(stack([part[at : at + 2 * block] for part in (d2_hi, d2_lo)]))
         acc[1][...] += dot_nt(side(lefts), side(rights))
-    return stack(parts) * (1.0 - h1 * h1)
+    return stack(parts) * slope1
 
 
 def first_backward(d1, back_ref):
@@ -470,7 +470,7 @@
 def x_forward(tiles, weights, hid):
     h1, h1_pair, h2, h2_pair, gates = limiter_forward([split3(one) for one in x_windows(tiles)], weights, hid)
     cells = x_cells(tiles)
-    return h1_pair, h2_pair, gates, face_flux(*edge_states(cells, gates))
+    return h1, h2, h1_pair, h2_pair, gates, face_flux(*edge_states(cells, gates))
 
 
 def update_cells(plane_rows, flux_rows):
@@ -480,7 +480,7 @@
 
 
 def x_forward_kernel(state, first_x, mid, mid_bias, out, out_bias,
-                     middle, h1_hi, h1_lo, h2_hi, h2_lo, gates_out, flux):
+                     middle, h1_hi, h1_lo, h2_hi, h2_lo, slope1, gates_out, flux):
     nx, ny = state.shape[1:]
     groups = nx // FACES
     half = groups // PAIR
@@ -490,9 +490,10 @@
 
     def step_of(step, _):
         tiles = pair_tiles(planes, step, half)
-        h1_pair, h2_pair, gates, fluxes = x_forward(tiles, x_weights, hid)
+        h1, h2, h1_pair, h2_pair, gates, fluxes = x_forward(tiles, x_weights, hid)
         for target, value in zip((h1_hi, h1_lo, h2_hi, h2_lo, gates_out), h1_pair + h2_pair + (gates,)):
             target[step] = value
+        slope1[step] = 1.0 - h1 * h1
         for c in range(4):
             for k in range(PAIR):
                 flux[c, row_block(step + k * half + 1), :] = fluxes[c][:, k * ny : (k + 1) * ny]
@@ -508,7 +509,7 @@
             middle[c, row_block(group), :] = update_cells(planes[c][row_block(group), :], both)
         return 0
 
-    lax.fori_loop(0, groups, update, 0)
+    lax.fori_loop(0, groups, update, 0, unroll=4)
 
 
 def y_order(planes):
@@ -530,7 +531,9 @@
         d_left = [jnp.where(halo_mask, d, 0.0) for d in d_left]
         d_right = [jnp.where(halo_mask, d, 0.0) for d in d_right]
     d3_full, direct = edge_backward(cells, gates, d_left, d_right)
-    d1_full = limiter_backward(d3_full, h1, h2, h1_pair, h2_pair, out_back, mid_back, acc, hid)
+    d1_full = limiter_backward(
+        d3_full, 1.0 - h1 * h1, 1.0 - h2 * h2, h1_pair, h2_pair, out_back, mid_back, acc, hid
+    )
     d1 = split(d1_full)
     d_window = y_unwindow(first_backward(d1, first_y_back))
     if acc is not None:
@@ -559,7 +562,7 @@
 def back_kernel(state, cot, middle, own, from_first, from_second,
                 first_x, first_y, first_bias, mid, mid_bias, out, out_bias,
                 out_back, mid_back, first_y_back,
-                h1_hi, h1_lo, h2_hi, h2_lo, gates_in,
+                h1_hi, h1_lo, h2_hi, h2_lo, slope1, gates_in,
                 base, d1_hi, d1_lo, g_weights,
                 rim_state, rim_cot, rim_flux, rim_middle, rim_grad, d_middle,
                 acc_x, acc_y, acc_mid, acc_out, acc_out_bias):
@@ -612,7 +615,7 @@
             for k in range(RIM_PAIR)
         ]
         tiles = [side([one[c] for one in sets]) for c in range(4)]
-        fluxes = x_forward(tiles, x_weights, hid)[3]
+        fluxes = x_forward(tiles, x_weights, hid)[-1]
         for c in range(4):
             for k in range(RIM_PAIR):
                 rim_flux[c, row_block(step + k * rim_half + 1), :] = fluxes[c][:, k * ny : (k + 1) * ny]
@@ -711,7 +714,6 @@
         gates = gates_in[step]
         h1_pair = (h1_hi[step], h1_lo[step])
         h2_pair = (h2_hi[step], h2_lo[step])
-        h1 = h1_pair[0].astype(F32) + h1_pair[1].astype(F32)
         h2 = h2_pair[0].astype(F32) + h2_pair[1].astype(F32)
         cells = x_cells(tiles)
         left, right = edge_states(cells, gates)
@@ -719,7 +721,7 @@
         d_left, d_right = face_flux_backward(left, right, d_flux)
         d3_full, direct = edge_backward(cells, gates, d_left, d_right)
         d1_full = limiter_backward(
-            d3_full, h1, h2, h1_pair, h2_pair, out_back, mid_back, (acc_x, acc_mid, acc_out, acc_out_bias), hid
+            d3_full, slope1[step], 1.0 - h2 * h2, h1_pair, h2_pair, out_back, mid_back, (acc_x, acc_mid, acc_out, acc_out_bias), hid
         )
         d1 = split(d1_full)
         d1_hi[step], d1_lo[step] = d1
@@ -915,6 +917,7 @@
         x_forward_kernel,
         [shape((4, nx, ny), F32)]
         + [shape((half, wide, lanes), BF16)] * 4
+        + [shape((half, wide, lanes), F32)]
         + [shape((half, 64, lanes), F32)],
         [state, matrices[0]] + matrices[3:7],
         scratch=[pltpu.VMEM((4, nx + FACES, ny), F32)],

time: 54.8 us -> 55.1 us (level)
  no operation moved by 1% of the time
where the time goes in v10:
time: 55.1 us; the launch traced here: 54.8 us
  Pallas kernels  35.2 us (64%)
  starting transfers between devices  14.5 us (26%)
  waiting for transfers between devices  4.45 us (8%)
  between operations  0.71 us (1%)
    pallas_call x5, Pallas kernels, call(): pl.pallas_call(kernel, out_shape=outs, in_specs=in_spaces or whole(len(op...  35.2 us
    ppermute x7, starting transfers between devices, sum_rounds(): lax.ppermute(values, axes, [(i, i ^ one) for i in range(size)])  7.95 us
    ppermute x2, starting transfers between devices, body(): lax.ppermute(one, axes, swap)  6.53 us
    ppermute x7, waiting for transfers between devices, sum_rounds(): lax.ppermute(values, axes, [(i, i ^ one) for i in range(size)])  4.44 us
  transfers between devices with their start and end apart: 9, of which 4 were waited for; matrix products, arithmetic and copies ran while one was open for 0% of the time, Pallas kernels for 13%

profile of v10, /device:TPU:0, one launch (start us, length us, event | category | flops | bytes accessed | tf_op | source)
XLA Modules:
  0.0 54.8 jit_solution(16838369038918403767)
XLA Ops:
  0.6 2.8 %shard_map.169 = (f32[8,32,128]{2,1,0:T(8,128)S(1)}, f32[8,8,128]{2,1,0:T(8,128)S(1)}, f32[8,8,128]{2,1,0:T(8,128)S(1)}, f32[4,256,128]{2,1,0:T(8,128)S(1)}, f32...) custom-call(f32[1,256,128]{2,1,0:T(8,128)} %den.1, ...), custom_call_target="tpu_custom_call" | custom-call | tf_op jit(solution)/shard_map/pallas_call | solution.py:836
  3.4 3.1 %collective-permute-start = (f32[8,8,128]{2,1,0:T(8,128)S(1)}, f32[8,8,128]{2,1,0:T(8,128)S(1)}, u32[]{:S(2)}, u32[]{:S(2)}) collective-permute-start(f32[8,8,128]{2,1,0:T(8,128)S(1)} %get-tuple-element.54), channel_id=1, source_target_pairs={{0,1},{1,0},{2,3},{3,2},{4,5},{5,4},{6,7},{7,6},{8,9},{9,8},{10,11... | collective-permute-start | bytes 98312 | tf_op jit(solution)/shard_map/ppermute | solution.py:913
  6.5 3.4 %collective-permute-start.1 = (f32[8,8,128]{2,1,0:T(8,128)S(1)}, f32[8,8,128]{2,1,0:T(8,128)S(1)}, u32[]{:S(2)}, u32[]{:S(2)}) collective-permute-start(f32[8,8,128]{2,1,0:T(8,128)S(1)} %get-tuple-element.55), channel_id=1, source_target_pairs={{0,7},{1,2},{2,1},{3,4},{4,3},{5,6},{6,5},{7,0},{8,15},{9,10},{10,... | collective-permute-start | bytes 98312 | tf_op jit(solution)/shard_map/ppermute | solution.py:913
  10.0 5.3 %shard_map.170 = (f32[4,256,128]{2,1,0:T(8,128)S(1)}, bf16[4,256,1024]{2,1,0:T(8,128)(2,1)S(1)}, bf16[4,256,1024]{2,1,0:T(8,128)(2,1)S(1)}, bf16[4,256,1024]{2,1...) custom-call(f32[4,256,128]{2,1,0:T(8,128)S(1)} %get-tuple-element.45, ...), custom_call_target="tpu_custom_call" | custom-call | flops 10000000000 | bytes 10000000 | tf_op jit(solution)/shard_map/pallas_call | solution.py:836
  15.3 0.0 collective-permute-done.from_first
  15.3 0.0 collective-permute-done.1.from_second
  15.3 24.4 %shard_map.171 = (f32[4,256,128]{2,1,0:T(8,128)S(1)}, bf16[4,256,1024]{2,1,0:T(8,128)(2,1)S(1)}, bf16[4,256,1024]{2,1,0:T(8,128)(2,1)S(1)}, f32[40,128]{1,0:T(8,128)S(1)}) custom-call(f32[4,256,128]{2,1,0:T(8,128)S(1)} %get-tuple-element.45.state, f32[4,256,128]{2,1,0:T(8,128)S(1)} %get-tuple-element.46.cot, f32[4,256,128]{2,1,0:T(8,128)S(1)} %get-tuple-element.52.middle, ...), custom_call_target="tpu_custom_call" | custom-call | flops 40000000000 | bytes 20000000 | tf_op jit(solution)/shard_map/pallas_call | solution.py:836
  39.7 0.0 collective-permute-start.2
  39.7 1.2 %collective-permute-done.2 = f32[40,128]{1,0:T(8,128)S(1)} collective-permute-done((f32[40,128]{1,0:T(8,128)S(1)}, f32[40,128]{1,0:T(8,128)S(1)}, u32[]{:S(2)}, u32[]{:S(2)}) %collective-permute-start.2) | collective-permute-done | bytes 20512 | tf_op jit(solution)/shard_map/ppermute | solution.py:862
  40.9 1.4 %collective-permute-start.5 = (f32[40,128]{1,0:T(8,128)S(1)}, f32[40,128]{1,0:T(8,128)S(1)}, u32[]{:S(2)}, u32[]{:S(2)}) collective-permute-start(f32[40,128]{1,0:T(8,128)S(1)} %add.21._), channel_id=1, source_target_pairs={{0,20},{1,21},{2,22},{3,23},{4,16},{5,17},{6,18},{7,19},{8,28},{9,... | collective-permute-start | bytes 61448 | tf_op jit(solution)/shard_map/ppermute | solution.py:862
  42.3 1.5 %collective-permute-start.4 = (f32[40,128]{1,0:T(8,128)S(1)}, f32[40,128]{1,0:T(8,128)S(1)}, u32[]{:S(2)}, u32[]{:S(2)}) collective-permute-start(f32[40,128]{1,0:T(8,128)S(1)} %add.21._), channel_id=1, source_target_pairs={{0,4},{1,5},{2,6},{3,7},{4,0},{5,1},{6,2},{7,3},{8,12},{9,13},{10,... | collective-permute-start | bytes 61448 | tf_op jit(solution)/shard_map/ppermute | solution.py:862
  43.8 0.5 collective-permute-start.3
  44.4 1.2 %collective-permute-done.5 = f32[40,128]{1,0:T(8,128)S(1)} collective-permute-done((f32[40,128]{1,0:T(8,128)S(1)}, f32[40,128]{1,0:T(8,128)S(1)}, u32[]{:S(2)}, u32[]{:S(2)}) %collective-permute-start.5) | collective-permute-done | bytes 20512 | tf_op jit(solution)/shard_map/ppermute | solution.py:862
  45.6 0.5 collective-permute-done.4
  46.1 1.5 %collective-permute-done.3 = f32[40,128]{1,0:T(8,128)S(1)} collective-permute-done((f32[40,128]{1,0:T(8,128)S(1)}, f32[40,128]{1,0:T(8,128)S(1)}, u32[]{:S(2)}, u32[]{:S(2)}) %collective-permute-start.3) | collective-permute-done | bytes 20512 | tf_op jit(solution)/shard_map/ppermute | solution.py:862
  47.6 1.4 %collective-permute-start.8 = (f32[40,128]{1,0:T(8,128)S(1)}, f32[40,128]{1,0:T(8,128)S(1)}, u32[]{:S(2)}, u32[]{:S(2)}) collective-permute-start(f32[40,128]{1,0:T(8,128)S(1)} %add_add_fusion.1), channel_id=1, source_target_pairs={{0,3},{1,2},{2,1},{3,0},{4,7},{5,6},{6,5},{7,4},{8,11},{9,10},{10,... | collective-permute-start | bytes 61448 | tf_op jit(solution)/shard_map/ppermute | solution.py:862
  49.0 0.0 collective-permute-start.7
  49.0 3.0 %collective-permute-start.6 = (f32[40,128]{1,0:T(8,128)S(1)}, f32[40,128]{1,0:T(8,128)S(1)}, u32[]{:S(2)}, u32[]{:S(2)}) collective-permute-start(f32[40,128]{1,0:T(8,128)S(1)} %add_add_fusion.1), channel_id=1, source_target_pairs={{0,2},{1,3},{2,0},{3,1},{4,6},{5,7},{6,4},{7,5},{8,10},{9,11},{10,... | collective-permute-start | bytes 61448 | tf_op jit(solution)/shard_map/ppermute | solution.py:862
  52.1 2.1 %shard_map.172 = (f32[1,256,128]{2,1,0:T(8,128)}, f32[1,2,256,128]{3,2,1,0:T(8,128)}, f32[1,256,128]{2,1,0:T(8,128)}) custom-call(f32[4,256,128]{2,1,0:T(8,128)S(1)} %get-tuple-element.67.base, bf16[4,256,1024]{2,1,0:T(8,128)(2,1)S(1)} %get-tuple-element.68.d1_hi, bf16[4,256,1024]{2,1,0:T(8,128)(2,1)S(1)} %get-tuple-element.69.d1_lo, ...), custom_call_target="tpu_custom_call" | custom-call | flops 2000000000 | bytes 1000000 | tf_op jit(solution)/shard_map/pallas_call | solution.py:836
  54.1 0.0 collective-permute-done.8
  54.1 0.0 collective-permute-done.7
  54.1 0.0 collective-permute-done.6
  54.2 0.7 %shard_map.173 = (f32[16,32]{1,0:T(8,128)}, f32[1,32]{1,0:T(1,128)}, f32[32,32]{1,0:T(8,128)}, f32[1,32]{1,0:T(1,128)}, f32[8,32]{1,0:T(8,128)}, /*index=5*/f32[1,8]{1,0:T(1,128)}) custom-call(f32[40,128]{1,0:T(8,128)S(1)} %add_add_fusion.total), custom_call_target="tpu_custom_call" | custom-call | tf_op jit(solution)/shard_map/pallas_call | solution.py:836
  (3 shorter events, 0.0 us)
Async XLA Ops:
  3.4 11.8 %collective-permute-start = (f32[8,8,128]{2,1,0:T(8,128)S(1)}, f32[8,8,128]{2,1,0:T(8,128)S(1)}, u32[]{:S(2)}, u32[]{:S(2)}) collective-permute-start(f32[8,8,128]{2,1,0:T(8,128)S(1)} %get-tuple-element.54), channel_id=1, source_target_pairs={{0,1},{1,0},{2,3},{3,2},{4,5},{5,4},{6,7},{7,6},{8,9},{9,8},{10,11... | collective-permute-start | bytes 98312 | tf_op jit(solution)/shard_map/ppermute | solution.py:913
  6.5 8.7 %collective-permute-start.1 = (f32[8,8,128]{2,1,0:T(8,128)S(1)}, f32[8,8,128]{2,1,0:T(8,128)S(1)}, u32[]{:S(2)}, u32[]{:S(2)}) collective-permute-start(f32[8,8,128]{2,1,0:T(8,128)S(1)} %get-tuple-element.55), channel_id=1, source_target_pairs={{0,7},{1,2},{2,1},{3,4},{4,3},{5,6},{6,5},{7,0},{8,15},{9,10},{10,... | collective-permute-start | bytes 98312 | tf_op jit(solution)/shard_map/ppermute | solution.py:913
  39.7 1.2 %collective-permute-start.2 = (f32[40,128]{1,0:T(8,128)S(1)}, f32[40,128]{1,0:T(8,128)S(1)}, u32[]{:S(2)}, u32[]{:S(2)}) collective-permute-start(f32[40,128]{1,0:T(8,128)S(1)} %get-tuple-element.71), channel_id=1, source_target_pairs={{0,8},{1,9},{2,10},{3,11},{4,12},{5,13},{6,14},{7,15},{8,0},{9,1},... | collective-permute-start | bytes 61448 | tf_op jit(solution)/shard_map/ppermute | solution.py:862
  40.9 4.7 %collective-permute-start.5 = (f32[40,128]{1,0:T(8,128)S(1)}, f32[40,128]{1,0:T(8,128)S(1)}, u32[]{:S(2)}, u32[]{:S(2)}) collective-permute-start(f32[40,128]{1,0:T(8,128)S(1)} %add.21._), channel_id=1, source_target_pairs={{0,20},{1,21},{2,22},{3,23},{4,16},{5,17},{6,18},{7,19},{8,28},{9,... | collective-permute-start | bytes 61448 | tf_op jit(solution)/shard_map/ppermute | solution.py:862
  42.3 3.8 %collective-permute-start.4 = (f32[40,128]{1,0:T(8,128)S(1)}, f32[40,128]{1,0:T(8,128)S(1)}, u32[]{:S(2)}, u32[]{:S(2)}) collective-permute-start(f32[40,128]{1,0:T(8,128)S(1)} %add.21._), channel_id=1, source_target_pairs={{0,4},{1,5},{2,6},{3,7},{4,0},{5,1},{6,2},{7,3},{8,12},{9,13},{10,... | collective-permute-start | bytes 61448 | tf_op jit(solution)/shard_map/ppermute | solution.py:862
  43.8 3.8 %collective-permute-start.3 = (f32[40,128]{1,0:T(8,128)S(1)}, f32[40,128]{1,0:T(8,128)S(1)}, u32[]{:S(2)}, u32[]{:S(2)}) collective-permute-start(f32[40,128]{1,0:T(8,128)S(1)} %add.21._), channel_id=1, source_target_pairs={{0,16},{1,17},{2,18},{3,19},{4,20},{5,21},{6,22},{7,23},{8,24},{9,... | collective-permute-start | bytes 61448 | tf_op jit(solution)/shard_map/ppermute | solution.py:862
  47.6 6.5 %collective-permute-start.8 = (f32[40,128]{1,0:T(8,128)S(1)}, f32[40,128]{1,0:T(8,128)S(1)}, u32[]{:S(2)}, u32[]{:S(2)}) collective-permute-start(f32[40,128]{1,0:T(8,128)S(1)} %add_add_fusion.1), channel_id=1, source_target_pairs={{0,3},{1,2},{2,1},{3,0},{4,7},{5,6},{6,5},{7,4},{8,11},{9,10},{10,... | collective-permute-start | bytes 61448 | tf_op jit(solution)/shard_map/ppermute | solution.py:862
  49.0 5.1 %collective-permute-start.7 = (f32[40,128]{1,0:T(8,128)S(1)}, f32[40,128]{1,0:T(8,128)S(1)}, u32[]{:S(2)}, u32[]{:S(2)}) collective-permute-start(f32[40,128]{1,0:T(8,128)S(1)} %add_add_fusion.1), channel_id=1, source_target_pairs={{0,1},{1,0},{2,3},{3,2},{4,5},{5,4},{6,7},{7,6},{8,9},{9,8},{10,11... | collective-permute-start | bytes 61448 | tf_op jit(solution)/shard_map/ppermute | solution.py:862
  49.0 5.1 %collective-permute-start.6 = (f32[40,128]{1,0:T(8,128)S(1)}, f32[40,128]{1,0:T(8,128)S(1)}, u32[]{:S(2)}, u32[]{:S(2)}) collective-permute-start(f32[40,128]{1,0:T(8,128)S(1)} %add_add_fusion.1), channel_id=1, source_target_pairs={{0,2},{1,3},{2,0},{3,1},{4,6},{5,7},{6,4},{7,5},{8,10},{9,11},{10,... | collective-permute-start | bytes 61448 | tf_op jit(solution)/shard_map/ppermute | solution.py:862

commit v11 on v9

--- a/solution.py
+++ b/solution.py
@@ -215,25 +215,29 @@
 def limiter_forward(first, weights, hid):
     first_ref, first_bias_ref, mid_ref, mid_bias_ref, out_ref, out_bias_ref = weights
     width = first[0][0].shape[1]
-    if first_bias_ref is None:
-        ones = [jnp.ones((ONES, width), BF16)]
-        h1 = stack([jnp.tanh(dot(first_ref[...], stack(stacked(one) + ones))) for one in first])
-    else:
-        parts = []
-        for high, middle, low in first:
+    ones = [jnp.ones((ONES, width), BF16)]
+    firsts = []
+    for one in first:
+        if first_bias_ref is None:
+            firsts.append(dot(first_ref[...], stack(stacked(one) + ones)))
+        else:
+            high, middle, low = one
             both = dot(first_ref[...], stack([high, middle, low, high]))
             half = both.shape[0] // 2
-            parts.append(jnp.tanh(both[:half] + both[half:] + spread(first_bias_ref, width)))
-        h1 = stack(parts)
-    h1_parts = split3(h1)
+            firsts.append(both[:half] + both[half:] + spread(first_bias_ref, width))
     block = 2 * hid
-    parts = []
-    for at in range(0, FACES * hid, block):
-        high, middle, low = (p[at : at + block] for p in h1_parts)
-        both = dot(mid_ref[...], stack([high, middle, low, high]))
-        parts.append(jnp.tanh(both[:block] + both[block:] + spread(mid_bias_ref, width)))
-    h2 = stack(parts)
-    h2_parts = split3(h2)
+    h1, h1_parts, h2, h2_parts = [], [], [], []
+    for values in firsts:
+        for at in range(0, values.shape[0], block):
+            h1.append(jnp.tanh(values[at : at + block]))
+            high, middle, low = split3(h1[-1])
+            h1_parts.append((high, middle))
+            both = dot(mid_ref[...], stack([high, middle, low, high]))
+            h2.append(jnp.tanh(both[:block] + both[block:] + spread(mid_bias_ref, width)))
+            h2_parts.append(split3(h2[-1]))
+    h1, h2 = stack(h1), stack(h2)
+    h1_parts = tuple(stack([one[k] for one in h1_parts]) for k in range(2))
+    h2_parts = tuple(stack([one[k] for one in h2_parts]) for k in range(3))
     rows = 8 * FACES
     a = dot(out_ref[...], h2_parts[0])
     b = dot(out_ref[: 2 * rows, :], h2_parts[1])
@@ -241,7 +245,7 @@
     gates = jnp.tanh(
         ((a[2 * rows :] + b[rows:] + c) + (a[rows : 2 * rows] + b[:rows])) + a[:rows] + spread(out_bias_ref, width)
     )
-    return h1, h1_parts[:2], h2, h2_parts[:2], gates
+    return h1, h1_parts, h2, h2_parts[:2], gates
 
 
 def limiter_backward(d3, h1, h2, h1_pair, h2_pair, out_back_ref, mid_back_ref, acc, hid):
@@ -250,12 +254,14 @@
     if acc is not None:
         acc[2][...] += dot_nt(stack(list(h2_pair)), stack([d3_hi, d3_lo]))
         acc[3][...] += d3
-    d2_hi, d2_lo = split(dh2 * (1.0 - h2 * h2))
     block = 2 * hid
-    parts = []
+    d2, d1 = [], []
     for at in range(0, FACES * hid, block):
-        hi, lo = d2_hi[at : at + block], d2_lo[at : at + block]
-        parts.append(dot(mid_back_ref[...], stack([hi, hi, lo])))
+        one1, one2 = h1[at : at + block], h2[at : at + block]
+        high, low = split(dh2[at : at + block] * (1.0 - one2 * one2))
+        d2.append((high, low))
+        d1.append(split(dot(mid_back_ref[...], stack([high, high, low])) * (1.0 - one1 * one1)))
+    d2_hi, d2_lo = (stack([one[k] for one in d2]) for k in range(2))
     if acc is not None:
         ones = jnp.ones((ONES, d3.shape[1]), BF16)
         lefts, rights = [], []
@@ -263,7 +269,7 @@
             lefts.append(stack([part[at : at + 2 * block] for part in h1_pair] + [ones]))
             rights.append(stack([part[at : at + 2 * block] for part in (d2_hi, d2_lo)]))
         acc[1][...] += dot_nt(side(lefts), side(rights))
-    return stack(parts) * (1.0 - h1 * h1)
+    return tuple(stack([one[k] for one in d1]) for k in range(2))
 
 
 def first_backward(d1, back_ref):
@@ -530,8 +536,7 @@
         d_left = [jnp.where(halo_mask, d, 0.0) for d in d_left]
         d_right = [jnp.where(halo_mask, d, 0.0) for d in d_right]
     d3_full, direct = edge_backward(cells, gates, d_left, d_right)
-    d1_full = limiter_backward(d3_full, h1, h2, h1_pair, h2_pair, out_back, mid_back, acc, hid)
-    d1 = split(d1_full)
+    d1 = limiter_backward(d3_full, h1, h2, h1_pair, h2_pair, out_back, mid_back, acc, hid)
     d_window = y_unwindow(first_backward(d1, first_y_back))
     if acc is not None:
         add_first_grads(window, d1, acc[0])
@@ -718,10 +723,9 @@
         d_flux = [courant * (turn(d, -2, 0)[:FACES] - turn(d, -1, 0)[:FACES]) for d in d_tiles]
         d_left, d_right = face_flux_backward(left, right, d_flux)
         d3_full, direct = edge_backward(cells, gates, d_left, d_right)
-        d1_full = limiter_backward(
+        d1 = limiter_backward(
             d3_full, h1, h2, h1_pair, h2_pair, out_back, mid_back, (acc_x, acc_mid, acc_out, acc_out_bias), hid
         )
-        d1 = split(d1_full)
         d1_hi[step], d1_lo[step] = d1
         add_first_grads([split(one) for one in x_windows(tiles)], d1, acc_x)
         later = []

time: 54.8 us -> 54.8 us (level)
  no operation moved by 1% of the time
where the time goes in v11:
time: 54.8 us; the launch traced here: 54.6 us
  Pallas kernels  34.9 us (64%)
  starting transfers between devices  14.5 us (26%)
  waiting for transfers between devices  4.44 us (8%)
  between operations  0.71 us (1%)
    pallas_call x5, Pallas kernels, call(): pl.pallas_call(kernel, out_shape=outs, in_specs=in_spaces or whole(len(op...  34.9 us
    ppermute x7, starting transfers between devices, sum_rounds(): lax.ppermute(values, axes, [(i, i ^ one) for i in range(size)])  7.95 us
    ppermute x2, starting transfers between devices, body(): lax.ppermute(one, axes, swap)  6.53 us
    ppermute x7, waiting for transfers between devices, sum_rounds(): lax.ppermute(values, axes, [(i, i ^ one) for i in range(size)])  4.43 us
  transfers between devices with their start and end apart: 9, of which 4 were waited for; matrix products, arithmetic and copies ran while one was open for 0% of the time, Pallas kernels for 13%

profile of v11, /device:TPU:0, one launch (start us, length us, event | category | flops | bytes accessed | tf_op | source)
XLA Modules:
  0.0 54.6 jit_solution(2535164178392800265)
XLA Ops:
  0.6 2.8 %shard_map.169 = (f32[8,32,128]{2,1,0:T(8,128)S(1)}, f32[8,8,128]{2,1,0:T(8,128)S(1)}, f32[8,8,128]{2,1,0:T(8,128)S(1)}, f32[4,256,128]{2,1,0:T(8,128)S(1)}, f32...) custom-call(f32[1,256,128]{2,1,0:T(8,128)} %den.1, ...), custom_call_target="tpu_custom_call" | custom-call | tf_op jit(solution)/shard_map/pallas_call | solution.py:838
  3.4 3.1 %collective-permute-start = (f32[8,8,128]{2,1,0:T(8,128)S(1)}, f32[8,8,128]{2,1,0:T(8,128)S(1)}, u32[]{:S(2)}, u32[]{:S(2)}) collective-permute-start(f32[8,8,128]{2,1,0:T(8,128)S(1)} %get-tuple-element.53), channel_id=1, source_target_pairs={{0,1},{1,0},{2,3},{3,2},{4,5},{5,4},{6,7},{7,6},{8,9},{9,8},{10,11... | collective-permute-start | bytes 98312 | tf_op jit(solution)/shard_map/ppermute | solution.py:915
  6.5 3.4 %collective-permute-start.1 = (f32[8,8,128]{2,1,0:T(8,128)S(1)}, f32[8,8,128]{2,1,0:T(8,128)S(1)}, u32[]{:S(2)}, u32[]{:S(2)}) collective-permute-start(f32[8,8,128]{2,1,0:T(8,128)S(1)} %get-tuple-element.54), channel_id=1, source_target_pairs={{0,7},{1,2},{2,1},{3,4},{4,3},{5,6},{6,5},{7,0},{8,15},{9,10},{10,... | collective-permute-start | bytes 98312 | tf_op jit(solution)/shard_map/ppermute | solution.py:915
  10.0 4.9 %shard_map.170 = (f32[4,256,128]{2,1,0:T(8,128)S(1)}, bf16[4,256,1024]{2,1,0:T(8,128)(2,1)S(1)}, bf16[4,256,1024]{2,1,0:T(8,128)(2,1)S(1)}, bf16[4,256,1024]{2,1...) custom-call(f32[4,256,128]{2,1,0:T(8,128)S(1)} %get-tuple-element.44.state, ...), custom_call_target="tpu_custom_call" | custom-call | flops 10000000000 | bytes 10000000 | tf_op jit(solution)/shard_map/pallas_call | solution.py:838
  14.9 0.0 collective-permute-done.from_first
  14.9 0.0 collective-permute-done.1.from_second
  14.9 24.5 %shard_map.171 = (f32[4,256,128]{2,1,0:T(8,128)S(1)}, bf16[4,256,1024]{2,1,0:T(8,128)(2,1)S(1)}, bf16[4,256,1024]{2,1,0:T(8,128)(2,1)S(1)}, f32[40,128]{1,0:T(8,128)S(1)}) custom-call(f32[4,256,128]{2,1,0:T(8,128)S(1)} %get-tuple-element.44.state, f32[4,256,128]{2,1,0:T(8,128)S(1)} %get-tuple-element.45.cot, f32[4,256,128]{2,1,0:T(8,128)S(1)} %get-tuple-element.51.middle, ...), custom_call_target="tpu_custom_call" | custom-call | flops 40000000000 | bytes 20000000 | tf_op jit(solution)/shard_map/pallas_call | solution.py:838
  39.4 0.0 collective-permute-start.2
  39.4 1.2 %collective-permute-done.2 = f32[40,128]{1,0:T(8,128)S(1)} collective-permute-done((f32[40,128]{1,0:T(8,128)S(1)}, f32[40,128]{1,0:T(8,128)S(1)}, u32[]{:S(2)}, u32[]{:S(2)}) %collective-permute-start.2) | collective-permute-done | bytes 20512 | tf_op jit(solution)/shard_map/ppermute | solution.py:864
  40.6 1.5 %collective-permute-start.5 = (f32[40,128]{1,0:T(8,128)S(1)}, f32[40,128]{1,0:T(8,128)S(1)}, u32[]{:S(2)}, u32[]{:S(2)}) collective-permute-start(f32[40,128]{1,0:T(8,128)S(1)} %add.21._), channel_id=1, source_target_pairs={{0,20},{1,21},{2,22},{3,23},{4,16},{5,17},{6,18},{7,19},{8,28},{9,... | collective-permute-start | bytes 61448 | tf_op jit(solution)/shard_map/ppermute | solution.py:864
  42.1 1.5 %collective-permute-start.4 = (f32[40,128]{1,0:T(8,128)S(1)}, f32[40,128]{1,0:T(8,128)S(1)}, u32[]{:S(2)}, u32[]{:S(2)}) collective-permute-start(f32[40,128]{1,0:T(8,128)S(1)} %add.21._), channel_id=1, source_target_pairs={{0,4},{1,5},{2,6},{3,7},{4,0},{5,1},{6,2},{7,3},{8,12},{9,13},{10,... | collective-permute-start | bytes 61448 | tf_op jit(solution)/shard_map/ppermute | solution.py:864
  43.5 0.5 %collective-permute-start.3 = (f32[40,128]{1,0:T(8,128)S(1)}, f32[40,128]{1,0:T(8,128)S(1)}, u32[]{:S(2)}, u32[]{:S(2)}) collective-permute-start(f32[40,128]{1,0:T(8,128)S(1)} %add.21._), channel_id=1, source_target_pairs={{0,16},{1,17},{2,18},{3,19},{4,20},{5,21},{6,22},{7,23},{8,24},{9,... | collective-permute-start | bytes 61448 | tf_op jit(solution)/shard_map/ppermute | solution.py:864
  44.1 1.2 %collective-permute-done.5 = f32[40,128]{1,0:T(8,128)S(1)} collective-permute-done((f32[40,128]{1,0:T(8,128)S(1)}, f32[40,128]{1,0:T(8,128)S(1)}, u32[]{:S(2)}, u32[]{:S(2)}) %collective-permute-start.5) | collective-permute-done | bytes 20512 | tf_op jit(solution)/shard_map/ppermute | solution.py:864
  45.3 0.6 %collective-permute-done.4 = f32[40,128]{1,0:T(8,128)S(1)} collective-permute-done((f32[40,128]{1,0:T(8,128)S(1)}, f32[40,128]{1,0:T(8,128)S(1)}, u32[]{:S(2)}, u32[]{:S(2)}) %collective-permute-start.4) | collective-permute-done | bytes 20512 | tf_op jit(solution)/shard_map/ppermute | solution.py:864
  45.8 1.5 %collective-permute-done.3 = f32[40,128]{1,0:T(8,128)S(1)} collective-permute-done((f32[40,128]{1,0:T(8,128)S(1)}, f32[40,128]{1,0:T(8,128)S(1)}, u32[]{:S(2)}, u32[]{:S(2)}) %collective-permute-start.3) | collective-permute-done | bytes 20512 | tf_op jit(solution)/shard_map/ppermute | solution.py:864
  47.3 1.4 %collective-permute-start.8 = (f32[40,128]{1,0:T(8,128)S(1)}, f32[40,128]{1,0:T(8,128)S(1)}, u32[]{:S(2)}, u32[]{:S(2)}) collective-permute-start(f32[40,128]{1,0:T(8,128)S(1)} %add_add_fusion.1), channel_id=1, source_target_pairs={{0,3},{1,2},{2,1},{3,0},{4,7},{5,6},{6,5},{7,4},{8,11},{9,10},{10,... | collective-permute-start | bytes 61448 | tf_op jit(solution)/shard_map/ppermute | solution.py:864
  48.8 0.0 collective-permute-start.7
  48.8 3.0 %collective-permute-start.6 = (f32[40,128]{1,0:T(8,128)S(1)}, f32[40,128]{1,0:T(8,128)S(1)}, u32[]{:S(2)}, u32[]{:S(2)}) collective-permute-start(f32[40,128]{1,0:T(8,128)S(1)} %add_add_fusion.1), channel_id=1, source_target_pairs={{0,2},{1,3},{2,0},{3,1},{4,6},{5,7},{6,4},{7,5},{8,10},{9,11},{10,... | collective-permute-start | bytes 61448 | tf_op jit(solution)/shard_map/ppermute | solution.py:864
  51.8 2.1 %shard_map.172 = (f32[1,256,128]{2,1,0:T(8,128)}, f32[1,2,256,128]{3,2,1,0:T(8,128)}, f32[1,256,128]{2,1,0:T(8,128)}) custom-call(f32[4,256,128]{2,1,0:T(8,128)S(1)} %get-tuple-element.65.base, bf16[4,256,1024]{2,1,0:T(8,128)(2,1)S(1)} %get-tuple-element.66.d1_hi, bf16[4,256,1024]{2,1,0:T(8,128)(2,1)S(1)} %get-tuple-element.67.d1_lo, ...), custom_call_target="tpu_custom_call" | custom-call | flops 2000000000 | bytes 1000000 | tf_op jit(solution)/shard_map/pallas_call | solution.py:838
  53.9 0.0 collective-permute-done.8
  53.9 0.0 collective-permute-done.7
  53.9 0.0 collective-permute-done.6
  53.9 0.7 %shard_map.173 = (f32[16,32]{1,0:T(8,128)}, f32[1,32]{1,0:T(1,128)}, f32[32,32]{1,0:T(8,128)}, f32[1,32]{1,0:T(1,128)}, f32[8,32]{1,0:T(8,128)}, /*index=5*/f32[1,8]{1,0:T(1,128)}) custom-call(f32[40,128]{1,0:T(8,128)S(1)} %add_add_fusion.total), custom_call_target="tpu_custom_call" | custom-call | tf_op jit(solution)/shard_map/pallas_call | solution.py:838
  (3 shorter events, 0.0 us)
Async XLA Ops:
  3.4 11.5 %collective-permute-start = (f32[8,8,128]{2,1,0:T(8,128)S(1)}, f32[8,8,128]{2,1,0:T(8,128)S(1)}, u32[]{:S(2)}, u32[]{:S(2)}) collective-permute-start(f32[8,8,128]{2,1,0:T(8,128)S(1)} %get-tuple-element.53), channel_id=1, source_target_pairs={{0,1},{1,0},{2,3},{3,2},{4,5},{5,4},{6,7},{7,6},{8,9},{9,8},{10,11... | collective-permute-start | bytes 98312 | tf_op jit(solution)/shard_map/ppermute | solution.py:915
  6.5 8.4 %collective-permute-start.1 = (f32[8,8,128]{2,1,0:T(8,128)S(1)}, f32[8,8,128]{2,1,0:T(8,128)S(1)}, u32[]{:S(2)}, u32[]{:S(2)}) collective-permute-start(f32[8,8,128]{2,1,0:T(8,128)S(1)} %get-tuple-element.54), channel_id=1, source_target_pairs={{0,7},{1,2},{2,1},{3,4},{4,3},{5,6},{6,5},{7,0},{8,15},{9,10},{10,... | collective-permute-start | bytes 98312 | tf_op jit(solution)/shard_map/ppermute | solution.py:915
  39.4 1.2 %collective-permute-start.2 = (f32[40,128]{1,0:T(8,128)S(1)}, f32[40,128]{1,0:T(8,128)S(1)}, u32[]{:S(2)}, u32[]{:S(2)}) collective-permute-start(f32[40,128]{1,0:T(8,128)S(1)} %get-tuple-element.69), channel_id=1, source_target_pairs={{0,8},{1,9},{2,10},{3,11},{4,12},{5,13},{6,14},{7,15},{8,0},{9,1},... | collective-permute-start | bytes 61448 | tf_op jit(solution)/shard_map/ppermute | solution.py:864
  40.6 4.7 %collective-permute-start.5 = (f32[40,128]{1,0:T(8,128)S(1)}, f32[40,128]{1,0:T(8,128)S(1)}, u32[]{:S(2)}, u32[]{:S(2)}) collective-permute-start(f32[40,128]{1,0:T(8,128)S(1)} %add.21._), channel_id=1, source_target_pairs={{0,20},{1,21},{2,22},{3,23},{4,16},{5,17},{6,18},{7,19},{8,28},{9,... | collective-permute-start | bytes 61448 | tf_op jit(solution)/shard_map/ppermute | solution.py:864
  42.1 3.8 %collective-permute-start.4 = (f32[40,128]{1,0:T(8,128)S(1)}, f32[40,128]{1,0:T(8,128)S(1)}, u32[]{:S(2)}, u32[]{:S(2)}) collective-permute-start(f32[40,128]{1,0:T(8,128)S(1)} %add.21._), channel_id=1, source_target_pairs={{0,4},{1,5},{2,6},{3,7},{4,0},{5,1},{6,2},{7,3},{8,12},{9,13},{10,... | collective-permute-start | bytes 61448 | tf_op jit(solution)/shard_map/ppermute | solution.py:864
  43.5 3.8 %collective-permute-start.3 = (f32[40,128]{1,0:T(8,128)S(1)}, f32[40,128]{1,0:T(8,128)S(1)}, u32[]{:S(2)}, u32[]{:S(2)}) collective-permute-start(f32[40,128]{1,0:T(8,128)S(1)} %add.21._), channel_id=1, source_target_pairs={{0,16},{1,17},{2,18},{3,19},{4,20},{5,21},{6,22},{7,23},{8,24},{9,... | collective-permute-start | bytes 61448 | tf_op jit(solution)/shard_map/ppermute | solution.py:864
  47.3 6.5 %collective-permute-start.8 = (f32[40,128]{1,0:T(8,128)S(1)}, f32[40,128]{1,0:T(8,128)S(1)}, u32[]{:S(2)}, u32[]{:S(2)}) collective-permute-start(f32[40,128]{1,0:T(8,128)S(1)} %add_add_fusion.1), channel_id=1, source_target_pairs={{0,3},{1,2},{2,1},{3,0},{4,7},{5,6},{6,5},{7,4},{8,11},{9,10},{10,... | collective-permute-start | bytes 61448 | tf_op jit(solution)/shard_map/ppermute | solution.py:864
  48.8 5.1 %collective-permute-start.7 = (f32[40,128]{1,0:T(8,128)S(1)}, f32[40,128]{1,0:T(8,128)S(1)}, u32[]{:S(2)}, u32[]{:S(2)}) collective-permute-start(f32[40,128]{1,0:T(8,128)S(1)} %add_add_fusion.1), channel_id=1, source_target_pairs={{0,1},{1,0},{2,3},{3,2},{4,5},{5,4},{6,7},{7,6},{8,9},{9,8},{10,11... | collective-permute-start | bytes 61448 | tf_op jit(solution)/shard_map/ppermute | solution.py:864
  48.8 5.1 %collective-permute-start.6 = (f32[40,128]{1,0:T(8,128)S(1)}, f32[40,128]{1,0:T(8,128)S(1)}, u32[]{:S(2)}, u32[]{:S(2)}) collective-permute-start(f32[40,128]{1,0:T(8,128)S(1)} %add_add_fusion.1), channel_id=1, source_target_pairs={{0,2},{1,3},{2,0},{3,1},{4,6},{5,7},{6,4},{7,5},{8,10},{9,11},{10,... | collective-permute-start | bytes 61448 | tf_op jit(solution)/shard_map/ppermute | solution.py:864

commit v12 on v11

--- a/solution.py
+++ b/solution.py
@@ -504,7 +504,7 @@
                 flux[c, row_block(step + k * half + 1), :] = fluxes[c][:, k * ny : (k + 1) * ny]
         return 0
 
-    lax.fori_loop(0, half, step_of, 0)
+    lax.fori_loop(0, half, step_of, 0, unroll=2)
     for c in range(4):
         flux[c, :FACES, :] = flux[c, nx : nx + FACES, :]
 
@@ -514,7 +514,7 @@
             middle[c, row_block(group), :] = update_cells(planes[c][row_block(group), :], both)
         return 0
 
-    lax.fori_loop(0, groups, update, 0)
+    lax.fori_loop(0, groups, update, 0, unroll=4)
 
 
 def y_order(planes):
@@ -705,7 +705,7 @@
                 d_middle[c, rows, :] = cot[c, rows, :] + gathered[c] + from_rim
         return 0
 
-    lax.fori_loop(0, half, main_y, 0)
+    lax.fori_loop(0, half, main_y, 0, unroll=2)
 
     planes = [state.at[c] for c in range(4)]
     d_planes = [d_middle.at[c] for c in range(4)]
@@ -741,7 +741,7 @@
         return tuple(later)
 
     start = tuple(jnp.zeros((FACES, PAIR * ny), F32) for _ in range(4))
-    last = lax.fori_loop(0, half, main_x, start)
+    last = lax.fori_loop(0, half, main_x, start, unroll=2)
     for c in range(4):
         for k in range(PAIR):
             at = (k + 1) % PAIR * half * FACES

time: 54.8 us -> 53.3 us (0.973)
  Pallas kernels: 34.9 us -> 33.4 us
    pallas_call x5, Pallas kernels: 34.9 us -> 33.4 us  [call(): pl.pallas_call(kernel, out_shape=outs, in_specs=in_spaces or whole(len(op...]
  transfers between devices with their start and end apart: 9 -> 9, of which waited for: 4 -> 4; matrix products, arithmetic and copies ran while one was open for 0% -> 0% of each run, Pallas kernels for 13% -> 12%
where the time goes in v12:
time: 53.3 us; the launch traced here: 53.1 us
  Pallas kernels  33.4 us (63%)
  starting transfers between devices  14.5 us (27%)
  waiting for transfers between devices  4.46 us (8%)
  between operations  0.71 us (1%)
    pallas_call x5, Pallas kernels, call(): pl.pallas_call(kernel, out_shape=outs, in_specs=in_spaces or whole(len(op...  33.4 us
    ppermute x7, starting transfers between devices, sum_rounds(): lax.ppermute(values, axes, [(i, i ^ one) for i in range(size)])  7.95 us
    ppermute x2, starting transfers between devices, body(): lax.ppermute(one, axes, swap)  6.51 us
    ppermute x7, waiting for transfers between devices, sum_rounds(): lax.ppermute(values, axes, [(i, i ^ one) for i in range(size)])  4.46 us
  transfers between devices with their start and end apart: 9, of which 4 were waited for; matrix products, arithmetic and copies ran while one was open for 0% of the time, Pallas kernels for 12%

profile of v12, /device:TPU:0, one launch (start us, length us, event | category | flops | bytes accessed | tf_op | source)
XLA Modules:
  0.0 53.1 jit_solution(5622619661800005837)
XLA Ops:
  0.6 2.8 %shard_map.169 = (f32[8,32,128]{2,1,0:T(8,128)S(1)}, f32[8,8,128]{2,1,0:T(8,128)S(1)}, f32[8,8,128]{2,1,0:T(8,128)S(1)}, f32[4,256,128]{2,1,0:T(8,128)S(1)}, f32...) custom-call(f32[1,256,128]{2,1,0:T(8,128)} %den.1, ...), custom_call_target="tpu_custom_call" | custom-call | tf_op jit(solution)/shard_map/pallas_call | solution.py:838
  3.5 3.1 %collective-permute-start = (f32[8,8,128]{2,1,0:T(8,128)S(1)}, f32[8,8,128]{2,1,0:T(8,128)S(1)}, u32[]{:S(2)}, u32[]{:S(2)}) collective-permute-start(f32[8,8,128]{2,1,0:T(8,128)S(1)} %get-tuple-element.53), channel_id=1, source_target_pairs={{0,1},{1,0},{2,3},{3,2},{4,5},{5,4},{6,7},{7,6},{8,9},{9,8},{10,11... | collective-permute-start | bytes 98312 | tf_op jit(solution)/shard_map/ppermute | solution.py:915
  6.5 3.4 %collective-permute-start.1 = (f32[8,8,128]{2,1,0:T(8,128)S(1)}, f32[8,8,128]{2,1,0:T(8,128)S(1)}, u32[]{:S(2)}, u32[]{:S(2)}) collective-permute-start(f32[8,8,128]{2,1,0:T(8,128)S(1)} %get-tuple-element.54), channel_id=1, source_target_pairs={{0,7},{1,2},{2,1},{3,4},{4,3},{5,6},{6,5},{7,0},{8,15},{9,10},{10,... | collective-permute-start | bytes 98312 | tf_op jit(solution)/shard_map/ppermute | solution.py:915
  10.0 4.5 %shard_map.170 = (f32[4,256,128]{2,1,0:T(8,128)S(1)}, bf16[4,256,1024]{2,1,0:T(8,128)(2,1)S(1)}, bf16[4,256,1024]{2,1,0:T(8,128)(2,1)S(1)}, bf16[4,256,1024]{2,1...) custom-call(f32[4,256,128]{2,1,0:T(8,128)S(1)} %get-tuple-element.44.state, ...), custom_call_target="tpu_custom_call" | custom-call | flops 10000000000 | bytes 10000000 | tf_op jit(solution)/shard_map/pallas_call | solution.py:838
  14.5 0.0 collective-permute-done.from_first
  14.5 0.0 collective-permute-done.1.from_second
  14.5 23.4 %shard_map.171 = (f32[4,256,128]{2,1,0:T(8,128)S(1)}, bf16[4,256,1024]{2,1,0:T(8,128)(2,1)S(1)}, bf16[4,256,1024]{2,1,0:T(8,128)(2,1)S(1)}, f32[40,128]{1,0:T(8,128)S(1)}) custom-call(f32[4,256,128]{2,1,0:T(8,128)S(1)} %get-tuple-element.44.state, f32[4,256,128]{2,1,0:T(8,128)S(1)} %get-tuple-element.45.cot, f32[4,256,128]{2,1,0:T(8,128)S(1)} %get-tuple-element.51.middle, ...), custom_call_target="tpu_custom_call" | custom-call | flops 40000000000 | bytes 20000000 | tf_op jit(solution)/shard_map/pallas_call | solution.py:838
  37.9 0.0 collective-permute-start.2
  37.9 1.2 %collective-permute-done.2 = f32[40,128]{1,0:T(8,128)S(1)} collective-permute-done((f32[40,128]{1,0:T(8,128)S(1)}, f32[40,128]{1,0:T(8,128)S(1)}, u32[]{:S(2)}, u32[]{:S(2)}) %collective-permute-start.2) | collective-permute-done | bytes 20512 | tf_op jit(solution)/shard_map/ppermute | solution.py:864
  39.1 1.4 %collective-permute-start.5 = (f32[40,128]{1,0:T(8,128)S(1)}, f32[40,128]{1,0:T(8,128)S(1)}, u32[]{:S(2)}, u32[]{:S(2)}) collective-permute-start(f32[40,128]{1,0:T(8,128)S(1)} %add.21._), channel_id=1, source_target_pairs={{0,20},{1,21},{2,22},{3,23},{4,16},{5,17},{6,18},{7,19},{8,28},{9,... | collective-permute-start | bytes 61448 | tf_op jit(solution)/shard_map/ppermute | solution.py:864
  40.5 1.5 %collective-permute-start.4 = (f32[40,128]{1,0:T(8,128)S(1)}, f32[40,128]{1,0:T(8,128)S(1)}, u32[]{:S(2)}, u32[]{:S(2)}) collective-permute-start(f32[40,128]{1,0:T(8,128)S(1)} %add.21._), channel_id=1, source_target_pairs={{0,4},{1,5},{2,6},{3,7},{4,0},{5,1},{6,2},{7,3},{8,12},{9,13},{10,... | collective-permute-start | bytes 61448 | tf_op jit(solution)/shard_map/ppermute | solution.py:864
  42.1 0.5 collective-permute-start.3
  42.6 1.2 %collective-permute-done.5 = f32[40,128]{1,0:T(8,128)S(1)} collective-permute-done((f32[40,128]{1,0:T(8,128)S(1)}, f32[40,128]{1,0:T(8,128)S(1)}, u32[]{:S(2)}, u32[]{:S(2)}) %collective-permute-start.5) | collective-permute-done | bytes 20512 | tf_op jit(solution)/shard_map/ppermute | solution.py:864
  43.8 0.5 %collective-permute-done.4 = f32[40,128]{1,0:T(8,128)S(1)} collective-permute-done((f32[40,128]{1,0:T(8,128)S(1)}, f32[40,128]{1,0:T(8,128)S(1)}, u32[]{:S(2)}, u32[]{:S(2)}) %collective-permute-start.4) | collective-permute-done | bytes 20512 | tf_op jit(solution)/shard_map/ppermute | solution.py:864
  44.3 1.5 %collective-permute-done.3 = f32[40,128]{1,0:T(8,128)S(1)} collective-permute-done((f32[40,128]{1,0:T(8,128)S(1)}, f32[40,128]{1,0:T(8,128)S(1)}, u32[]{:S(2)}, u32[]{:S(2)}) %collective-permute-start.3) | collective-permute-done | bytes 20512 | tf_op jit(solution)/shard_map/ppermute | solution.py:864
  45.9 1.4 %collective-permute-start.8 = (f32[40,128]{1,0:T(8,128)S(1)}, f32[40,128]{1,0:T(8,128)S(1)}, u32[]{:S(2)}, u32[]{:S(2)}) collective-permute-start(f32[40,128]{1,0:T(8,128)S(1)} %add_add_fusion.1), channel_id=1, source_target_pairs={{0,3},{1,2},{2,1},{3,0},{4,7},{5,6},{6,5},{7,4},{8,11},{9,10},{10,... | collective-permute-start | bytes 61448 | tf_op jit(solution)/shard_map/ppermute | solution.py:864
  47.3 0.0 collective-permute-start.7
  47.3 3.0 %collective-permute-start.6 = (f32[40,128]{1,0:T(8,128)S(1)}, f32[40,128]{1,0:T(8,128)S(1)}, u32[]{:S(2)}, u32[]{:S(2)}) collective-permute-start(f32[40,128]{1,0:T(8,128)S(1)} %add_add_fusion.1), channel_id=1, source_target_pairs={{0,2},{1,3},{2,0},{3,1},{4,6},{5,7},{6,4},{7,5},{8,10},{9,11},{10,... | collective-permute-start | bytes 61448 | tf_op jit(solution)/shard_map/ppermute | solution.py:864
  50.3 2.1 %shard_map.172 = (f32[1,256,128]{2,1,0:T(8,128)}, f32[1,2,256,128]{3,2,1,0:T(8,128)}, f32[1,256,128]{2,1,0:T(8,128)}) custom-call(f32[4,256,128]{2,1,0:T(8,128)S(1)} %get-tuple-element.65.base, bf16[4,256,1024]{2,1,0:T(8,128)(2,1)S(1)} %get-tuple-element.66.d1_hi, bf16[4,256,1024]{2,1,0:T(8,128)(2,1)S(1)} %get-tuple-element.67.d1_lo, ...), custom_call_target="tpu_custom_call" | custom-call | flops 2000000000 | bytes 1000000 | tf_op jit(solution)/shard_map/pallas_call | solution.py:838
  52.4 0.0 collective-permute-done.8
  52.4 0.0 collective-permute-done.7
  52.4 0.0 collective-permute-done.6
  52.4 0.7 %shard_map.173 = (f32[16,32]{1,0:T(8,128)}, f32[1,32]{1,0:T(1,128)}, f32[32,32]{1,0:T(8,128)}, f32[1,32]{1,0:T(1,128)}, f32[8,32]{1,0:T(8,128)}, /*index=5*/f32[1,8]{1,0:T(1,128)}) custom-call(f32[40,128]{1,0:T(8,128)S(1)} %add_add_fusion.total), custom_call_target="tpu_custom_call" | custom-call | tf_op jit(solution)/shard_map/pallas_call | solution.py:838
  (3 shorter events, 0.0 us)
Async XLA Ops:
  3.5 11.0 %collective-permute-start = (f32[8,8,128]{2,1,0:T(8,128)S(1)}, f32[8,8,128]{2,1,0:T(8,128)S(1)}, u32[]{:S(2)}, u32[]{:S(2)}) collective-permute-start(f32[8,8,128]{2,1,0:T(8,128)S(1)} %get-tuple-element.53), channel_id=1, source_target_pairs={{0,1},{1,0},{2,3},{3,2},{4,5},{5,4},{6,7},{7,6},{8,9},{9,8},{10,11... | collective-permute-start | bytes 98312 | tf_op jit(solution)/shard_map/ppermute | solution.py:915
  6.5 8.0 %collective-permute-start.1 = (f32[8,8,128]{2,1,0:T(8,128)S(1)}, f32[8,8,128]{2,1,0:T(8,128)S(1)}, u32[]{:S(2)}, u32[]{:S(2)}) collective-permute-start(f32[8,8,128]{2,1,0:T(8,128)S(1)} %get-tuple-element.54), channel_id=1, source_target_pairs={{0,7},{1,2},{2,1},{3,4},{4,3},{5,6},{6,5},{7,0},{8,15},{9,10},{10,... | collective-permute-start | bytes 98312 | tf_op jit(solution)/shard_map/ppermute | solution.py:915
  37.9 1.2 %collective-permute-start.2 = (f32[40,128]{1,0:T(8,128)S(1)}, f32[40,128]{1,0:T(8,128)S(1)}, u32[]{:S(2)}, u32[]{:S(2)}) collective-permute-start(f32[40,128]{1,0:T(8,128)S(1)} %get-tuple-element.69), channel_id=1, source_target_pairs={{0,8},{1,9},{2,10},{3,11},{4,12},{5,13},{6,14},{7,15},{8,0},{9,1},... | collective-permute-start | bytes 61448 | tf_op jit(solution)/shard_map/ppermute | solution.py:864
  39.1 4.7 %collective-permute-start.5 = (f32[40,128]{1,0:T(8,128)S(1)}, f32[40,128]{1,0:T(8,128)S(1)}, u32[]{:S(2)}, u32[]{:S(2)}) collective-permute-start(f32[40,128]{1,0:T(8,128)S(1)} %add.21._), channel_id=1, source_target_pairs={{0,20},{1,21},{2,22},{3,23},{4,16},{5,17},{6,18},{7,19},{8,28},{9,... | collective-permute-start | bytes 61448 | tf_op jit(solution)/shard_map/ppermute | solution.py:864
  40.5 3.8 %collective-permute-start.4 = (f32[40,128]{1,0:T(8,128)S(1)}, f32[40,128]{1,0:T(8,128)S(1)}, u32[]{:S(2)}, u32[]{:S(2)}) collective-permute-start(f32[40,128]{1,0:T(8,128)S(1)} %add.21._), channel_id=1, source_target_pairs={{0,4},{1,5},{2,6},{3,7},{4,0},{5,1},{6,2},{7,3},{8,12},{9,13},{10,... | collective-permute-start | bytes 61448 | tf_op jit(solution)/shard_map/ppermute | solution.py:864
  42.1 3.8 %collective-permute-start.3 = (f32[40,128]{1,0:T(8,128)S(1)}, f32[40,128]{1,0:T(8,128)S(1)}, u32[]{:S(2)}, u32[]{:S(2)}) collective-permute-start(f32[40,128]{1,0:T(8,128)S(1)} %add.21._), channel_id=1, source_target_pairs={{0,16},{1,17},{2,18},{3,19},{4,20},{5,21},{6,22},{7,23},{8,24},{9,... | collective-permute-start | bytes 61448 | tf_op jit(solution)/shard_map/ppermute | solution.py:864
  45.9 6.5 %collective-permute-start.8 = (f32[40,128]{1,0:T(8,128)S(1)}, f32[40,128]{1,0:T(8,128)S(1)}, u32[]{:S(2)}, u32[]{:S(2)}) collective-permute-start(f32[40,128]{1,0:T(8,128)S(1)} %add_add_fusion.1), channel_id=1, source_target_pairs={{0,3},{1,2},{2,1},{3,0},{4,7},{5,6},{6,5},{7,4},{8,11},{9,10},{10,... | collective-permute-start | bytes 61448 | tf_op jit(solution)/shard_map/ppermute | solution.py:864
  47.3 5.1 %collective-permute-start.7 = (f32[40,128]{1,0:T(8,128)S(1)}, f32[40,128]{1,0:T(8,128)S(1)}, u32[]{:S(2)}, u32[]{:S(2)}) collective-permute-start(f32[40,128]{1,0:T(8,128)S(1)} %add_add_fusion.1), channel_id=1, source_target_pairs={{0,1},{1,0},{2,3},{3,2},{4,5},{5,4},{6,7},{7,6},{8,9},{9,8},{10,11... | collective-permute-start | bytes 61448 | tf_op jit(solution)/shard_map/ppermute | solution.py:864
  47.3 5.1 %collective-permute-start.6 = (f32[40,128]{1,0:T(8,128)S(1)}, f32[40,128]{1,0:T(8,128)S(1)}, u32[]{:S(2)}, u32[]{:S(2)}) collective-permute-start(f32[40,128]{1,0:T(8,128)S(1)} %add_add_fusion.1), channel_id=1, source_target_pairs={{0,2},{1,3},{2,0},{3,1},{4,6},{5,7},{6,4},{7,5},{8,10},{9,11},{10,... | collective-permute-start | bytes 61448 | tf_op jit(solution)/shard_map/ppermute | solution.py:864
